TPU v7x, 128 devices: a whole 4x4x4 slice. The times are simulated.
128 devices in a mesh: dp: 16 (over y, z), fsdp: 8 (over x, core).
Axes of the slice: x: 4, y: 4, z: 4, core: 2. Of those that a mesh axis runs over, the one named last changes fastest.
Arguments:
- activations: bfloat16 [81920, 4096], P(('dp', 'fsdp')), may hold values from -6 to 6
- out_grad: bfloat16 [81920, 11008], P(('dp', 'fsdp')), may hold values from -24 to 24
- projector: bfloat16 [4096, 512], P('fsdp'), may hold values from -0.09375 to 0.09375
- weight: bfloat16 [4096, 11008], P('fsdp', 'dp'), may hold values from -6 to 6
- first_moment: float32 [11008, 512], P(('dp', 'fsdp')), may hold values from -6 to 6
- second_moment: float32 [11008, 512], P(('dp', 'fsdp')), may hold values from 0.25 to 4
Outputs:
- new_weight: bfloat16 [4096, 11008], P(None, 'dp')
- new_first: float32 [11008, 512], P(('dp', 'fsdp'))
- new_second: float32 [11008, 512], P(('dp', 'fsdp'))
All inputs are finite; a program needn't handle non-finite values.
Results may differ from a plain program's by a relative error of at most 0.0049.
Values may be sent and summed in bfloat16 or wider, within the bound.
No kernel may reach another device: no remote copies, remote signals or barrier semaphores. Data moves between devices by JAX's collectives and lax.ppermute only.
A program may use at most 192 MiB of HBM per device.

v0:
```python
import math

import jax
import jax.numpy as jnp
from jax import lax
from jax.sharding import PartitionSpec as P

beta_first = 0.9
beta_second = 0.95
correct_first = 1.0 - 0.9**4
correct_second = 1.0 - 0.95**4
epsilon = 1e-08
step_size = 4.0


def on_device(activations, out_grad, projector, weight, first_moment, second_moment):
    devices_all = lax.axis_size("dp") * lax.axis_size("fsdp")
    scale = 1.0 / math.sqrt(activations.shape[0] * devices_all)
    columns = activations
    reduced = jnp.dot(
        columns,
        lax.all_gather(projector, "fsdp", axis=0, tiled=True),
        preferred_element_type=jnp.float32,
    ).astype(jnp.bfloat16)
    columns = out_grad
    partial_rows = lax.psum_scatter(
        lax.dot_general(
            columns, reduced, (((0,), (0,)), ((), ())), preferred_element_type=jnp.float32
        ),
        "dp",
        scatter_dimension=0,
        tiled=True,
    )
    grad = lax.psum_scatter(partial_rows, "fsdp", scatter_dimension=0, tiled=True)
    grad = grad * scale
    new_first = beta_first * first_moment + (1.0 - beta_first) * grad
    new_second = beta_second * second_moment + (1.0 - beta_second) * grad * grad
    direction = (
        new_first / correct_first / (jnp.sqrt(new_second / correct_second) + epsilon)
    ).astype(jnp.bfloat16)
    step_block = lax.all_gather(direction, "fsdp", axis=0, tiled=True)
    delta = lax.dot_general(
        projector, step_block, (((1,), (1,)), ((), ())), preferred_element_type=jnp.float32
    )
    new_shard = (weight.astype(jnp.float32) - step_size * delta).astype(jnp.bfloat16)
    new_weight = lax.all_gather(new_shard, "fsdp", axis=0, tiled=True)
    return (new_weight, new_first, new_second)


def solution(mesh):
    in_specs = (
        P(("dp", "fsdp"), None),
        P(("dp", "fsdp"), None),
        P("fsdp", None),
        P("fsdp", "dp"),
        P(("dp", "fsdp"), None),
        P(("dp", "fsdp"), None),
    )
    out_specs = (P(None, "dp"), P(("dp", "fsdp"), None), P(("dp", "fsdp"), None))
    return jax.shard_map(
        on_device, mesh=mesh, in_specs=in_specs, out_specs=out_specs, check_vma=False
    )
```

profile of v0, /device:TPU:1, one launch (start us, length us, event | category | flops | bytes accessed | tf_op | source)
XLA Modules:
  0.0 370.4 jit_solution(10163562314320105538)
XLA Ops:
  7.2 0.0 all-gather.4.cloned.1.call-start
  7.2 0.7 all-gather.4.cloned.1.call-update
  7.9 0.0 reduce-scatter.5.cloned.1.call-start
  7.9 37.5 %all-gather.4.cloned.1.call-done = bf16[4096,512]{1,0:T(8,128)(2,1)} async-done(((bf16[512,512]{1,0:T(8,128)(2,1)}), bf16[4096,512]{1,0:T(8,128)(2,1)}) %all-gather.4.cloned.1.call-update) | async-done | bytes 4194320 | tf_op jit(solution)/shard_map/all_gather | solution.py:22
  45.5 28.6 %convolution_bitcast_fusion = f32[11008,512]{0,1:T(8,128)} fusion(bf16[640,11008]{1,0:T(8,128)(2,1)} %param.7, bf16[640,4096]{1,0:T(8,128)(2,1)} %param.6, bf16[4096,512]{1,0:T(8,128)(2,1)} %all-gather.4.cloned.1.call-done), kind=kOutput, calls=%fused_computation | convolution fusion | flops 9898885120 | bytes 46071808 | tf_op jit(solution)/shard_map/dot_general | solution.py:27
  74.1 22.7 %copy.23 = f32[11008,512]{1,0:T(8,128)} copy(f32[11008,512]{0,1:T(8,128)} %convolution_bitcast_fusion) | data formatting | bytes 45088768
  96.8 0.0 reduce-scatter.5.cloned.1.call-update
  96.8 0.0 copy-start.1
  96.8 0.0 copy-start.2
  96.8 0.0 copy-start.4
  96.9 0.0 copy-start
  96.9 0.0 copy-start.3
  96.9 0.0 all-reduce.3.cloned.1.call-start
  96.9 139.5 %reduce-scatter.5.cloned.1.call-done = f32[688,512]{1,0:T(8,128)} async-done(((f32[11008,512]{1,0:T(8,128)}), f32[688,512]{1,0:T(8,128)}) %reduce-scatter.5.cloned.1.call-update) | async-done | bytes 1409040
  236.5 3.0 copy.24
  239.4 0.0 all-reduce.3.cloned.1.call-update
  239.5 0.0 all-gather.6.cloned.1.call-start
  239.5 0.0 copy-done.1
  239.5 0.1 copy.18
  239.7 0.1 copy.19
  239.8 0.6 dynamic-slice
  241.1 60.2 %all-reduce.3.cloned.1.call-done = f32[688,512]{0,1:T(8,128)} async-done(((f32[688,512]{0,1:T(8,128)}), f32[688,512]{0,1:T(8,128)}) %all-reduce.3.cloned.1.call-update) | async-done | bytes 1409040
  301.2 1.3 fusion.3
  302.5 0.1 copy.20
  302.7 15.8 %all-gather = bf16[8,86,512]{2,1,0:T(8,128)(2,1)S(1)} all-gather(bf16[1,86,512]{2,1,0:T(8,128)(2,1)S(1)} %copy.20), channel_id=1, replica_groups=mesh['dp'=16,'fsdp'=8] {'fsdp'}, dimensions={0}, use_global_device_ids=true | all-gather | bytes 792576 | tf_op jit(solution)/shard_map/all_gather | solution.py:41
  318.5 0.2 reshape.7
  318.7 1.4 fusion.2
  320.1 0.0 all-gather.6.cloned.1.call-update
  320.1 0.8 copy.21
  320.9 0.8 copy.22
  321.7 36.3 %all-gather.6.cloned.1.call-done = bf16[4096,688]{0,1:T(8,128)(2,1)} async-done(((bf16[512,688]{0,1:T(8,128)(2,1)}), bf16[4096,688]{0,1:T(8,128)(2,1)}) %all-gather.6.cloned.1.call-update) | async-done | bytes 5636112 | tf_op jit(solution)/shard_map/all_gather | solution.py:46
  358.1 5.8 %copy.29 = bf16[4096,688]{0,1:T(8,128)(2,1)} copy(bf16[4096,688]{0,1:T(8,128)(2,1)} %all-gather.6.cloned.1.call-done) | data formatting | bytes 11272192
  (4 shorter events, 0.0 us)
Async XLA Ops:
  7.2 38.3 %all-gather.4.cloned.1.call-start = ((), (), s32[]{:S(2)}) async-start(), calls=%async_computation.1 | async-start | bytes 4718592 | tf_op jit(solution)/shard_map/all_gather | solution.py:22
  7.9 228.6 %reduce-scatter.5.cloned.1.call-start = ((), (), s32[]{:S(2)}) async-start(), calls=%async_computation.3 | async-start | bytes 23953408
  96.8 142.7 %copy-start.1 = (f32[86,512]{1,0:T(8,128)S(1)}, f32[86,512]{1,0:T(8,128)}, u32[]{:S(2)}) copy-start(f32[86,512]{1,0:T(8,128)} %param.10) | copy-start | bytes 528388
  96.8 142.8 %copy-start.2 = (f32[86,512]{1,0:T(8,128)S(1)}, f32[86,512]{1,0:T(8,128)}, u32[]{:S(2)}) copy-start(f32[86,512]{1,0:T(8,128)} %param.11) | copy-start | bytes 528388
  96.8 143.0 %copy-start.4 = (u32[128]{0:T(128)S(1)}, u32[128]{0:T(128)}, u32[]{:S(2)}) copy-start(u32[128]{0:T(128)} %constant.26) | copy-start | bytes 1540
  96.9 221.8 %copy-start = (bf16[512,512]{1,0:T(8,128)(2,1)S(1)}, bf16[512,512]{1,0:T(8,128)(2,1)}, u32[]{:S(2)}) copy-start(bf16[512,512]{1,0:T(8,128)(2,1)} %param.8) | copy-start | bytes 1572868
  96.9 221.8 %copy-start.3 = (bf16[512,688]{0,1:T(8,128)(2,1)S(1)}, bf16[512,688]{0,1:T(8,128)(2,1)}, u32[]{:S(2)}) copy-start(bf16[512,688]{0,1:T(8,128)(2,1)} %param.9) | copy-start | bytes 2113540
  96.9 204.4 %all-reduce.3.cloned.1.call-start = ((), (), s32[]{:S(2)}) async-start(), calls=%async_computation.4 | async-start | bytes 3145728
  239.5 118.6 %all-gather.6.cloned.1.call-start = ((), (), s32[]{:S(2)}) async-start(), calls=%async_computation.2 | async-start | bytes 6340608 | tf_op jit(solution)/shard_map/all_gather | solution.py:46
Sparse Core Ops, SparseCore 0:
  9.7 35.6 all-gather.3
  96.9 139.4 reduce-scatter.4
  239.6 61.6 all-reduce.2
  320.2 37.7 all-gather.5
where the time goes:
time: 371 us; the launch traced here: 370 us
  waiting for transfers between devices  274 us (74%)
  local copies, waits for them, and re-layouts  34.3 us (9%)
  matrix products  30 us (8%)
  blocking collectives  15.8 us (4%)
  between operations  14.5 us (4%)
    unnamed x6, waiting for transfers between devices  200 us
    all_gather x1, waiting for transfers between devices, on_device(): lax.all_gather(projector, 'fsdp', axis=0, tiled=True)  37.5 us
    all_gather x1, waiting for transfers between devices, on_device(): new_weight = lax.all_gather(new_shard, 'fsdp', axis=0, tiled=True)  36.3 us
    unnamed x20, local copies, waits for them, and re-layouts  34.3 us
    dot_general x1, matrix products, on_device(): lax.dot_general(columns, reduced, (((0,), (0,)), ((), ())), preferred_ele...  28.6 us
    all_gather x1, blocking collectives, on_device(): step_block = lax.all_gather(direction, 'fsdp', axis=0, tiled=True)  15.8 us
  transfers between devices with their start and end apart: 4, of which 4 were waited for; matrix products, arithmetic and copies ran while one was open for 1% of the time, Pallas kernels for 0%

commit v1 on v0

v1 whole, which is shorter than its diff:
```python
import math

import jax
import jax.numpy as jnp
from jax import lax
from jax.experimental import pallas as pl
from jax.experimental.pallas import tpu as pltpu
from jax.sharding import Mesh
from jax.sharding import PartitionSpec as P

beta_first = 0.9
beta_second = 0.95
correct_first = 1.0 - 0.9**4
correct_second = 1.0 - 0.95**4
epsilon = 1e-08
step_size = 4.0

SIDE = 4
SWAP = ((0, 1), (1, 0))


def hop(array, axis, distance):
    return lax.ppermute(array, axis, [(i, (i + distance) % SIDE) for i in range(SIDE)])


def grad_kernel(mine_ref, other_ref, reduced_ref, reduced_other_ref, a_ref, b_ref):
    contract = (((0,), (0,)), ((), ()))
    total = lax.dot_general(
        mine_ref[...], reduced_ref[...], contract, preferred_element_type=jnp.float32
    )
    total += lax.dot_general(
        other_ref[...], reduced_other_ref[...], contract, preferred_element_type=jnp.float32
    )
    total = total.astype(jnp.bfloat16)
    half = a_ref.shape[1]
    a_ref[...] = total[:, :half]
    b_ref[...] = total[:, half:]


def partial_grad(mine, other, reduced, reduced_other, tile=2816):
    tokens, hidden = mine.shape
    columns = reduced.shape[1]
    half = columns // 2
    return pl.pallas_call(
        grad_kernel,
        grid=(pl.cdiv(hidden, tile),),
        in_specs=[pl.BlockSpec((tokens, tile), lambda i: (0, i))] * 2
        + [pl.BlockSpec((tokens, columns), lambda i: (0, 0))] * 2,
        out_specs=[pl.BlockSpec((tile, half), lambda i: (i, 0))] * 2,
        out_shape=[jax.ShapeDtypeStruct((hidden, half), jnp.bfloat16)] * 2,
        cost_estimate=pl.CostEstimate(
            flops=4 * tokens * hidden * columns,
            bytes_accessed=4 * tokens * hidden + 2 * hidden * columns,
            transcendentals=0,
        ),
        compiler_params=pltpu.CompilerParams(vmem_limit_bytes=56 << 20),
        name="partial_grad",
    )(mine, other, reduced, reduced_other)


def sum_along(blocks, axis, me):
    total = lax.dynamic_index_in_dim(blocks, me, 0, keepdims=False).astype(jnp.float32)
    arrived = []
    for distance in (1, SIDE - 1, 2):
        to = lax.rem(me + distance, SIDE)
        arrived.append(hop(lax.dynamic_index_in_dim(blocks, to, 0, keepdims=False), axis, distance))
    for part in arrived:
        total += part.astype(jnp.float32)
    return total


def on_device(activations, out_grad, projector, weight, first_moment, second_moment):
    y, z, core = lax.axis_index("y"), lax.axis_index("z"), lax.axis_index("core")
    rank = projector.shape[1]
    half = rank // 2
    quarter = half // 2
    scale = 1.0 / math.sqrt(activations.shape[0] * SIDE**3 * 2)

    def own(array, axis):
        return lax.dynamic_slice_in_dim(array, core * half, half, axis)

    def others(array, axis):
        return lax.dynamic_slice_in_dim(array, (1 - core) * half, half, axis)

    projector_all = lax.all_gather(projector, ("x", "core"), axis=0, tiled=True)
    out_grad_other = lax.ppermute(out_grad, "core", SWAP)
    moments = jnp.stack([first_moment, second_moment])
    rows = moments.shape[1]
    moments_other = lax.ppermute(others(moments, 2), "core", SWAP)
    moments_own = own(moments, 2)
    moments = jnp.where(
        core == 0,
        jnp.concatenate([moments_own, moments_other], axis=1),
        jnp.concatenate([moments_other, moments_own], axis=1),
    )

    reduced = jnp.dot(
        activations, projector_all, preferred_element_type=jnp.float32
    ).astype(jnp.bfloat16)
    reduced_other = lax.ppermute(others(reduced, 1), "core", SWAP)
    weight, reduced_own = lax.optimization_barrier((weight, own(reduced, 1)))
    weight_all = lax.all_gather(weight, ("x", "core"), axis=0, tiled=True)

    a, b = partial_grad(out_grad, out_grad_other, reduced_own, reduced_other)
    block = a.shape[0] // SIDE**2
    a = a.reshape(SIDE, SIDE, block, quarter)
    b = b.reshape(SIDE, SIDE, block, quarter).swapaxes(0, 1)
    a = sum_along(a, "y", y).astype(jnp.bfloat16)
    b = sum_along(b, "z", z).astype(jnp.bfloat16)
    a = a.reshape(SIDE**2, block // SIDE, quarter)
    b = b.reshape(SIDE**2, block // SIDE, quarter)
    a = lax.all_to_all(a, ("z", "x"), 0, 0, tiled=True)
    b = lax.all_to_all(b, ("y", "x"), 0, 0, tiled=True)
    grad = jnp.concatenate(
        [jnp.sum(a.astype(jnp.float32), axis=0), jnp.sum(b.astype(jnp.float32), axis=0)], axis=1
    )
    grad = grad * scale

    new_first = beta_first * moments[0] + (1.0 - beta_first) * grad
    new_second = beta_second * moments[1] + (1.0 - beta_second) * grad * grad
    direction = (
        new_first / correct_first / (jnp.sqrt(new_second / correct_second) + epsilon)
    ).astype(jnp.bfloat16)

    direction = lax.all_gather(direction, ("x", "core"), axis=0)
    direction = direction.reshape(SIDE, 2, block // SIDE, half)
    contract = (((1,), (1,)), ((), ()))
    delta = 0.0
    for part in range(2):
        delta += lax.dot_general(
            projector_all[:, part * half : (part + 1) * half],
            direction[:, part].reshape(block, half),
            contract,
            preferred_element_type=jnp.float32,
        )
    new_weight = (weight_all.astype(jnp.float32) - step_size * delta).astype(jnp.bfloat16)

    news = jnp.stack([new_first, new_second])
    kept = lax.dynamic_slice_in_dim(news, core * rows, rows, 1)
    came = lax.ppermute(
        lax.dynamic_slice_in_dim(news, (1 - core) * rows, rows, 1), "core", SWAP
    )
    news = jnp.where(
        core == 0,
        jnp.concatenate([kept, came], axis=2),
        jnp.concatenate([came, kept], axis=2),
    )
    return (new_weight, news[0], news[1])


def solution(mesh):
    grid = Mesh(mesh.devices.reshape(SIDE, SIDE, SIDE, 2), ("y", "z", "x", "core"))
    everywhere, group = ("y", "z", "x", "core"), ("x", "core")
    in_specs = (
        P(everywhere, None),
        P(everywhere, None),
        P(group, None),
        P(group, ("y", "z")),
        P(everywhere, None),
        P(everywhere, None),
    )
    out_specs = (P(None, ("y", "z")), P(everywhere, None), P(everywhere, None))
    return jax.shard_map(
        on_device, mesh=grid, in_specs=in_specs, out_specs=out_specs, check_vma=False
    )
```

time: 371 us -> 187 us (0.50)
  waiting for transfers between devices: 274 us -> 76.6 us
  starting transfers between devices: 0.16 us -> 26.4 us
  local copies, waits for them, and re-layouts: 34.3 us -> 9.71 us
  Pallas kernels: 0 us -> 16.3 us
  matrix products: 30 us -> 24 us
  other arithmetic: 1.3 us -> 6.41 us
    unnamed x6 -> x2, waiting for transfers between devices: 200 us -> 0.03 us
    all_gather x2, waiting for transfers between devices: 73.9 us -> 36.7 us  [the longest x1 36.7 us: on_device(): projector_all = lax.all_gather(projector, ('x', 'core'), axis=0, tiled=True)]
    unnamed x20 -> x5, local copies, waits for them, and re-layouts: 34.3 us -> 0.8 us
    ppermute x0 -> x10, waiting for transfers between devices: none -> 26.1 us  [the longest x6 23.7 us: hop(): lax.ppermute(array, axis, [(i, (i + distance) % SIDE) for i in range(SIDE)])]
    ppermute x0 -> x10, starting transfers between devices: none -> 17.4 us  [the longest x6 9.62 us: hop(): lax.ppermute(array, axis, [(i, (i + distance) % SIDE) for i in range(SIDE)])]
    pallas_call x0 -> x1, Pallas kernels: none -> 16.3 us  [partial_grad(): pl.pallas_call(grad_kernel, grid=(pl.cdiv(hidden, tile),), in_specs=[pl.B...]
    all_to_all x0 -> x2, waiting for transfers between devices: none -> 13.8 us  [the longest x1 7.34 us: on_device(): a = lax.all_to_all(a, ('z', 'x'), 0, 0, tiled=True)]
    all_to_all x0 -> x2, starting transfers between devices: none -> 8.93 us  [the longest x1 5.32 us: on_device(): a = lax.all_to_all(a, ('z', 'x'), 0, 0, tiled=True)]
  transfers between devices with their start and end apart: 4 -> 14, of which waited for: 4 -> 7; matrix products, arithmetic and copies ran while one was open for 1% -> 16% of each run, Pallas kernels for 0% -> 9%
where the time goes in v1:
time: 187 us
  waiting for transfers between devices  76.6 us (41%)
  starting transfers between devices  26.4 us (14%)
  matrix products  24 us (13%)
  Pallas kernels  16.3 us (9%)
  between operations  14.2 us (8%)
  blocking collectives  13.3 us (7%)
  local copies, waits for them, and re-layouts  9.71 us (5%)
  other arithmetic  6.41 us (3%)
    all_gather x1, waiting for transfers between devices, on_device(): projector_all = lax.all_gather(projector, ('x', 'core'), axis=0, tiled=True)  36.7 us
    ppermute x6, waiting for transfers between devices, hop(): lax.ppermute(array, axis, [(i, (i + distance) % SIDE) for i in range(SIDE)])  23.7 us
    dot_general x2, matrix products, on_device(): lax.dot_general(projector_all[:, part * half:(part + 1) * half], directio...  17.4 us
    pallas_call x1, Pallas kernels, partial_grad(): pl.pallas_call(grad_kernel, grid=(pl.cdiv(hidden, tile),), in_specs=[pl.B...  16.3 us
    all_gather x1, blocking collectives, on_device(): direction = lax.all_gather(direction, ('x', 'core'), axis=0)  13.3 us
    ppermute x6, starting transfers between devices, hop(): lax.ppermute(array, axis, [(i, (i + distance) % SIDE) for i in range(SIDE)])  9.62 us
    all_to_all x1, waiting for transfers between devices, on_device(): a = lax.all_to_all(a, ('z', 'x'), 0, 0, tiled=True)  7.34 us
    dot_general x1, matrix products, on_device(): jnp.dot(activations, projector_all, preferred_element_type=jnp.float32)  6.62 us
  transfers between devices with their start and end apart: 14, of which 7 were waited for; matrix products, arithmetic and copies ran while one was open for 16% of the time, Pallas kernels for 9%

profile of v1, /device:TPU:1, one launch (start us, length us, event | category | flops | bytes accessed | tf_op | source)
XLA Modules:
  0.0 187.0 jit_solution(2664906679803831235)
XLA Ops:
  7.2 1.5 collective-permute-start.1
  8.8 36.7 %all-gather.3.cloned.1.call-done = bf16[4096,512]{1,0:T(8,128)(2,1)} async-done(((bf16[512,512]{1,0:T(8,128)(2,1)}), bf16[4096,512]{1,0:T(8,128)(2,1)}) %all-gather.3.cloned.1.call-update) | async-done | bytes 4194320 | tf_op jit(solution)/shard_map/all_gather | solution.py:85
  45.5 6.6 %convolution_convert_fusion = bf16[640,512]{1,0:T(8,128)(2,1)S(1)} fusion(bf16[640,4096]{1,0:T(8,128)(2,1)} %param.6, bf16[4096,512]{1,0:T(8,128)(2,1)} %all-gather.3.cloned.1.call-done), kind=kOutput, calls=%fused_computation.15 | convolution fusion | flops 2684682240 | bytes 10092544 | tf_op jit(solution)/shard_map/dot_general | solution.py:97
  52.1 0.8 constant_dynamic-slice_fusion
  53.2 1.4 collective-permute-done.2.reduced_other_ref
  55.4 16.3 %partial_grad.1 = (bf16[11008,128]{1,0:T(8,128)(2,1)}, bf16[11008,128]{1,0:T(8,128)(2,1)}) custom-call(bf16[640,11008]{1,0:T(8,128)(2,1)} %mine_ref.1, bf16[640,11008]{1,0:T(8,128)(2,1)} %collective-permute-done.1.other_ref, bf16[640,256]{1,0:T(8,128)(2,1)} %get-tuple-element.8.reduced_ref, bf16[640,256]{1,0:T(8,128)(2,1)} %copy-done.1), custom_call_target="tpu_custom_call" | custom-call | flops 7214202880 | bytes 33816576 | tf_op jit(solution)/shard_map/partial_grad/pallas_call | solution.py:44
  71.7 2.9 %dynamic-slice_bitcast_fusion.5 = (bf16[4,688,128]{2,1,0:T(8,128)(2,1)}, bf16[4,688,128]{2,1,0:T(8,128)(2,1)S(1)}, bf16[4,688,128]{2,1,0:T(8,128)(2,1)}) fusion(bf16[4,4,688,128]{3,2,1,0:T(8,128)(2,1)} %bitcast.50, s32[]{:T(128)S(6)} %select_n.60, s32[]{:T(128)S(6)} %select_n.62, s32[]{:T(128)S(6)} %select_n.61), kind=kLoop, calls=%fused_computation.21 | loop fusion | bytes 4227084 | tf_op jit(solution)/shard_map/jit(dynamic_index_in_dim)/squeeze | solution.py:66
  74.6 1.2 collective-permute-start.3
  75.7 1.5 collective-permute-start.4
  77.3 1.5 collective-permute-start.5
  78.7 1.4 dynamic-slice_bitcast_fusion.2
  80.1 1.3 collective-permute-start.6
  81.4 1.4 collective-permute-start.7
  82.8 10.5 %collective-permute-done.3 = bf16[4,688,128]{2,1,0:T(8,128)(2,1)} collective-permute-done((bf16[4,688,128]{2,1,0:T(8,128)(2,1)}, bf16[4,688,128]{2,1,0:T(8,128)(2,1)}, u32[]{:S(2)}, u32[]{:S(2)}) %collective-permute-start.3) | collective-permute-done | bytes 704544 | tf_op jit(solution)/shard_map/ppermute | solution.py:23
  93.2 2.8 %collective-permute-start.8 = (bf16[4,688,128]{2,1,0:T(8,128)(2,1)}, bf16[4,688,128]{2,1,0:T(8,128)(2,1)}, u32[]{:S(2)}, u32[]{:S(2)}) collective-permute-start(bf16[4,688,128]{2,1,0:T(8,128)(2,1)} %get-tuple-element.18), channel_id=1, source_target_pairs={{0,16},{8,24},{16,0},{24,8},{1,17},{9,25},{17,1},{25,9},{2,18},{10... | collective-permute-start | bytes 2113544 | tf_op jit(solution)/shard_map/ppermute | solution.py:23
  96.0 13.2 %collective-permute-done.5 = bf16[4,688,128]{2,1,0:T(8,128)(2,1)} collective-permute-done((bf16[4,688,128]{2,1,0:T(8,128)(2,1)S(1)}, bf16[4,688,128]{2,1,0:T(8,128)(2,1)}, u32[]{:S(2)}, u32[]{:S(2)}) %collective-permute-start.5) | collective-permute-done | bytes 704544 | tf_op jit(solution)/shard_map/ppermute | solution.py:23
  109.2 2.1 %fusion.9 = bf16[4,688,128]{2,1,0:T(8,128)(2,1)S(1)} fusion(bf16[4,688,128]{2,1,0:T(8,128)(2,1)} %collective-permute-done.5, bf16[4,688,128]{2,1,0:T(8,128)(2,1)} %collective-permute-done.4, bf16[4,688,128]{2,1,0:T(8,128)(2,1)} %collective-permute-done.3, bf16[4,4,688,128]{3,2,1,0:T(8,128)(2,1)} %bitcast.51, s32[]{:T(128)S(6)} %select_n.59), kind=kLoop, calls=%fused_computation.14 | loop fusion | flops 2818048 | bytes 3522564 | tf_op jit(solution)/shard_map/convert_element_type | solution.py:108
  111.3 1.0 reshape.124
  112.3 5.3 %all-to-all-start = ((bf16[16,172,128]{2,1,0:T(8,128)(2,1)}), bf16[16,172,128]{2,1,0:T(8,128)(2,1)S(1)}, u32[]{:S(2)}, u32[]{:S(2)}) async-start(bf16[16,172,128]{2,1,0:T(8,128)(2,1)} %reshape.124), calls=%async_computation | async-start | bytes 1441792 | tf_op jit(solution)/shard_map/all_to_all | solution.py:112
  117.7 2.8 %fusion.6 = bf16[4,688,128]{2,1,0:T(8,128)(2,1)} fusion(bf16[4,688,128]{2,1,0:T(8,128)(2,1)} %collective-permute-done.8, bf16[4,688,128]{2,1,0:T(8,128)(2,1)} %collective-permute-done.7, bf16[4,688,128]{2,1,0:T(8,128)(2,1)} %collective-permute-done.6, bf16[4,4,688,128]{3,2,1,0:T(8,128)(2,1)S(1)} %bitcast.49, s32[]{:T(128)S(6)} %select_n.63), kind=kLoop, calls=%fused_computation.10 | loop fusion | flops 2818048 | bytes 3522564 | tf_op jit(solution)/shard_map/convert_element_type | solution.py:109
  120.4 2.0 %reshape.126 = bf16[16,172,128]{2,1,0:T(8,128)(2,1)} reshape(bf16[4,688,128]{2,1,0:T(8,128)(2,1)} %fusion.6) | data formatting | bytes 1409024 | tf_op jit(solution)/shard_map/reshape | solution.py:111
  122.4 7.3 %all-to-all-done = bf16[16,172,128]{2,1,0:T(8,128)(2,1)S(1)} async-done(((bf16[16,172,128]{2,1,0:T(8,128)(2,1)}), bf16[16,172,128]{2,1,0:T(8,128)(2,1)S(1)}, u32[]{:S(2)}, u32[]{:S(2)}) %all-to-all-start) | async-done | bytes 704544 | tf_op jit(solution)/shard_map/all_to_all | solution.py:112
  129.8 3.6 %all-to-all-start.1 = ((bf16[16,172,128]{2,1,0:T(8,128)(2,1)}), bf16[16,172,128]{2,1,0:T(8,128)(2,1)S(1)}, u32[]{:S(2)}, u32[]{:S(2)}) async-start(bf16[16,172,128]{2,1,0:T(8,128)(2,1)} %reshape.126), calls=%async_computation.1 | async-start | bytes 1441792 | tf_op jit(solution)/shard_map/all_to_all | solution.py:113
  133.4 1.1 fusion.13
  134.4 2.5 %collective-permute-start = (f32[2,86,256]{2,1,0:T(8,128)S(1)}, f32[2,86,256]{2,1,0:T(8,128)S(1)}, u32[]{:S(2)}, u32[]{:S(2)}) collective-permute-start(f32[2,86,256]{2,1,0:T(8,128)S(1)} %get-tuple-element.29), channel_id=1, source_target_pairs={{0,1},{1,0},{2,3},{3,2},{4,5},{5,4},{6,7},{7,6},{8,9},{9,8},{10,11... | collective-permute-start | bytes 528392 | tf_op jit(solution)/shard_map/ppermute | solution.py:89
  137.0 1.0 collective-permute-done
  138.2 6.5 %all-to-all-done.1 = bf16[16,172,128]{2,1,0:T(8,128)(2,1)S(1)} async-done(((bf16[16,172,128]{2,1,0:T(8,128)(2,1)}), bf16[16,172,128]{2,1,0:T(8,128)(2,1)S(1)}, u32[]{:S(2)}, u32[]{:S(2)}) %all-to-all-start.1) | async-done | bytes 704544 | tf_op jit(solution)/shard_map/all_to_all | solution.py:113
  145.0 3.4 %collective-permute-start.9 = (f32[2,86,256]{2,1,0:T(8,128)S(1)}, f32[2,86,256]{2,1,0:T(8,128)S(1)}, u32[]{:S(2)}, u32[]{:S(2)}) collective-permute-start(f32[2,86,256]{2,1,0:T(8,128)S(1)} %get-tuple-element.27), channel_id=1, source_target_pairs={{0,1},{1,0},{2,3},{3,2},{4,5},{5,4},{6,7},{7,6},{8,9},{9,8},{10,11... | collective-permute-start | bytes 528392 | tf_op jit(solution)/shard_map/ppermute | solution.py:140
  148.4 13.3 %all_gather.12 = bf16[8,172,256]{2,1,0:T(8,128)(2,1)S(1)} all-gather(bf16[1,172,256]{2,1,0:T(8,128)(2,1)S(1)} %get-tuple-element.11), channel_id=1, replica_groups=mesh['y'=4,'z'=4,'x'=4,'core'=2] {'x','core'}, dimensions={0}, use_global_device_ids=true | all-gather | bytes 792576 | tf_op jit(solution)/shard_map/all_gather | solution.py:125
  161.9 7.5 %fusion.2 = f32[688,4096]{1,0:T(8,128)} fusion(bf16[688,256]{1,0:T(8,128)(2,1)S(1)} %reshape_squeeze.6, bf16[4096,512]{1,0:T(8,128)(2,1)} %all-gather.3.cloned.1.call-done), kind=kOutput, calls=%fused_computation.3 | convolution fusion | flops 1442840576 | bytes 13721600 | tf_op jit(solution)/shard_map/dot_general | solution.py:130
  169.5 0.8 slice_bitcast_fusion.2
  170.2 9.9 %fusion = bf16[4096,688]{0,1:T(8,128)(2,1)} fusion(f32[688,4096]{1,0:T(8,128)} %fusion.2, bf16[4096,688]{0,1:T(8,128)(2,1)} %all-gather.5.cloned.1.call-done, bf16[688,256]{1,0:T(8,128)(2,1)S(1)} %reshape_squeeze.7, bf16[4096,512]{1,0:T(8,128)(2,1)} %all-gather.3.cloned.1.call-done), kind=kOutput, calls=%fused_computation.1 | convolution fusion | flops 1456930816 | bytes 24993792 | tf_op jit(solution)/shard_map/dot_general | solution.py:130
  (25 shorter events, 1.9 us)
Async XLA Ops:
  7.2 38.3 %all-gather.3.cloned.1.call-start = ((), (), s32[]{:S(2)}) async-start(), calls=%async_computation.2 | async-start | bytes 4718592 | tf_op jit(solution)/shard_map/all_gather | solution.py:85
  7.2 47.4 %collective-permute-start.1 = (bf16[640,11008]{1,0:T(8,128)(2,1)}, bf16[640,11008]{1,0:T(8,128)(2,1)}, u32[]{:S(2)}, u32[]{:S(2)}) collective-permute-start(bf16[640,11008]{1,0:T(8,128)(2,1)} %mine_ref.1), channel_id=1, source_target_pairs={{0,1},{1,0},{2,3},{3,2},{4,5},{5,4},{6,7},{7,6},{8,9},{9,8},{10,11... | collective-permute-start | bytes 42270728 | tf_op jit(solution)/shard_map/ppermute | solution.py:86
  8.7 161.5 %all-gather.5.cloned.1.call-start = ((), (), s32[]{:S(2)}) async-start(), calls=%async_computation.3 | async-start | bytes 6340608 | tf_op jit(solution)/shard_map/all_gather | solution.py:102
  52.9 1.7 collective-permute-start.2
  54.6 0.8 copy-start.1
  71.7 7.1 %copy-start = (bf16[11008,128]{1,0:T(8,128)(2,1)S(1)}, bf16[11008,128]{1,0:T(8,128)(2,1)}, u32[]{:S(2)}) copy-start(bf16[11008,128]{1,0:T(8,128)(2,1)} %get-tuple-element.10) | copy-start | bytes 8454148
  74.6 18.7 %collective-permute-start.3 = (bf16[4,688,128]{2,1,0:T(8,128)(2,1)}, bf16[4,688,128]{2,1,0:T(8,128)(2,1)}, u32[]{:S(2)}, u32[]{:S(2)}) collective-permute-start(bf16[4,688,128]{2,1,0:T(8,128)(2,1)} %get-tuple-element.14), channel_id=1, source_target_pairs={{0,32},{32,64},{64,96},{96,0},{1,33},{33,65},{65,97},{97,1},{2,34}... | collective-permute-start | bytes 2113544 | tf_op jit(solution)/shard_map/ppermute | solution.py:23
  75.7 20.3 %collective-permute-start.4 = (bf16[4,688,128]{2,1,0:T(8,128)(2,1)}, bf16[4,688,128]{2,1,0:T(8,128)(2,1)}, u32[]{:S(2)}, u32[]{:S(2)}) collective-permute-start(bf16[4,688,128]{2,1,0:T(8,128)(2,1)} %get-tuple-element.16), channel_id=1, source_target_pairs={{0,96},{32,0},{64,32},{96,64},{1,97},{33,1},{65,33},{97,65},{2,98}... | collective-permute-start | bytes 2113544 | tf_op jit(solution)/shard_map/ppermute | solution.py:23
  77.3 32.0 %collective-permute-start.5 = (bf16[4,688,128]{2,1,0:T(8,128)(2,1)S(1)}, bf16[4,688,128]{2,1,0:T(8,128)(2,1)}, u32[]{:S(2)}, u32[]{:S(2)}) collective-permute-start(bf16[4,688,128]{2,1,0:T(8,128)(2,1)S(1)} %get-tuple-element.15), channel_id=1, source_target_pairs={{0,64},{32,96},{64,0},{96,32},{1,65},{33,97},{65,1},{97,33},{2,66}... | collective-permute-start | bytes 2113544 | tf_op jit(solution)/shard_map/ppermute | solution.py:23
  80.1 37.5 %collective-permute-start.6 = (bf16[4,688,128]{2,1,0:T(8,128)(2,1)}, bf16[4,688,128]{2,1,0:T(8,128)(2,1)}, u32[]{:S(2)}, u32[]{:S(2)}) collective-permute-start(bf16[4,688,128]{2,1,0:T(8,128)(2,1)} %get-tuple-element.17), channel_id=1, source_target_pairs={{0,8},{8,16},{16,24},{24,0},{1,9},{9,17},{17,25},{25,1},{2,10},{10... | collective-permute-start | bytes 2113544 | tf_op jit(solution)/shard_map/ppermute | solution.py:23
  81.4 36.3 %collective-permute-start.7 = (bf16[4,688,128]{2,1,0:T(8,128)(2,1)}, bf16[4,688,128]{2,1,0:T(8,128)(2,1)}, u32[]{:S(2)}, u32[]{:S(2)}) collective-permute-start(bf16[4,688,128]{2,1,0:T(8,128)(2,1)} %get-tuple-element.19), channel_id=1, source_target_pairs={{0,24},{8,0},{16,8},{24,16},{1,25},{9,1},{17,9},{25,17},{2,26},{10... | collective-permute-start | bytes 2113544 | tf_op jit(solution)/shard_map/ppermute | solution.py:23
  93.2 24.4 %collective-permute-start.8 = (bf16[4,688,128]{2,1,0:T(8,128)(2,1)}, bf16[4,688,128]{2,1,0:T(8,128)(2,1)}, u32[]{:S(2)}, u32[]{:S(2)}) collective-permute-start(bf16[4,688,128]{2,1,0:T(8,128)(2,1)} %get-tuple-element.18), channel_id=1, source_target_pairs={{0,16},{8,24},{16,0},{24,8},{1,17},{9,25},{17,1},{25,9},{2,18},{10... | collective-permute-start | bytes 2113544 | tf_op jit(solution)/shard_map/ppermute | solution.py:23
  112.3 17.5 %all-to-all-start = ((bf16[16,172,128]{2,1,0:T(8,128)(2,1)}), bf16[16,172,128]{2,1,0:T(8,128)(2,1)S(1)}, u32[]{:S(2)}, u32[]{:S(2)}) async-start(bf16[16,172,128]{2,1,0:T(8,128)(2,1)} %reshape.124), calls=%async_computation | async-start | bytes 1441792 | tf_op jit(solution)/shard_map/all_to_all | solution.py:112
  129.8 14.9 %all-to-all-start.1 = ((bf16[16,172,128]{2,1,0:T(8,128)(2,1)}), bf16[16,172,128]{2,1,0:T(8,128)(2,1)S(1)}, u32[]{:S(2)}, u32[]{:S(2)}) async-start(bf16[16,172,128]{2,1,0:T(8,128)(2,1)} %reshape.126), calls=%async_computation.1 | async-start | bytes 1441792 | tf_op jit(solution)/shard_map/all_to_all | solution.py:113
  134.4 3.6 %collective-permute-start = (f32[2,86,256]{2,1,0:T(8,128)S(1)}, f32[2,86,256]{2,1,0:T(8,128)S(1)}, u32[]{:S(2)}, u32[]{:S(2)}) collective-permute-start(f32[2,86,256]{2,1,0:T(8,128)S(1)} %get-tuple-element.29), channel_id=1, source_target_pairs={{0,1},{1,0},{2,3},{3,2},{4,5},{5,4},{6,7},{7,6},{8,9},{9,8},{10,11... | collective-permute-start | bytes 528392 | tf_op jit(solution)/shard_map/ppermute | solution.py:89
  145.0 24.4 %collective-permute-start.9 = (f32[2,86,256]{2,1,0:T(8,128)S(1)}, f32[2,86,256]{2,1,0:T(8,128)S(1)}, u32[]{:S(2)}, u32[]{:S(2)}) collective-permute-start(f32[2,86,256]{2,1,0:T(8,128)S(1)} %get-tuple-element.27), channel_id=1, source_target_pairs={{0,1},{1,0},{2,3},{3,2},{4,5},{5,4},{6,7},{7,6},{8,9},{9,8},{10,11... | collective-permute-start | bytes 528392 | tf_op jit(solution)/shard_map/ppermute | solution.py:140
Sparse Core Ops, SparseCore 0:
  9.7 35.6 all-gather.2
  53.0 38.0 all-gather.4

commit v2 on v1

v2 whole, which is shorter than its diff:
```python
import functools
import math

import jax
import jax.numpy as jnp
from jax import lax
from jax.experimental import pallas as pl
from jax.experimental.pallas import tpu as pltpu
from jax.sharding import Mesh
from jax.sharding import PartitionSpec as P

beta_first = 0.9
beta_second = 0.95
correct_first = 1.0 - 0.9**4
correct_second = 1.0 - 0.95**4
epsilon = 1e-08
step_size = 4.0

SIDE = 4
SWAP = ((0, 1), (1, 0))
CORE, FIRST, PLACE = 0, 1, 9
DISTANCES = (2, 3, 1, 0)


def hop(array, axis, distance):
    return lax.ppermute(array, axis, [(i, (i + distance) % SIDE) for i in range(SIDE)])


VMEM = pl.BlockSpec(memory_space=pltpu.VMEM)
SMEM = pl.BlockSpec(memory_space=pltpu.SMEM)


def in_vmem(kernel, name, out_shape, *operands, scratch=(), limit=16, table=None):
    first = [] if table is None else [SMEM]
    operands = operands if table is None else (table, *operands)
    return pl.pallas_call(
        kernel,
        in_specs=first + [VMEM] * (len(operands) - len(first)),
        out_specs=jax.tree.map(lambda _: VMEM, out_shape),
        out_shape=out_shape,
        scratch_shapes=list(scratch),
        compiler_params=pltpu.CompilerParams(vmem_limit_bytes=limit << 20),
        name=name,
    )(*operands)


ANY = pl.BlockSpec(memory_space=pl.ANY)


def diagonal_kernel(
    numbers, at_ref, mine_ref, other_ref, reduced_ref, reduced_other_ref, *refs
):
    outs, (windows, reduced, held, sems) = refs[:-4], refs[-4:]
    contract = (((0,), (0,)), ((), ()))
    tokens, hidden = mine_ref.shape
    hidden //= 2
    window = held.shape[0]
    blocks, block, _ = outs[0].shape
    offset = pl.multiple_of(at_ref[CORE] * hidden, 128)
    skips, copies = [], []
    for i, (n, j) in enumerate((n, j) for n in numbers for j in range(blocks)):
        first = at_ref[FIRST + blocks * n + j] * block
        start = pl.multiple_of(jnp.minimum(first // 128 * 128, hidden - window), 128)
        skips.append(pl.multiple_of(first - start, 16))
        copies.append(
            [
                pltpu.make_async_copy(
                    ref.at[:, pl.ds(pl.multiple_of(start + offset, 128), window)],
                    windows.at[i, pl.ds(side * tokens, tokens)],
                    sems.at[i, side],
                )
                for side, ref in enumerate((mine_ref, other_ref))
            ]
        )
        for copy in copies[-1]:
            copy.start()
    reduced[:tokens] = reduced_ref[...]
    reduced[tokens:] = reduced_other_ref[...]
    for i, skip in enumerate(skips):
        for copy in copies[i]:
            copy.wait()
        total = lax.dot_general(
            windows[i], reduced[...], contract, preferred_element_type=jnp.float32
        )
        held[...] = total.astype(held.dtype)
        outs[i // blocks][i % blocks] = held[pl.ds(skip, block)]


def diagonal_grad(numbers, table, mine, other, reduced, reduced_other):
    tokens, hidden = mine.shape
    columns = reduced.shape[1]
    out = jax.ShapeDtypeStruct((2, hidden // SIDE**2, columns), jnp.bfloat16)
    window = 896
    count = 2 * len(numbers)
    return pl.pallas_call(
        functools.partial(diagonal_kernel, numbers),
        in_specs=[SMEM] + [ANY] * 2 + [VMEM] * 2,
        out_specs=[VMEM] * len(numbers),
        out_shape=[out] * len(numbers),
        scratch_shapes=[
            pltpu.VMEM((count, 2 * tokens, window), jnp.bfloat16),
            pltpu.VMEM((2 * tokens, columns), jnp.bfloat16),
            pltpu.VMEM((window, columns), jnp.bfloat16),
            pltpu.SemaphoreType.DMA((count, 2)),
        ],
        cost_estimate=pl.CostEstimate(
            flops=4 * count * tokens * window * columns,
            bytes_accessed=4 * count * tokens * window,
            transcendentals=0,
        ),
        compiler_params=pltpu.CompilerParams(vmem_limit_bytes=52 << 20),
        name="diagonal_grad",
    )(table, mine, other, reduced, reduced_other)


def total_of(parts, *index):
    total = parts[0][index].astype(jnp.float32)
    for part in parts[1:]:
        total += part[index].astype(jnp.float32)
    return total


def halves_kernel(at_ref, *refs):
    parts, outs = refs[:4], refs[4:6]
    half = outs[0].shape[2]
    for which in range(2):

        @pl.when(at_ref[CORE] == which)
        def _():
            for j in range(2):
                total = total_of(parts, j).astype(outs[0].dtype)
                outs[which][j] = total[:, :half]
                outs[1 - which][j] = total[:, half:]


def sum_halves(table, parts):
    blocks, block, columns = parts[0].shape
    out = jax.ShapeDtypeStruct((blocks, block, columns // 2), jnp.bfloat16)
    return in_vmem(halves_kernel, "sum_halves", [out, out], *parts, table=table)


def quarters_kernel(at_ref, *refs):
    sides, out = refs[:2], refs[2]
    rows = out.shape[1]
    for which in range(2):

        @pl.when(at_ref[CORE] == which)
        def _():
            for k in range(SIDE):
                block = sides[(k // 2 + which) % 2][k % 2]
                for i in range(SIDE):
                    out[SIDE * k + i] = block[i * rows : (i + 1) * rows]


def in_quarters(table, mine, other):
    blocks, block, half = mine.shape
    return in_vmem(
        quarters_kernel, "in_quarters",
        jax.ShapeDtypeStruct((2 * blocks * SIDE, block // SIDE, half), jnp.bfloat16),
        mine, other, table=table,
    )


def update_kernel(
    at_ref, direction_ref, projector_ref, weight_ref, out_ref,
    direction, projectors, weights, outs, sems,
):
    parts, depth = projectors.shape[:2]
    contract = (((1,), (1,)), ((), ()))
    places = [
        pl.ds(pl.multiple_of(at_ref[PLACE + i] * depth, depth), depth) for i in range(parts)
    ]
    loads, stores = [], []
    for i, place in enumerate(places):
        loads.append(
            [
                pltpu.make_async_copy(
                    projector_ref.at[pl.ds(i * depth, depth)], projectors.at[i], sems.at[0, i]
                ),
                pltpu.make_async_copy(weight_ref.at[:, place], weights.at[i], sems.at[1, i]),
            ]
        )
        for copy in loads[-1]:
            copy.start()
    pieces, rows, columns = direction_ref.shape
    for i in range(pieces):
        direction[
            i // 2 * rows : (i // 2 + 1) * rows, i % 2 * columns : (i % 2 + 1) * columns
        ] = direction_ref[i]
    for i, place in enumerate(places):
        for copy in loads[i]:
            copy.wait()
        delta = lax.dot_general(
            direction[...], projectors[i], contract, preferred_element_type=jnp.float32
        )
        outs[i] = (weights[i].astype(jnp.float32) - step_size * delta).astype(outs.dtype)
        stores.append(pltpu.make_async_copy(outs.at[i], out_ref.at[:, place], sems.at[2, i]))
        stores[-1].start()
    for copy in stores:
        copy.wait()


def update(table, direction, projector, weight):
    block, width = weight.shape
    rank = projector.shape[1]
    parts = 8
    depth = width // parts
    return pl.pallas_call(
        update_kernel,
        in_specs=[SMEM, VMEM, ANY, ANY],
        out_specs=ANY,
        out_shape=jax.ShapeDtypeStruct(weight.shape, weight.dtype),
        scratch_shapes=[
            pltpu.VMEM((block, rank), direction.dtype),
            pltpu.VMEM((parts, depth, rank), projector.dtype),
            pltpu.VMEM((parts, block, depth), weight.dtype),
            pltpu.VMEM((parts, block, depth), weight.dtype),
            pltpu.SemaphoreType.DMA((3, parts)),
        ],
        cost_estimate=pl.CostEstimate(
            flops=2 * block * width * rank,
            bytes_accessed=4 * block * width + 2 * width * rank,
            transcendentals=0,
        ),
        compiler_params=pltpu.CompilerParams(vmem_limit_bytes=58 << 20),
        name="update",
    )(table, direction, projector, weight)


def exchange(array, distance):
    pairs = []
    for i in range(SIDE):
        for j in range(SIDE):
            pairs.append(((SIDE * i + j) * 2, (SIDE * ((i - distance) % SIDE) + j) * 2))
            pairs.append(((SIDE * i + j) * 2 + 1, (SIDE * i + (j + distance) % SIDE) * 2 + 1))
    return lax.ppermute(array, ("y", "z", "core"), pairs)


def on_device(activations, out_grad, projector, weight, first_moment, second_moment):
    y, z, x, core = (lax.axis_index(name) for name in ("y", "z", "x", "core"))
    depth, rank = projector.shape
    half = rank // 2
    scale = 1.0 / math.sqrt(activations.shape[0] * SIDE**3 * 2)

    def own(array, axis):
        return lax.dynamic_slice_in_dim(array, core * half, half, axis)

    def others(array, axis):
        return lax.dynamic_slice_in_dim(array, (1 - core) * half, half, axis)

    def swap(array):
        return lax.ppermute(array, "core", SWAP)

    firsts = [
        SIDE * j + lax.rem(z - y + 2 * core + j + SIDE + distance, SIDE)
        for distance in DISTANCES
        for j in range(2)
    ]
    places = [
        2 * lax.rem(x + r, SIDE) + which for r in (0, 1, 3, 2) for which in (core, 1 - core)
    ]
    table = jnp.stack([core, *firsts, *places]).astype(jnp.int32)
    table, projector, out_grad = lax.optimization_barrier((table, projector, out_grad))

    def product(place, part):
        return jnp.dot(
            lax.dynamic_slice_in_dim(activations, places[place] * depth, depth, 1),
            part,
            preferred_element_type=jnp.float32,
        )

    near = [hop(projector, "x", -1), hop(projector, "x", 1)]
    here = [projector, swap(projector)]
    other = swap(out_grad)
    total = product(0, here[0]) + product(1, here[1])
    near, total = lax.optimization_barrier((near, total))
    half_depth = depth // 2
    far = [hop(near[1][:half_depth], "x", 1), hop(near[0][half_depth:], "x", -1)]
    near = [near[0], swap(near[0]), near[1], swap(near[1])]
    for place, part in enumerate(near):
        total += product(2 + place, part)
    far, total = lax.optimization_barrier((far, total))
    far = [jnp.concatenate(far, axis=0)]
    far += [swap(far[0])]
    for place, part in enumerate(far):
        total += product(6 + place, part)
    reduced = total.astype(jnp.bfloat16)
    reduced_other = swap(reduced)

    first_moment, second_moment, _ = lax.optimization_barrier(
        (first_moment, second_moment, near[0])
    )
    moments = jnp.stack([first_moment, second_moment])
    rows = moments.shape[1]
    moments_other = swap(others(moments, 2))
    moments_own = own(moments, 2)
    moments = jnp.where(
        core == 0,
        jnp.concatenate([moments_own, moments_other], axis=1),
        jnp.concatenate([moments_other, moments_own], axis=1),
    )
    weight, _ = lax.optimization_barrier((weight, far[0]))
    weight_all = lax.all_gather(weight, ("x", "core"), axis=0, tiled=True)

    sums = []
    for number, distance in enumerate(DISTANCES):
        (part,) = diagonal_grad((number,), table, out_grad, other, reduced, reduced_other)
        sums.append(exchange(part, distance) if distance else part)
    parts = [*here, *near, *far]
    sums[3], parts = lax.optimization_barrier((sums[3], parts))
    projector_all = jnp.concatenate(parts, axis=0)
    mine, other = sum_halves(table, sums)
    quarters = lax.all_to_all(
        in_quarters(table, mine, swap(other)), ("y", "z", "x"), 0, 0, tiled=True,
        axis_index_groups=[
            [
                (i * SIDE + (i + diagonal) % SIDE) * SIDE + j
                for i in range(SIDE)
                for j in range(SIDE)
            ]
            for diagonal in range(SIDE)
        ],
    )
    grad = jnp.sum(quarters.astype(jnp.float32), axis=0)
    grad = grad * scale

    new_first = beta_first * moments[0] + (1.0 - beta_first) * grad
    new_second = beta_second * moments[1] + (1.0 - beta_second) * grad * grad
    direction = (
        new_first / correct_first / (jnp.sqrt(new_second / correct_second) + epsilon)
    ).astype(jnp.bfloat16)

    direction, projector_all = lax.optimization_barrier((direction, projector_all))
    direction = lax.all_gather(direction, ("x", "core"), axis=0)
    new_first, new_second, direction = lax.optimization_barrier(
        (new_first, new_second, direction)
    )
    new_weight = update(table, direction, projector_all, weight_all.T).T

    news = jnp.stack([new_first, new_second])
    kept = lax.dynamic_slice_in_dim(news, core * rows, rows, 1)
    came = swap(lax.dynamic_slice_in_dim(news, (1 - core) * rows, rows, 1))
    news = jnp.where(
        core == 0,
        jnp.concatenate([kept, came], axis=2),
        jnp.concatenate([came, kept], axis=2),
    )
    return (new_weight, news[0], news[1])


def solution(mesh):
    grid = Mesh(mesh.devices.reshape(SIDE, SIDE, SIDE, 2), ("y", "z", "x", "core"))
    everywhere, group = ("y", "z", "x", "core"), ("x", "core")
    in_specs = (
        P(everywhere, None),
        P(everywhere, None),
        P(group, None),
        P(group, ("y", "z")),
        P(everywhere, None),
        P(everywhere, None),
    )
    out_specs = (P(None, ("y", "z")), P(everywhere, None), P(everywhere, None))
    return jax.shard_map(
        on_device, mesh=grid, in_specs=in_specs, out_specs=out_specs, check_vma=False
    )
```

time: 187 us -> 159 us (0.85)
  waiting for transfers between devices: 76.6 us -> 40.5 us
  Pallas kernels: 16.3 us -> 35.7 us
  matrix products: 24 us -> 9.12 us
  blocking collectives: 13.3 us -> 16.1 us
  other arithmetic: 6.41 us -> 4.26 us
    all_gather x1 -> x0, waiting for transfers between devices: 36.7 us -> none  [on_device(): projector_all = lax.all_gather(projector, ('x', 'core'), axis=0, tiled=True)]
    pallas_call x1 -> x7, Pallas kernels: 16.3 us -> 35.7 us  [the longest x4 24.7 us: diagonal_grad(): pl.pallas_call(functools.partial(diagonal_kernel, numbers), in_specs=[SME...]
    ppermute x4 -> x12, waiting for transfers between devices: 2.42 us -> 19.7 us  [the longest x3 11.8 us: exchange(): return lax.ppermute(array, ('y', 'z', 'core'), pairs)]
    dot_general x3 -> x8, matrix products: 24 us -> 9.12 us  [product(): jnp.dot(lax.dynamic_slice_in_dim(activations, places[place] * depth, dept...]
    ppermute x6 -> x4, waiting for transfers between devices: 23.7 us -> 11.2 us  [hop(): lax.ppermute(array, axis, [(i, (i + distance) % SIDE) for i in range(SIDE)])]
    unnamed x5 -> x32, local copies, waits for them, and re-layouts: 0.8 us -> 8.53 us
    convert_element_type x2 -> x0, other arithmetic: 4.88 us -> none  [the longest x1 2.77 us: on_device(): b = sum_along(b, 'z', z).astype(jnp.bfloat16)]
    ppermute x6 -> x4, starting transfers between devices: 9.62 us -> 5.3 us  [hop(): lax.ppermute(array, axis, [(i, (i + distance) % SIDE) for i in range(SIDE)])]
  transfers between devices with their start and end apart: 14 -> 18, of which waited for: 7 -> 10; matrix products, arithmetic and copies ran while one was open for 16% -> 14% of each run, Pallas kernels for 9% -> 22%
where the time goes in v2:
time: 159 us
  waiting for transfers between devices  40.5 us (25%)
  Pallas kernels  35.7 us (22%)
  starting transfers between devices  27.7 us (17%)
  blocking collectives  16.1 us (10%)
  between operations  14.3 us (9%)
  local copies, waits for them, and re-layouts  11.3 us (7%)
  matrix products  9.12 us (6%)
  other arithmetic  4.26 us (3%)
    pallas_call x4, Pallas kernels, diagonal_grad(): pl.pallas_call(functools.partial(diagonal_kernel, numbers), in_specs=[SME...  24.7 us
    all_gather x1, blocking collectives, on_device(): direction = lax.all_gather(direction, ('x', 'core'), axis=0)  16.1 us
    ppermute x3, waiting for transfers between devices, exchange(): return lax.ppermute(array, ('y', 'z', 'core'), pairs)  11.8 us
    ppermute x4, waiting for transfers between devices, hop(): lax.ppermute(array, axis, [(i, (i + distance) % SIDE) for i in range(SIDE)])  11.2 us
    all_to_all x1, starting transfers between devices, on_device(): lax.all_to_all(in_quarters(table, mine, swap(other)), ('y', 'z', 'x'), 0,...  10.4 us
    all_to_all x1, waiting for transfers between devices, on_device(): lax.all_to_all(in_quarters(table, mine, swap(other)), ('y', 'z', 'x'), 0,...  9.53 us
    dot_general x8, matrix products, product(): jnp.dot(lax.dynamic_slice_in_dim(activations, places[place] * depth, dept...  9.12 us
    unnamed x32, local copies, waits for them, and re-layouts  8.53 us
  transfers between devices with their start and end apart: 18, of which 10 were waited for; matrix products, arithmetic and copies ran while one was open for 14% of the time, Pallas kernels for 22%

profile of v2, /device:TPU:1, one launch (start us, length us, event | category | flops | bytes accessed | tf_op | source)
XLA Modules:
  0.0 159.0 jit_solution(7085433235316686413)
XLA Ops:
  7.4 1.5 collective-permute-start.4
  8.9 2.6 %collective-permute-start = (bf16[512,512]{1,0:T(8,128)(2,1)}, bf16[512,512]{1,0:T(8,128)(2,1)S(1)}, u32[]{:S(2)}, u32[]{:S(2)}) collective-permute-start(bf16[512,512]{1,0:T(8,128)(2,1)} %param.8), channel_id=1, source_target_pairs={{0,6},{2,0},{4,2},{6,4},{1,7},{3,1},{5,3},{7,5},{8,14},{10,8},{12,... | collective-permute-start | bytes 1572872 | tf_op jit(solution)/shard_map/ppermute | solution.py:26
  11.5 1.9 %fusion.17 = f32[640,512]{1,0:T(8,128)S(1)} fusion(bf16[512,512]{1,0:T(8,128)(2,1)} %param.8, bf16[640,4096]{1,0:T(8,128)(2,1)} %param.6, s32[]{:T(128)S(6)} %select_n.53), kind=kOutput, calls=%fused_computation.17 | convolution fusion | flops 335544320 | bytes 2490372 | tf_op jit(solution)/shard_map/dot_general | solution.py:266
  13.4 2.8 %collective-permute-done.2 = bf16[512,512]{1,0:T(8,128)(2,1)S(1)} collective-permute-done((bf16[512,512]{1,0:T(8,128)(2,1)}, bf16[512,512]{1,0:T(8,128)(2,1)S(1)}, u32[]{:S(2)}, u32[]{:S(2)}) %collective-permute-start.2) | collective-permute-done | bytes 524320 | tf_op jit(solution)/shard_map/ppermute | solution.py:252
  16.2 1.8 %convolution_add_fusion = f32[640,512]{1,0:T(8,128)S(1)} fusion(f32[640,512]{1,0:T(8,128)S(1)} %fusion.17, bf16[512,512]{1,0:T(8,128)(2,1)S(1)} %collective-permute-done.2, bf16[640,4096]{1,0:T(8,128)(2,1)} %param.6, s32[]{:T(128)S(6)} %select_n.54), kind=kOutput, calls=%fused_computation.1 | convolution fusion | flops 335872000 | bytes 3801092 | tf_op jit(solution)/shard_map/dot_general | solution.py:266
  18.0 4.7 %collective-permute-done = bf16[512,512]{1,0:T(8,128)(2,1)S(1)} collective-permute-done((bf16[512,512]{1,0:T(8,128)(2,1)}, bf16[512,512]{1,0:T(8,128)(2,1)S(1)}, u32[]{:S(2)}, u32[]{:S(2)}) %collective-permute-start) | collective-permute-done | bytes 524320 | tf_op jit(solution)/shard_map/ppermute | solution.py:26
  22.7 3.0 %collective-permute-done.1 = bf16[512,512]{1,0:T(8,128)(2,1)S(1)} collective-permute-done((bf16[512,512]{1,0:T(8,128)(2,1)}, bf16[512,512]{1,0:T(8,128)(2,1)S(1)}, u32[]{:S(2)}, u32[]{:S(2)}) %collective-permute-start.1) | collective-permute-done | bytes 524320 | tf_op jit(solution)/shard_map/ppermute | solution.py:26
  25.7 1.7 %collective-permute-start.7 = (bf16[512,512]{1,0:T(8,128)(2,1)S(1)}, bf16[512,512]{1,0:T(8,128)(2,1)S(1)}, u32[]{:S(2)}, u32[]{:S(2)}) collective-permute-start(bf16[512,512]{1,0:T(8,128)(2,1)S(1)} %collective-permute-done), channel_id=1, source_target_pairs={{0,1},{1,0},{2,3},{3,2},{4,5},{5,4},{6,7},{7,6},{8,9},{9,8},{10,11... | collective-permute-start | bytes 1572872 | tf_op jit(solution)/shard_map/ppermute | solution.py:252
  27.6 2.7 %collective-permute-start.6 = (bf16[256,512]{1,0:T(8,128)(2,1)S(1)}, bf16[256,512]{1,0:T(8,128)(2,1)S(1)}, u32[]{:S(2)}, u32[]{:S(2)}) collective-permute-start(bf16[256,512]{1,0:T(8,128)(2,1)S(1)} %slice.20), channel_id=1, source_target_pairs={{0,6},{2,0},{4,2},{6,4},{1,7},{3,1},{5,3},{7,5},{8,14},{10,8},{12,... | collective-permute-start | bytes 786440 | tf_op jit(solution)/shard_map/ppermute | solution.py:26
  32.7 3.6 %collective-permute-done.5 = bf16[256,512]{1,0:T(8,128)(2,1)S(1)} collective-permute-done((bf16[256,512]{1,0:T(8,128)(2,1)S(1)}, bf16[256,512]{1,0:T(8,128)(2,1)S(1)}, u32[]{:S(2)}, u32[]{:S(2)}) %collective-permute-start.5) | collective-permute-done | bytes 262176 | tf_op jit(solution)/shard_map/ppermute | solution.py:26
  36.3 1.3 collective-permute-start.9
  37.7 1.6 fusion.4
  39.3 1.8 %add_convert_fusion.reduced_ref = bf16[640,512]{1,0:T(8,128)(2,1)S(1)} fusion(f32[640,512]{1,0:T(8,128)S(1)} %add_add_fusion, f32[640,512]{1,0:T(8,128)S(1)} %fusion.4, bf16[512,512]{1,0:T(8,128)(2,1)} %collective-permute-done.9, bf16[640,4096]{1,0:T(8,128)(2,1)} %param.6, s32[]{:T(128)S(6)} %select_n.63), kind=kOutput, calls=%fused_computation.2 | convolution fusion | flops 336527360 | bytes 4456452 | tf_op jit(solution)/shard_map/dot_general | solution.py:266
  41.6 1.7 %collective-permute-done.10.reduced_other_ref = bf16[640,512]{1,0:T(8,128)(2,1)S(1)} collective-permute-done((bf16[640,512]{1,0:T(8,128)(2,1)S(1)}, bf16[640,512]{1,0:T(8,128)(2,1)S(1)}, u32[]{:S(2)}, u32[]{:S(2)}) %collective-permute-start.10) | collective-permute-done | bytes 655392 | tf_op jit(solution)/shard_map/ppermute | solution.py:252
  43.3 6.2 %diagonal_grad.4 = bf16[2,688,512]{2,1,0:T(8,128)(2,1)} custom-call(s32[17]{0:T(128)S(1)} %stack.89.at_ref, bf16[640,11008]{1,0:T(8,128)(2,1)} %mine_ref.3, bf16[640,11008]{1,0:T(8,128)(2,1)} %collective-permute-done.4.other_ref, bf16[640,512]{1,0:T(8,128)(2,1)S(1)} %add_convert_fusion.reduced_ref, bf16[640,512]{1,0:T(8,128)(2,1)S(1)} %collective-permute-done.10.reduced_other_ref), custom_call_target="tpu_custom_call" | custom-call | flops 2348810240 | bytes 4587520 | tf_op jit(solution)/shard_map/diagonal_grad/pallas_call | solution.py:95
  49.5 3.7 %collective-permute-start.11 = (bf16[2,688,512]{2,1,0:T(8,128)(2,1)}, bf16[2,688,512]{2,1,0:T(8,128)(2,1)S(1)}, u32[]{:S(2)}, u32[]{:S(2)}) collective-permute-start(bf16[2,688,512]{2,1,0:T(8,128)(2,1)} %diagonal_grad.4), channel_id=1, source_target_pairs={{0,64},{1,17},{8,72},{9,25},{16,80},{17,1},{24,88},{25,9},{32,96},... | collective-permute-start | bytes 4227080 | tf_op jit(solution)/shard_map/ppermute | solution.py:236
  53.2 6.2 %diagonal_grad.5 = bf16[2,688,512]{2,1,0:T(8,128)(2,1)} custom-call(s32[17]{0:T(128)S(1)} %stack.89.at_ref, bf16[640,11008]{1,0:T(8,128)(2,1)} %mine_ref.3, bf16[640,11008]{1,0:T(8,128)(2,1)} %collective-permute-done.4.other_ref, bf16[640,512]{1,0:T(8,128)(2,1)S(1)} %add_convert_fusion.reduced_ref, bf16[640,512]{1,0:T(8,128)(2,1)S(1)} %collective-permute-done.10.reduced_other_ref), custom_call_target="tpu_custom_call" | custom-call | flops 2348810240 | bytes 4587520 | tf_op jit(solution)/shard_map/diagonal_grad/pallas_call | solution.py:95
  60.0 6.2 %diagonal_grad.6 = bf16[2,688,512]{2,1,0:T(8,128)(2,1)} custom-call(s32[17]{0:T(128)S(1)} %stack.89.at_ref, bf16[640,11008]{1,0:T(8,128)(2,1)} %mine_ref.3, bf16[640,11008]{1,0:T(8,128)(2,1)} %collective-permute-done.4.other_ref, bf16[640,512]{1,0:T(8,128)(2,1)S(1)} %add_convert_fusion.reduced_ref, bf16[640,512]{1,0:T(8,128)(2,1)S(1)} %collective-permute-done.10.reduced_other_ref), custom_call_target="tpu_custom_call" | custom-call | flops 2348810240 | bytes 4587520 | tf_op jit(solution)/shard_map/diagonal_grad/pallas_call | solution.py:95
  67.3 6.2 %diagonal_grad.7.refs_3_ = bf16[2,688,512]{2,1,0:T(8,128)(2,1)} custom-call(s32[17]{0:T(128)S(1)} %stack.89.at_ref, bf16[640,11008]{1,0:T(8,128)(2,1)} %mine_ref.3, bf16[640,11008]{1,0:T(8,128)(2,1)} %collective-permute-done.4.other_ref, bf16[640,512]{1,0:T(8,128)(2,1)S(1)} %add_convert_fusion.reduced_ref, ...), custom_call_target="tpu_custom_call" | custom-call | flops 2348810240 | bytes 4587520 | tf_op jit(solution)/shard_map/diagonal_grad/pallas_call | solution.py:95
  73.5 11.8 %collective-permute-done.12.refs_1_ = bf16[2,688,512]{2,1,0:T(8,128)(2,1)S(1)} collective-permute-done((bf16[2,688,512]{2,1,0:T(8,128)(2,1)}, bf16[2,688,512]{2,1,0:T(8,128)(2,1)S(1)}, u32[]{:S(2)}, u32[]{:S(2)}) %collective-permute-start.12) | collective-permute-done | bytes 1409056 | tf_op jit(solution)/shard_map/ppermute | solution.py:236
  85.3 1.4 copy-done
  88.4 1.8 %collective-permute-done.14.refs_1_ = bf16[2,688,256]{2,1,0:T(8,128)(2,1)S(1)} collective-permute-done((bf16[2,688,256]{2,1,0:T(8,128)(2,1)S(1)}, bf16[2,688,256]{2,1,0:T(8,128)(2,1)S(1)}, u32[]{:S(2)}, u32[]{:S(2)}) %collective-permute-start.14) | collective-permute-done | bytes 704544 | tf_op jit(solution)/shard_map/ppermute | solution.py:252
  90.2 1.8 %in_quarters.1 = bf16[16,172,256]{2,1,0:T(8,128)(2,1)} custom-call(s32[17]{0:T(128)S(1)} %stack.89.at_ref, bf16[2,688,256]{2,1,0:T(8,128)(2,1)S(1)} %get-tuple-element.43.refs_0_, bf16[2,688,256]{2,1,0:T(8,128)(2,1)S(1)} %collective-permute-done.14.refs_1_), custom_call_target="tpu_custom_call" | custom-call | tf_op jit(solution)/shard_map/in_quarters/pallas_call | solution.py:36
  92.0 10.4 %all-to-all-start = ((bf16[16,172,256]{2,1,0:T(8,128)(2,1)}), bf16[16,172,256]{2,1,0:T(8,128)(2,1)S(1)}, u32[]{:S(2)}, u32[]{:S(2)}) async-start(bf16[16,172,256]{2,1,0:T(8,128)(2,1)} %in_quarters.1), calls=%async_computation | async-start | bytes 2883584 | tf_op jit(solution)/shard_map/all_to_all | solution.py:313
  102.4 1.8 %fusion.22 = (f32[2,86,256]{2,1,0:T(8,128)}, f32[2,86,256]{2,1,0:T(8,128)}) fusion(s32[]{:T(128)S(6)} %select_n.55, f32[1,86,512]{2,1,0:T(8,128)} %bitcast.51, f32[1,86,512]{2,1,0:T(8,128)} %bitcast.52, s32[]{:T(128)S(6)} %select_n.56), kind=kLoop, calls=%fused_computation.32 | loop fusion | flops 88064 | bytes 704520 | tf_op jit(solution)/shard_map/stack | solution.py:293
  104.9 1.4 collective-permute-done.3
  106.3 2.0 %maximum_select_fusion = f32[2,172,256]{2,1,0:T(8,128)} fusion(f32[2,86,256]{2,1,0:T(8,128)} %collective-permute-done.3, f32[2,86,256]{2,1,0:T(8,128)} %get-tuple-element.66, pred[]{:T(512)S(6)} %eq.4), kind=kLoop, calls=%fused_computation.27 | loop fusion | flops 264192 | bytes 704513 | tf_op jit(solution)/shard_map/jit(_where)/select_n | solution.py:297
  109.1 1.9 %constant_dynamic-update-slice_fusion.8 = bf16[4096,512]{1,0:T(8,128)(2,1)} fusion(bf16[4096,512]{1,0:T(8,128)(2,1)} %constant_dynamic-update-slice_fusion.9, bf16[512,512]{1,0:T(8,128)(2,1)} %copy-done.6), kind=kLoop, calls=%fused_computation.50 | loop fusion | bytes 1048576
  115.2 1.9 %constant_dynamic-update-slice_fusion.2.projector_ref = bf16[4096,512]{1,0:T(8,128)(2,1)} fusion(bf16[4096,512]{1,0:T(8,128)(2,1)} %constant_dynamic-update-slice_fusion.3, bf16[512,512]{1,0:T(8,128)(2,1)} %collective-permute-done.9), kind=kLoop, calls=%fused_computation.44 | loop fusion | bytes 1048576 | tf_op jit(solution)/shard_map/concatenate | solution.py:311
  117.0 9.5 %all-to-all-done = bf16[16,172,256]{2,1,0:T(8,128)(2,1)S(1)} async-done(((bf16[16,172,256]{2,1,0:T(8,128)(2,1)}), bf16[16,172,256]{2,1,0:T(8,128)(2,1)S(1)}, u32[]{:S(2)}, u32[]{:S(2)}) %all-to-all-start) | async-done | bytes 1409056 | tf_op jit(solution)/shard_map/all_to_all | solution.py:313
  126.9 16.1 %all-gather.1.direction_ref = bf16[8,172,256]{2,1,0:T(8,128)(2,1)} all-gather(bf16[1,172,256]{2,1,0:T(8,128)(2,1)S(1)} %bitcast.50), channel_id=2, replica_groups=mesh['y'=4,'z'=4,'x'=4,'core'=2] {'x','core'}, dimensions={0}, use_global_device_ids=true | all-gather | bytes 792576 | tf_op jit(solution)/shard_map/all_gather | solution.py:334
  143.4 8.0 %update.1 = bf16[688,4096]{1,0:T(8,128)(2,1)} custom-call(s32[17]{0:T(128)} %copy-done.1, bf16[8,172,256]{2,1,0:T(8,128)(2,1)} %all-gather.1.direction_ref, bf16[4096,512]{1,0:T(8,128)(2,1)} %constant_dynamic-update-slice_fusion.2.projector_ref, bf16[688,4096]{1,0:T(8,128)(2,1)} %bitcast.46), custom_call_target="tpu_custom_call" | custom-call | flops 2885681152 | bytes 15466496 | tf_op jit(solution)/shard_map/update/pallas_call | solution.py:208
  (65 shorter events, 13.9 us)
Async XLA Ops:
  7.2 136.2 %all-gather.4.cloned.1.call-start = ((), (), s32[]{:S(2)}) async-start(), calls=%async_computation.1 | async-start | bytes 6340608 | tf_op jit(solution)/shard_map/all_gather | solution.py:303
  7.3 82.9 %copy-start.1 = (s32[17]{0:T(128)}, s32[17]{0:T(128)S(1)}, u32[]{:S(2)}) copy-start(s32[17]{0:T(128)S(1)} %stack.89.at_ref) | copy-start | bytes 208
  7.4 35.9 %collective-permute-start.4 = (bf16[640,11008]{1,0:T(8,128)(2,1)}, bf16[640,11008]{1,0:T(8,128)(2,1)}, u32[]{:S(2)}, u32[]{:S(2)}) collective-permute-start(bf16[640,11008]{1,0:T(8,128)(2,1)} %mine_ref.3), channel_id=1, source_target_pairs={{0,1},{1,0},{2,3},{3,2},{4,5},{5,4},{6,7},{7,6},{8,9},{9,8},{10,11... | collective-permute-start | bytes 42270728 | tf_op jit(solution)/shard_map/ppermute | solution.py:252
  8.9 7.4 %collective-permute-start.2 = (bf16[512,512]{1,0:T(8,128)(2,1)}, bf16[512,512]{1,0:T(8,128)(2,1)S(1)}, u32[]{:S(2)}, u32[]{:S(2)}) collective-permute-start(bf16[512,512]{1,0:T(8,128)(2,1)} %param.8), channel_id=1, source_target_pairs={{0,1},{1,0},{2,3},{3,2},{4,5},{5,4},{6,7},{7,6},{8,9},{9,8},{10,11... | collective-permute-start | bytes 1572872 | tf_op jit(solution)/shard_map/ppermute | solution.py:252
  8.9 13.8 %collective-permute-start = (bf16[512,512]{1,0:T(8,128)(2,1)}, bf16[512,512]{1,0:T(8,128)(2,1)S(1)}, u32[]{:S(2)}, u32[]{:S(2)}) collective-permute-start(bf16[512,512]{1,0:T(8,128)(2,1)} %param.8), channel_id=1, source_target_pairs={{0,6},{2,0},{4,2},{6,4},{1,7},{3,1},{5,3},{7,5},{8,14},{10,8},{12,... | collective-permute-start | bytes 1572872 | tf_op jit(solution)/shard_map/ppermute | solution.py:26
  11.5 14.2 %collective-permute-start.1 = (bf16[512,512]{1,0:T(8,128)(2,1)}, bf16[512,512]{1,0:T(8,128)(2,1)S(1)}, u32[]{:S(2)}, u32[]{:S(2)}) collective-permute-start(bf16[512,512]{1,0:T(8,128)(2,1)} %param.8), channel_id=1, source_target_pairs={{0,2},{2,4},{4,6},{6,0},{1,3},{3,5},{5,7},{7,1},{8,10},{10,12},{12... | collective-permute-start | bytes 1572872 | tf_op jit(solution)/shard_map/ppermute | solution.py:26
  11.5 18.7 %copy-start.2 = (bf16[640,4096]{1,0:T(8,128)(2,1)S(1)}, bf16[640,4096]{1,0:T(8,128)(2,1)}, u32[]{:S(2)}) copy-start(bf16[640,4096]{1,0:T(8,128)(2,1)} %param.6) | copy-start | bytes 15728644
  16.2 15.0 %copy-start.6 = (bf16[512,512]{1,0:T(8,128)(2,1)}, bf16[512,512]{1,0:T(8,128)(2,1)S(1)}, u32[]{:S(2)}) copy-start(bf16[512,512]{1,0:T(8,128)(2,1)S(1)} %collective-permute-done.2) | copy-start | bytes 1572868
  25.7 5.6 %collective-permute-start.7 = (bf16[512,512]{1,0:T(8,128)(2,1)S(1)}, bf16[512,512]{1,0:T(8,128)(2,1)S(1)}, u32[]{:S(2)}, u32[]{:S(2)}) collective-permute-start(bf16[512,512]{1,0:T(8,128)(2,1)S(1)} %collective-permute-done), channel_id=1, source_target_pairs={{0,1},{1,0},{2,3},{3,2},{4,5},{5,4},{6,7},{7,6},{8,9},{9,8},{10,11... | collective-permute-start | bytes 1572872 | tf_op jit(solution)/shard_map/ppermute | solution.py:252
  27.4 4.7 %collective-permute-start.8 = (bf16[512,512]{1,0:T(8,128)(2,1)S(1)}, bf16[512,512]{1,0:T(8,128)(2,1)S(1)}, u32[]{:S(2)}, u32[]{:S(2)}) collective-permute-start(bf16[512,512]{1,0:T(8,128)(2,1)S(1)} %collective-permute-done.1), channel_id=1, source_target_pairs={{0,1},{1,0},{2,3},{3,2},{4,5},{5,4},{6,7},{7,6},{8,9},{9,8},{10,11... | collective-permute-start | bytes 1572872 | tf_op jit(solution)/shard_map/ppermute | solution.py:252
  27.5 8.7 %collective-permute-start.5 = (bf16[256,512]{1,0:T(8,128)(2,1)S(1)}, bf16[256,512]{1,0:T(8,128)(2,1)S(1)}, u32[]{:S(2)}, u32[]{:S(2)}) collective-permute-start(bf16[256,512]{1,0:T(8,128)(2,1)S(1)} %slice.19), channel_id=1, source_target_pairs={{0,2},{2,4},{4,6},{6,0},{1,3},{3,5},{5,7},{7,1},{8,10},{10,12},{12... | collective-permute-start | bytes 786440 | tf_op jit(solution)/shard_map/ppermute | solution.py:26
  27.6 8.7 %collective-permute-start.6 = (bf16[256,512]{1,0:T(8,128)(2,1)S(1)}, bf16[256,512]{1,0:T(8,128)(2,1)S(1)}, u32[]{:S(2)}, u32[]{:S(2)}) collective-permute-start(bf16[256,512]{1,0:T(8,128)(2,1)S(1)} %slice.20), channel_id=1, source_target_pairs={{0,6},{2,0},{4,2},{6,4},{1,7},{3,1},{5,3},{7,5},{8,14},{10,8},{12,... | collective-permute-start | bytes 786440 | tf_op jit(solution)/shard_map/ppermute | solution.py:26
  31.3 0.8 copy-start.7
  32.1 4.1 %copy-start.9 = (bf16[512,512]{1,0:T(8,128)(2,1)}, bf16[512,512]{1,0:T(8,128)(2,1)S(1)}, u32[]{:S(2)}) copy-start(bf16[512,512]{1,0:T(8,128)(2,1)S(1)} %collective-permute-done.8) | copy-start | bytes 1572868
  36.3 13.2 %copy-start.3 = (bf16[512,512]{1,0:T(8,128)(2,1)}, bf16[512,512]{1,0:T(8,128)(2,1)S(1)}, u32[]{:S(2)}) copy-start(bf16[512,512]{1,0:T(8,128)(2,1)S(1)} %constant_dynamic-update-slice_fusion) | copy-start | bytes 1572868
  36.3 3.0 %collective-permute-start.9 = (bf16[512,512]{1,0:T(8,128)(2,1)S(1)}, bf16[512,512]{1,0:T(8,128)(2,1)}, u32[]{:S(2)}, u32[]{:S(2)}) collective-permute-start(bf16[512,512]{1,0:T(8,128)(2,1)S(1)} %constant_dynamic-update-slice_fusion), channel_id=1, source_target_pairs={{0,1},{1,0},{2,3},{3,2},{4,5},{5,4},{6,7},{7,6},{8,9},{9,8},{10,11... | collective-permute-start | bytes 1572872 | tf_op jit(solution)/shard_map/ppermute | solution.py:252
  41.1 2.2 %collective-permute-start.10 = (bf16[640,512]{1,0:T(8,128)(2,1)S(1)}, bf16[640,512]{1,0:T(8,128)(2,1)S(1)}, u32[]{:S(2)}, u32[]{:S(2)}) collective-permute-start(bf16[640,512]{1,0:T(8,128)(2,1)S(1)} %add_convert_fusion.reduced_ref), channel_id=1, source_target_pairs={{0,1},{1,0},{2,3},{3,2},{4,5},{5,4},{6,7},{7,6},{8,9},{9,8},{10,11... | collective-permute-start | bytes 1966088 | tf_op jit(solution)/shard_map/ppermute | solution.py:252
  49.5 24.0 %collective-permute-start.11 = (bf16[2,688,512]{2,1,0:T(8,128)(2,1)}, bf16[2,688,512]{2,1,0:T(8,128)(2,1)S(1)}, u32[]{:S(2)}, u32[]{:S(2)}) collective-permute-start(bf16[2,688,512]{2,1,0:T(8,128)(2,1)} %diagonal_grad.4), channel_id=1, source_target_pairs={{0,64},{1,17},{8,72},{9,25},{16,80},{17,1},{24,88},{25,9},{32,96},... | collective-permute-start | bytes 4227080 | tf_op jit(solution)/shard_map/ppermute | solution.py:236
  59.3 26.0 %collective-permute-start.12 = (bf16[2,688,512]{2,1,0:T(8,128)(2,1)}, bf16[2,688,512]{2,1,0:T(8,128)(2,1)S(1)}, u32[]{:S(2)}, u32[]{:S(2)}) collective-permute-start(bf16[2,688,512]{2,1,0:T(8,128)(2,1)} %diagonal_grad.5), channel_id=1, source_target_pairs={{0,32},{1,25},{8,40},{9,1},{16,48},{17,9},{24,56},{25,17},{32,64},... | collective-permute-start | bytes 4227080 | tf_op jit(solution)/shard_map/ppermute | solution.py:236
  66.2 19.1 %collective-permute-start.13 = (bf16[2,688,512]{2,1,0:T(8,128)(2,1)}, bf16[2,688,512]{2,1,0:T(8,128)(2,1)S(1)}, u32[]{:S(2)}, u32[]{:S(2)}) collective-permute-start(bf16[2,688,512]{2,1,0:T(8,128)(2,1)} %diagonal_grad.6), channel_id=1, source_target_pairs={{0,96},{1,9},{8,104},{9,17},{16,112},{17,25},{24,120},{25,1},{32,0... | collective-permute-start | bytes 4227080 | tf_op jit(solution)/shard_map/ppermute | solution.py:236
  85.3 1.4 copy-start
  87.9 2.3 %collective-permute-start.14 = (bf16[2,688,256]{2,1,0:T(8,128)(2,1)S(1)}, bf16[2,688,256]{2,1,0:T(8,128)(2,1)S(1)}, u32[]{:S(2)}, u32[]{:S(2)}) collective-permute-start(bf16[2,688,256]{2,1,0:T(8,128)(2,1)S(1)} %get-tuple-element.44), channel_id=1, source_target_pairs={{0,1},{1,0},{2,3},{3,2},{4,5},{5,4},{6,7},{7,6},{8,9},{9,8},{10,11... | collective-permute-start | bytes 2113544 | tf_op jit(solution)/shard_map/ppermute | solution.py:252
  90.2 18.1 %copy-start.5 = (bf16[512,512]{1,0:T(8,128)(2,1)S(1)}, bf16[512,512]{1,0:T(8,128)(2,1)}, u32[]{:S(2)}) copy-start(bf16[512,512]{1,0:T(8,128)(2,1)} %param.8) | copy-start | bytes 1572868
  92.0 34.6 %all-to-all-start = ((bf16[16,172,256]{2,1,0:T(8,128)(2,1)}), bf16[16,172,256]{2,1,0:T(8,128)(2,1)S(1)}, u32[]{:S(2)}, u32[]{:S(2)}) async-start(bf16[16,172,256]{2,1,0:T(8,128)(2,1)} %in_quarters.1), calls=%async_computation | async-start | bytes 2883584 | tf_op jit(solution)/shard_map/all_to_all | solution.py:313
  102.4 11.9 %copy-start.4 = (bf16[512,512]{1,0:T(8,128)(2,1)S(1)}, bf16[512,512]{1,0:T(8,128)(2,1)}, u32[]{:S(2)}) copy-start(bf16[512,512]{1,0:T(8,128)(2,1)} %copy-done.3) | copy-start | bytes 1572868
  104.3 2.0 %collective-permute-start.3 = (f32[2,86,256]{2,1,0:T(8,128)}, f32[2,86,256]{2,1,0:T(8,128)}, u32[]{:S(2)}, u32[]{:S(2)}) collective-permute-start(f32[2,86,256]{2,1,0:T(8,128)} %get-tuple-element.67), channel_id=1, source_target_pairs={{0,1},{1,0},{2,3},{3,2},{4,5},{5,4},{6,7},{7,6},{8,9},{9,8},{10,11... | collective-permute-start | bytes 528392 | tf_op jit(solution)/shard_map/ppermute | solution.py:252
  104.9 6.9 %copy-start.8 = (bf16[512,512]{1,0:T(8,128)(2,1)S(1)}, bf16[512,512]{1,0:T(8,128)(2,1)}, u32[]{:S(2)}) copy-start(bf16[512,512]{1,0:T(8,128)(2,1)} %copy-done.7) | copy-start | bytes 1572868
  104.9 8.6 %copy-start.10 = (bf16[512,512]{1,0:T(8,128)(2,1)S(1)}, bf16[512,512]{1,0:T(8,128)(2,1)}, u32[]{:S(2)}) copy-start(bf16[512,512]{1,0:T(8,128)(2,1)} %copy-done.9) | copy-start | bytes 1572868
  111.0 15.8 %copy-start.11 = (f32[2,172,256]{2,1,0:T(8,128)S(1)}, f32[2,172,256]{2,1,0:T(8,128)}, u32[]{:S(2)}) copy-start(f32[2,172,256]{2,1,0:T(8,128)} %maximum_select_fusion) | copy-start | bytes 1056772
  143.1 8.2 %collective-permute-start.15 = (f32[2,86,256]{2,1,0:T(8,128)S(1)}, f32[2,86,256]{2,1,0:T(8,128)S(1)}, u32[]{:S(2)}, u32[]{:S(2)}) collective-permute-start(f32[2,86,256]{2,1,0:T(8,128)S(1)} %get-tuple-element.65), channel_id=1, source_target_pairs={{0,1},{1,0},{2,3},{3,2},{4,5},{5,4},{6,7},{7,6},{8,9},{9,8},{10,11... | collective-permute-start | bytes 528392 | tf_op jit(solution)/shard_map/ppermute | solution.py:252
Sparse Core Ops, SparseCore 0:
  36.4 41.4 all-gather.3

commit v3 on v2

--- a/solution.py
+++ b/solution.py
@@ -18,7 +18,7 @@
 
 SIDE = 4
 SWAP = ((0, 1), (1, 0))
-CORE, FIRST, PLACE = 0, 1, 9
+CORE, FIRST, PLACE, FIRST_OUT, STRIDE, SECOND_OUT, QUARTER = 0, 1, 9, 17, 21, 22, 26
 DISTANCES = (2, 3, 1, 0)
 
 
@@ -139,9 +139,9 @@
     return in_vmem(halves_kernel, "sum_halves", [out, out], *parts, table=table)
 
 
-def quarters_kernel(at_ref, *refs):
-    sides, out = refs[:2], refs[2]
-    rows = out.shape[1]
+def first_kernel(at_ref, *refs):
+    sides, outs, held = refs[:2], refs[2:6], refs[6]
+    rows = held.shape[1]
     for which in range(2):
 
         @pl.when(at_ref[CORE] == which)
@@ -149,82 +149,137 @@
             for k in range(SIDE):
                 block = sides[(k // 2 + which) % 2][k % 2]
                 for i in range(SIDE):
-                    out[SIDE * k + i] = block[i * rows : (i + 1) * rows]
-
-
-def in_quarters(table, mine, other):
-    blocks, block, half = mine.shape
+                    held[SIDE * k + i] = block[i * rows : (i + 1) * rows]
+
+    for t, out in enumerate(outs):
+        for q in range(SIDE):
+            out[q] = held[at_ref[FIRST_OUT + t] + q * at_ref[STRIDE]]
+
+
+def first_parts(table, mine, other):
+    _, block, half = mine.shape
+    rows = block // SIDE
     return in_vmem(
-        quarters_kernel, "in_quarters",
-        jax.ShapeDtypeStruct((2 * blocks * SIDE, block // SIDE, half), jnp.bfloat16),
-        mine, other, table=table,
-    )
+        first_kernel, "first_parts",
+        [jax.ShapeDtypeStruct((SIDE, rows, half), jnp.bfloat16)] * SIDE, mine, other,
+        scratch=[pltpu.VMEM((SIDE**2, rows, half), jnp.bfloat16)], table=table,
+    )
+
+
+def second_kernel(at_ref, *refs):
+    parts, outs = refs[:4], refs[4:]
+    for t, out in enumerate(outs):
+        out[...] = total_of(parts, at_ref[SECOND_OUT + t]).astype(out.dtype)
+
+
+def second_parts(table, parts):
+    shape = parts[0].shape[1:]
+    return in_vmem(
+        second_kernel, "second_parts",
+        [jax.ShapeDtypeStruct(shape, jnp.float32)]
+        + [jax.ShapeDtypeStruct(shape, jnp.bfloat16)] * (SIDE - 1),
+        *parts, table=table,
+    )
+
+
+def cross(array, distance, diagonal_core):
+    pairs = []
+    for i in range(SIDE):
+        for j in range(SIDE):
+            for k in range(SIDE):
+                for core in range(2):
+                    to = [i, j, k]
+                    for axis in (0, 1) if core == diagonal_core else (2,):
+                        to[axis] = (to[axis] + distance) % SIDE
+                    flat = [((p * SIDE + q) * SIDE + r) * 2 + core for p, q, r in ((i, j, k), to)]
+                    pairs.append(tuple(flat))
+    return lax.ppermute(array, ("y", "z", "x", "core"), pairs)
+
+
+def stage_kernel(weight_ref, projector_ref, weight_out, projector_out, sems):
+    copies = [
+        pltpu.make_async_copy(weight_ref, weight_out, sems.at[0]),
+        pltpu.make_async_copy(projector_ref, projector_out, sems.at[1]),
+    ]
+    for copy in copies:
+        copy.start()
+    for copy in copies:
+        copy.wait()
+
+
+def stage(weight, projector):
+    return pl.pallas_call(
+        stage_kernel,
+        in_specs=[ANY] * 2,
+        out_specs=[VMEM] * 2,
+        out_shape=[
+            jax.ShapeDtypeStruct(weight.shape, weight.dtype),
+            jax.ShapeDtypeStruct(projector.shape, projector.dtype),
+        ],
+        scratch_shapes=[pltpu.SemaphoreType.DMA((2,))],
+        compiler_params=pltpu.CompilerParams(vmem_limit_bytes=16 << 20),
+        name="stage",
+    )(weight, projector)
 
 
 def update_kernel(
-    at_ref, direction_ref, projector_ref, weight_ref, out_ref,
-    direction, projectors, weights, outs, sems,
+    at_ref, own_ref, own_far_ref, other_ref, other_far_ref, projector_ref, weight_ref, out_ref,
+    quarters, direction,
 ):
-    parts, depth = projectors.shape[:2]
-    contract = (((1,), (1,)), ((), ()))
-    places = [
-        pl.ds(pl.multiple_of(at_ref[PLACE + i] * depth, depth), depth) for i in range(parts)
-    ]
-    loads, stores = [], []
-    for i, place in enumerate(places):
-        loads.append(
-            [
-                pltpu.make_async_copy(
-                    projector_ref.at[pl.ds(i * depth, depth)], projectors.at[i], sems.at[0, i]
-                ),
-                pltpu.make_async_copy(weight_ref.at[:, place], weights.at[i], sems.at[1, i]),
-            ]
-        )
-        for copy in loads[-1]:
-            copy.start()
-    pieces, rows, columns = direction_ref.shape
-    for i in range(pieces):
-        direction[
-            i // 2 * rows : (i // 2 + 1) * rows, i % 2 * columns : (i % 2 + 1) * columns
-        ] = direction_ref[i]
-    for i, place in enumerate(places):
-        for copy in loads[i]:
-            copy.wait()
-        delta = lax.dot_general(
-            direction[...], projectors[i], contract, preferred_element_type=jnp.float32
-        )
-        outs[i] = (weights[i].astype(jnp.float32) - step_size * delta).astype(outs.dtype)
-        stores.append(pltpu.make_async_copy(outs.at[i], out_ref.at[:, place], sems.at[2, i]))
-        stores[-1].start()
-    for copy in stores:
-        copy.wait()
-
-
-def update(table, direction, projector, weight):
+    i = pl.program_id(0)
+    rows, half = own_ref.shape
+    depth = out_ref.shape[1]
+
+    @pl.when(i == 0)
+    def _():
+        for which in range(2):
+
+            @pl.when(at_ref[CORE] == which)
+            def _():
+                for near, far, place in (
+                    (own_ref, own_far_ref, which), (other_ref, other_far_ref, 1 - which)
+                ):
+                    columns = pl.ds(place * half, half)
+                    quarters[at_ref[QUARTER], :, columns] = near[...]
+                    for t in range(1, SIDE):
+                        quarters[at_ref[QUARTER + t], :, columns] = far[t - 1]
+
+        for q in range(SIDE):
+            direction[q * rows : (q + 1) * rows] = quarters[q]
+
+    place = pl.ds(pl.multiple_of(at_ref[PLACE + i] * depth, depth), depth)
+    delta = lax.dot_general(
+        direction[...],
+        projector_ref[pl.ds(pl.multiple_of(i * depth, depth), depth)],
+        (((1,), (1,)), ((), ())),
+        preferred_element_type=jnp.float32,
+    )
+    out_ref[...] = (weight_ref[:, place].astype(jnp.float32) - step_size * delta).astype(
+        out_ref.dtype
+    )
+
+
+def update(table, own, own_far, other, other_far, projector, weight):
     block, width = weight.shape
     rank = projector.shape[1]
+    rows = own.shape[0]
     parts = 8
-    depth = width // parts
     return pl.pallas_call(
         update_kernel,
-        in_specs=[SMEM, VMEM, ANY, ANY],
-        out_specs=ANY,
+        grid_spec=pltpu.PrefetchScalarGridSpec(
+            num_scalar_prefetch=1,
+            grid=(parts,),
+            in_specs=[VMEM] * 6,
+            out_specs=pl.BlockSpec((block, width // parts), lambda i, at: (0, at[PLACE + i])),
+            scratch_shapes=[
+                pltpu.VMEM((SIDE, rows, rank), own.dtype),
+                pltpu.VMEM((block, rank), own.dtype),
+            ],
+        ),
         out_shape=jax.ShapeDtypeStruct(weight.shape, weight.dtype),
-        scratch_shapes=[
-            pltpu.VMEM((block, rank), direction.dtype),
-            pltpu.VMEM((parts, depth, rank), projector.dtype),
-            pltpu.VMEM((parts, block, depth), weight.dtype),
-            pltpu.VMEM((parts, block, depth), weight.dtype),
-            pltpu.SemaphoreType.DMA((3, parts)),
-        ],
-        cost_estimate=pl.CostEstimate(
-            flops=2 * block * width * rank,
-            bytes_accessed=4 * block * width + 2 * width * rank,
-            transcendentals=0,
-        ),
-        compiler_params=pltpu.CompilerParams(vmem_limit_bytes=58 << 20),
+        compiler_params=pltpu.CompilerParams(vmem_limit_bytes=20 << 20),
         name="update",
-    )(table, direction, projector, weight)
+    )(table, own, own_far, other, other_far, projector, weight)
 
 
 def exchange(array, distance):
@@ -259,7 +314,11 @@
     places = [
         2 * lax.rem(x + r, SIDE) + which for r in (0, 1, 3, 2) for which in (core, 1 - core)
     ]
-    table = jnp.stack([core, *firsts, *places]).astype(jnp.int32)
+    block_at = [lax.rem(y + t, SIDE) for t in range(SIDE)]
+    quarter_at = [lax.rem(x + t, SIDE) for t in range(SIDE)]
+    first_out = [jnp.where(core == 0, SIDE * p, q) for p, q in zip(block_at, quarter_at, strict=True)]
+    second_out = [jnp.where(core == 0, q, p) for p, q in zip(block_at, quarter_at, strict=True)]
+    table = jnp.stack([core, *firsts, *places, *first_out, 1 + 3 * core, *second_out, *quarter_at]).astype(jnp.int32)
     table, projector, out_grad = lax.optimization_barrier((table, projector, out_grad))
 
     def product(place, part):
@@ -309,19 +368,15 @@
     parts = [*here, *near, *far]
     sums[3], parts = lax.optimization_barrier((sums[3], parts))
     projector_all = jnp.concatenate(parts, axis=0)
+    sums[0], projector_all, weight_all, moments = lax.optimization_barrier(
+        (sums[0], projector_all, weight_all, moments)
+    )
     mine, other = sum_halves(table, sums)
-    quarters = lax.all_to_all(
-        in_quarters(table, mine, swap(other)), ("y", "z", "x"), 0, 0, tiled=True,
-        axis_index_groups=[
-            [
-                (i * SIDE + (i + diagonal) % SIDE) * SIDE + j
-                for i in range(SIDE)
-                for j in range(SIDE)
-            ]
-            for diagonal in range(SIDE)
-        ],
-    )
-    grad = jnp.sum(quarters.astype(jnp.float32), axis=0)
+    sums = first_parts(table, mine, swap(other))
+    sums = [sums[0], *(cross(sums[t], t, 0) for t in (2, 1, 3))]
+    sums = second_parts(table, sums)
+    sums = [sums[0], *(cross(sums[t], t, 1) for t in (2, 1, 3))]
+    grad = sum(part.astype(jnp.float32) for part in sums)
     grad = grad * scale
 
     new_first = beta_first * moments[0] + (1.0 - beta_first) * grad
@@ -330,12 +385,17 @@
         new_first / correct_first / (jnp.sqrt(new_second / correct_second) + epsilon)
     ).astype(jnp.bfloat16)
 
-    direction, projector_all = lax.optimization_barrier((direction, projector_all))
-    direction = lax.all_gather(direction, ("x", "core"), axis=0)
-    new_first, new_second, direction = lax.optimization_barrier(
-        (new_first, new_second, direction)
-    )
-    new_weight = update(table, direction, projector_all, weight_all.T).T
+    direction, projector_all, weight_all = lax.optimization_barrier(
+        (direction, projector_all, weight_all)
+    )
+    weight_all, projector_all = stage(weight_all.T, projector_all)
+    far = [hop(direction, "x", -t) for t in (2, 1, 3)]
+    other = swap(direction)
+    far, weight_all, projector_all = lax.optimization_barrier((far, weight_all, projector_all))
+    far = jnp.stack([far[1], far[0], far[2]])
+    other_far = swap(far)
+    new_weight = update(table, direction, far, other, other_far, projector_all, weight_all).T
+    new_first, new_second, _ = lax.optimization_barrier((new_first, new_second, far))
 
     news = jnp.stack([new_first, new_second])
     kept = lax.dynamic_slice_in_dim(news, core * rows, rows, 1)

time: 159 us -> 143 us (0.90)
  blocking collectives: 16.1 us -> 0 us
  starting transfers between devices: 27.7 us -> 35.2 us
  waiting for transfers between devices: 40.5 us -> 35.4 us
  other arithmetic: 4.26 us -> 1.11 us
  local copies, waits for them, and re-layouts: 11.3 us -> 9.08 us
    all_gather x1 -> x0, blocking collectives: 16.1 us -> none  [on_device(): direction = lax.all_gather(direction, ('x', 'core'), axis=0)]
    ppermute x0 -> x6, starting transfers between devices: none -> 13.6 us  [cross(): return lax.ppermute(array, ('y', 'z', 'x', 'core'), pairs)]
    ppermute x0 -> x6, waiting for transfers between devices: none -> 10.7 us  [cross(): return lax.ppermute(array, ('y', 'z', 'x', 'core'), pairs)]
    all_to_all x1 -> x0, starting transfers between devices: 10.4 us -> none  [on_device(): lax.all_to_all(in_quarters(table, mine, swap(other)), ('y', 'z', 'x'), 0,...]
    all_to_all x1 -> x0, waiting for transfers between devices: 9.53 us -> none  [on_device(): lax.all_to_all(in_quarters(table, mine, swap(other)), ('y', 'z', 'x'), 0,...]
    ppermute x3, waiting for transfers between devices: 11.8 us -> 7.49 us  [exchange(): return lax.ppermute(array, ('y', 'z', 'core'), pairs)]
    ppermute x4 -> x7, waiting for transfers between devices: 11.2 us -> 7.25 us  [hop(): lax.ppermute(array, axis, [(i, (i + distance) % SIDE) for i in range(SIDE)])]
    ppermute x4 -> x7, starting transfers between devices: 5.3 us -> 8.08 us  [hop(): lax.ppermute(array, axis, [(i, (i + distance) % SIDE) for i in range(SIDE)])]
  transfers between devices with their start and end apart: 18 -> 28, of which waited for: 10 -> 11; matrix products, arithmetic and copies ran while one was open for 14% -> 9% of each run, Pallas kernels for 22% -> 18%
where the time goes in v3:
time: 143 us
  Pallas kernels  36.6 us (26%)
  waiting for transfers between devices  35.4 us (25%)
  starting transfers between devices  35.2 us (25%)
  between operations  14.5 us (10%)
  matrix products  10.6 us (7%)
  local copies, waits for them, and re-layouts  9.08 us (6%)
    pallas_call x4, Pallas kernels, diagonal_grad(): pl.pallas_call(functools.partial(diagonal_kernel, numbers), in_specs=[SME...  24.9 us
    ppermute x6, starting transfers between devices, cross(): return lax.ppermute(array, ('y', 'z', 'x', 'core'), pairs)  13.6 us
    ppermute x6, waiting for transfers between devices, cross(): return lax.ppermute(array, ('y', 'z', 'x', 'core'), pairs)  10.7 us
    dot_general x8, matrix products, product(): jnp.dot(lax.dynamic_slice_in_dim(activations, places[place] * depth, dept...  10.6 us
    ppermute x11, waiting for transfers between devices, swap(): return lax.ppermute(array, 'core', SWAP)  9.98 us
    unnamed x50, local copies, waits for them, and re-layouts  8.13 us
    ppermute x7, starting transfers between devices, hop(): lax.ppermute(array, axis, [(i, (i + distance) % SIDE) for i in range(SIDE)])  8.08 us
    ppermute x11, starting transfers between devices, swap(): return lax.ppermute(array, 'core', SWAP)  7.84 us
  transfers between devices with their start and end apart: 28, of which 11 were waited for; matrix products, arithmetic and copies ran while one was open for 9% of the time, Pallas kernels for 18%

profile of v3, /device:TPU:1, one launch (start us, length us, event | category | flops | bytes accessed | tf_op | source)
XLA Modules:
  0.0 142.6 jit_solution(6160408728584491213)
XLA Ops:
  11.6 1.9 %fusion.17 = f32[640,512]{1,0:T(8,128)S(1)} fusion(bf16[512,512]{1,0:T(8,128)(2,1)} %param.8, bf16[640,4096]{1,0:T(8,128)(2,1)} %param.6, s32[]{:T(128)S(6)} %select_n.85), kind=kOutput, calls=%fused_computation.16 | convolution fusion | flops 335544320 | bytes 2490372 | tf_op jit(solution)/shard_map/dot_general | solution.py:325
  13.5 2.7 %collective-permute-done.3 = bf16[512,512]{1,0:T(8,128)(2,1)S(1)} collective-permute-done((bf16[512,512]{1,0:T(8,128)(2,1)}, bf16[512,512]{1,0:T(8,128)(2,1)S(1)}, u32[]{:S(2)}, u32[]{:S(2)}) %collective-permute-start.3) | collective-permute-done | bytes 524320 | tf_op jit(solution)/shard_map/ppermute | solution.py:307
  16.3 1.8 %convolution_add_fusion = f32[640,512]{1,0:T(8,128)S(1)} fusion(f32[640,512]{1,0:T(8,128)S(1)} %fusion.17, bf16[512,512]{1,0:T(8,128)(2,1)S(1)} %collective-permute-done.3, bf16[640,4096]{1,0:T(8,128)(2,1)} %param.6, s32[]{:T(128)S(6)} %select_n.86), kind=kOutput, calls=%fused_computation | convolution fusion | flops 335872000 | bytes 3801092 | tf_op jit(solution)/shard_map/dot_general | solution.py:325
  18.0 5.4 %collective-permute-done.2 = bf16[512,512]{1,0:T(8,128)(2,1)S(1)} collective-permute-done((bf16[512,512]{1,0:T(8,128)(2,1)}, bf16[512,512]{1,0:T(8,128)(2,1)S(1)}, u32[]{:S(2)}, u32[]{:S(2)}) %collective-permute-start.2) | collective-permute-done | bytes 524320 | tf_op jit(solution)/shard_map/ppermute | solution.py:26
  25.0 2.7 %collective-permute-start.5 = (bf16[256,512]{1,0:T(8,128)(2,1)S(1)}, bf16[256,512]{1,0:T(8,128)(2,1)S(1)}, u32[]{:S(2)}, u32[]{:S(2)}) collective-permute-start(bf16[256,512]{1,0:T(8,128)(2,1)S(1)} %slice.19), channel_id=1, source_target_pairs={{0,6},{2,0},{4,2},{6,4},{1,7},{3,1},{5,3},{7,5},{8,14},{10,8},{12,... | collective-permute-start | bytes 786440 | tf_op jit(solution)/shard_map/ppermute | solution.py:26
  28.7 3.3 %collective-permute-done.6 = bf16[512,512]{1,0:T(8,128)(2,1)S(1)} collective-permute-done((bf16[512,512]{1,0:T(8,128)(2,1)S(1)}, bf16[512,512]{1,0:T(8,128)(2,1)S(1)}, u32[]{:S(2)}, u32[]{:S(2)}) %collective-permute-start.6) | collective-permute-done | bytes 524320 | tf_op jit(solution)/shard_map/ppermute | solution.py:307
  32.6 1.6 %add_add_fusion = f32[640,512]{1,0:T(8,128)} fusion(f32[640,512]{1,0:T(8,128)S(1)} %fusion.10, f32[640,512]{1,0:T(8,128)S(1)} %fusion.12, f32[640,512]{1,0:T(8,128)S(1)} %convolution_add_fusion, f32[640,512]{1,0:T(8,128)S(1)} %fusion.14, bf16[512,512]{1,0:T(8,128)(2,1)S(1)} %collective-permute-done.7, bf16[640,4096]{1,0:T(8,128)(2,1)S(1)} %copy-done.4, ...), kind=kOutput, calls=%fused_computation.2 | convolution fusion | flops 336855040 | bytes 7733252 | tf_op jit(solution)/shard_map/dot_general | solution.py:325
  34.2 1.8 %collective-permute-done.4 = bf16[256,512]{1,0:T(8,128)(2,1)S(1)} collective-permute-done((bf16[256,512]{1,0:T(8,128)(2,1)S(1)}, bf16[256,512]{1,0:T(8,128)(2,1)S(1)}, u32[]{:S(2)}, u32[]{:S(2)}) %collective-permute-start.4) | collective-permute-done | bytes 262176 | tf_op jit(solution)/shard_map/ppermute | solution.py:26
  36.2 1.7 %collective-permute-start.8 = (bf16[512,512]{1,0:T(8,128)(2,1)S(1)}, bf16[512,512]{1,0:T(8,128)(2,1)S(1)}, u32[]{:S(2)}, u32[]{:S(2)}) collective-permute-start(bf16[512,512]{1,0:T(8,128)(2,1)S(1)} %constant_dynamic-update-slice_fusion), channel_id=1, source_target_pairs={{0,1},{1,0},{2,3},{3,2},{4,5},{5,4},{6,7},{7,6},{8,9},{9,8},{10,11... | collective-permute-start | bytes 1572872 | tf_op jit(solution)/shard_map/ppermute | solution.py:307
  37.8 1.6 %fusion.4 = f32[640,512]{1,0:T(8,128)S(1)} fusion(bf16[512,512]{1,0:T(8,128)(2,1)S(1)} %constant_dynamic-update-slice_fusion, bf16[640,4096]{1,0:T(8,128)(2,1)} %param.6, s32[]{:T(128)S(6)} %select_n.91), kind=kOutput, calls=%fused_computation.5 | convolution fusion | flops 335544320 | bytes 2490372 | tf_op jit(solution)/shard_map/dot_general | solution.py:325
  39.4 2.2 %add_convert_fusion.reduced_ref = bf16[640,512]{1,0:T(8,128)(2,1)S(1)} fusion(f32[640,512]{1,0:T(8,128)} %add_add_fusion, f32[640,512]{1,0:T(8,128)S(1)} %fusion.4, bf16[512,512]{1,0:T(8,128)(2,1)S(1)} %collective-permute-done.8, bf16[640,4096]{1,0:T(8,128)(2,1)} %param.6, s32[]{:T(128)S(6)} %select_n.92), kind=kOutput, calls=%fused_computation.1 | convolution fusion | flops 336527360 | bytes 4456452 | tf_op jit(solution)/shard_map/dot_general | solution.py:325
  43.8 6.2 %diagonal_grad.4 = bf16[2,688,512]{2,1,0:T(8,128)(2,1)} custom-call(s32[30]{0:T(128)S(1)} %stack.153.at_ref, bf16[640,11008]{1,0:T(8,128)(2,1)} %mine_ref.3, bf16[640,11008]{1,0:T(8,128)(2,1)} %collective-permute-done.other_ref, bf16[640,512]{1,0:T(8,128)(2,1)S(1)} %add_convert_fusion.reduced_ref, bf16[640,512]{1,0:T(8,128)(2,1)S(1)} %collective-permute-done.9.reduced_other_ref), custom_call_target="tpu_custom_call" | custom-call | flops 2348810240 | bytes 4587520 | tf_op jit(solution)/shard_map/diagonal_grad/pallas_call | solution.py:95
  50.0 3.9 %collective-permute-start.10 = (bf16[2,688,512]{2,1,0:T(8,128)(2,1)}, bf16[2,688,512]{2,1,0:T(8,128)(2,1)S(1)}, u32[]{:S(2)}, u32[]{:S(2)}) collective-permute-start(bf16[2,688,512]{2,1,0:T(8,128)(2,1)} %diagonal_grad.4), channel_id=1, source_target_pairs={{0,64},{1,17},{8,72},{9,25},{16,80},{17,1},{24,88},{25,9},{32,96},... | collective-permute-start | bytes 4227080 | tf_op jit(solution)/shard_map/ppermute | solution.py:291
  53.9 6.3 %diagonal_grad.6 = bf16[2,688,512]{2,1,0:T(8,128)(2,1)} custom-call(s32[30]{0:T(128)S(1)} %stack.153.at_ref, bf16[640,11008]{1,0:T(8,128)(2,1)} %mine_ref.3, bf16[640,11008]{1,0:T(8,128)(2,1)} %collective-permute-done.other_ref, bf16[640,512]{1,0:T(8,128)(2,1)S(1)} %add_convert_fusion.reduced_ref, bf16[640,512]{1,0:T(8,128)(2,1)S(1)} %collective-permute-done.9.reduced_other_ref), custom_call_target="tpu_custom_call" | custom-call | flops 2348810240 | bytes 4587520 | tf_op jit(solution)/shard_map/diagonal_grad/pallas_call | solution.py:95
  60.8 6.2 %diagonal_grad.7 = bf16[2,688,512]{2,1,0:T(8,128)(2,1)} custom-call(s32[30]{0:T(128)S(1)} %stack.153.at_ref, bf16[640,11008]{1,0:T(8,128)(2,1)} %mine_ref.3, bf16[640,11008]{1,0:T(8,128)(2,1)} %collective-permute-done.other_ref, bf16[640,512]{1,0:T(8,128)(2,1)S(1)} %add_convert_fusion.reduced_ref, bf16[640,512]{1,0:T(8,128)(2,1)S(1)} %collective-permute-done.9.reduced_other_ref), custom_call_target="tpu_custom_call" | custom-call | flops 2348810240 | bytes 4587520 | tf_op jit(solution)/shard_map/diagonal_grad/pallas_call | solution.py:95
  69.0 6.3 %diagonal_grad.5.refs_3_ = bf16[2,688,512]{2,1,0:T(8,128)(2,1)} custom-call(s32[30]{0:T(128)S(1)} %stack.153.at_ref, bf16[640,11008]{1,0:T(8,128)(2,1)} %mine_ref.3, bf16[640,11008]{1,0:T(8,128)(2,1)} %collective-permute-done.other_ref, bf16[640,512]{1,0:T(8,128)(2,1)S(1)} %add_convert_fusion.reduced_ref, ...), custom_call_target="tpu_custom_call" | custom-call | flops 2348810240 | bytes 4587520 | tf_op jit(solution)/shard_map/diagonal_grad/pallas_call | solution.py:95
  76.7 2.0 %copy-done.2 = bf16[4096,512]{1,0:T(8,128)(2,1)} copy-done((bf16[4096,512]{1,0:T(8,128)(2,1)}, bf16[4096,512]{1,0:T(8,128)(2,1)S(1)}, u32[]{:S(2)}) %copy-start.2) | copy-done | bytes 4194328
  78.7 7.5 %collective-permute-done.12.refs_1_ = bf16[2,688,512]{2,1,0:T(8,128)(2,1)} collective-permute-done((bf16[2,688,512]{2,1,0:T(8,128)(2,1)}, bf16[2,688,512]{2,1,0:T(8,128)(2,1)}, u32[]{:S(2)}, u32[]{:S(2)}) %collective-permute-start.12) | collective-permute-done | bytes 1409056 | tf_op jit(solution)/shard_map/ppermute | solution.py:291
  86.2 2.5 %sum_halves.1 = (bf16[2,688,256]{2,1,0:T(8,128)(2,1)S(1)}, bf16[2,688,256]{2,1,0:T(8,128)(2,1)S(1)}) custom-call(s32[30]{0:T(128)S(1)} %stack.153.at_ref, bf16[2,688,512]{2,1,0:T(8,128)(2,1)S(1)} %collective-permute-done.10.refs_0_, bf16[2,688,512]{2,1,0:T(8,128)(2,1)} %collective-permute-done.12.refs_1_, ...), custom_call_target="tpu_custom_call" | custom-call | tf_op jit(solution)/shard_map/sum_halves/pallas_call | solution.py:36
  89.0 1.9 %collective-permute-done.14.refs_1_ = bf16[2,688,256]{2,1,0:T(8,128)(2,1)S(1)} collective-permute-done((bf16[2,688,256]{2,1,0:T(8,128)(2,1)S(1)}, bf16[2,688,256]{2,1,0:T(8,128)(2,1)S(1)}, u32[]{:S(2)}, u32[]{:S(2)}) %collective-permute-start.14) | collective-permute-done | bytes 704544 | tf_op jit(solution)/shard_map/ppermute | solution.py:307
  92.3 2.3 %collective-permute-start.17 = (bf16[4,172,256]{2,1,0:T(8,128)(2,1)S(1)}, bf16[4,172,256]{2,1,0:T(8,128)(2,1)S(1)}, u32[]{:S(2)}, u32[]{:S(2)}) collective-permute-start(bf16[4,172,256]{2,1,0:T(8,128)(2,1)S(1)} %get-tuple-element.78), channel_id=1, source_target_pairs={{0,120},{1,7},{2,122},{3,1},{4,124},{5,3},{6,126},{7,5},{8,96},{9,... | collective-permute-start | bytes 1056776 | tf_op jit(solution)/shard_map/ppermute | solution.py:196
  94.5 5.4 %collective-permute-done.15.refs_1_ = bf16[4,172,256]{2,1,0:T(8,128)(2,1)S(1)} collective-permute-done((bf16[4,172,256]{2,1,0:T(8,128)(2,1)S(1)}, bf16[4,172,256]{2,1,0:T(8,128)(2,1)S(1)}, u32[]{:S(2)}, u32[]{:S(2)}) %collective-permute-start.15) | collective-permute-done | bytes 352288 | tf_op jit(solution)/shard_map/ppermute | solution.py:196
  99.9 3.4 %collective-permute-done.16.refs_2_ = bf16[4,172,256]{2,1,0:T(8,128)(2,1)S(1)} collective-permute-done((bf16[4,172,256]{2,1,0:T(8,128)(2,1)S(1)}, bf16[4,172,256]{2,1,0:T(8,128)(2,1)S(1)}, u32[]{:S(2)}, u32[]{:S(2)}) %collective-permute-start.16) | collective-permute-done | bytes 352288 | tf_op jit(solution)/shard_map/ppermute | solution.py:196
  104.0 6.0 %collective-permute-start.18 = (bf16[172,256]{1,0:T(8,128)(2,1)S(1)}, bf16[172,256]{1,0:T(8,128)(2,1)S(1)}, u32[]{:S(2)}, u32[]{:S(2)}) collective-permute-start(bf16[172,256]{1,0:T(8,128)(2,1)S(1)} %get-tuple-element.80), channel_id=1, source_target_pairs={{0,4},{1,81},{2,6},{3,83},{4,0},{5,85},{6,2},{7,87},{8,12},{9,89},... | collective-permute-start | bytes 264200 | tf_op jit(solution)/shard_map/ppermute | solution.py:196
  110.0 1.9 %collective-permute-start.19 = (bf16[172,256]{1,0:T(8,128)(2,1)S(1)}, bf16[172,256]{1,0:T(8,128)(2,1)S(1)}, u32[]{:S(2)}, u32[]{:S(2)}) collective-permute-start(bf16[172,256]{1,0:T(8,128)(2,1)S(1)} %get-tuple-element.81), channel_id=1, source_target_pairs={{0,2},{1,41},{2,4},{3,43},{4,6},{5,45},{6,0},{7,47},{8,10},{9,49},... | collective-permute-start | bytes 264200 | tf_op jit(solution)/shard_map/ppermute | solution.py:196
  111.9 2.9 %collective-permute-start.20 = (bf16[172,256]{1,0:T(8,128)(2,1)S(1)}, bf16[172,256]{1,0:T(8,128)(2,1)S(1)}, u32[]{:S(2)}, u32[]{:S(2)}) collective-permute-start(bf16[172,256]{1,0:T(8,128)(2,1)S(1)} %get-tuple-element.82), channel_id=1, source_target_pairs={{0,6},{1,121},{2,0},{3,123},{4,2},{5,125},{6,4},{7,127},{8,14},{9,... | collective-permute-start | bytes 264200 | tf_op jit(solution)/shard_map/ppermute | solution.py:196
  114.8 1.9 %collective-permute-done.19 = bf16[172,256]{1,0:T(8,128)(2,1)S(1)} collective-permute-done((bf16[172,256]{1,0:T(8,128)(2,1)S(1)}, bf16[172,256]{1,0:T(8,128)(2,1)S(1)}, u32[]{:S(2)}, u32[]{:S(2)}) %collective-permute-start.19) | collective-permute-done | bytes 88096 | tf_op jit(solution)/shard_map/ppermute | solution.py:196
  117.0 2.7 %collective-permute-start.22 = (bf16[172,256]{1,0:T(8,128)(2,1)S(1)}, bf16[172,256]{1,0:T(8,128)(2,1)S(1)}, u32[]{:S(2)}, u32[]{:S(2)}) collective-permute-start(bf16[172,256]{1,0:T(8,128)(2,1)S(1)} %get-tuple-element.85.own_ref), channel_id=1, source_target_pairs={{0,6},{2,0},{4,2},{6,4},{1,7},{3,1},{5,3},{7,5},{8,14},{10,8},{12,... | collective-permute-start | bytes 264200 | tf_op jit(solution)/shard_map/ppermute | solution.py:26
  119.7 2.6 %copy-done.1 = bf16[4096,688]{0,1:T(8,128)(2,1)S(1)} copy-done((bf16[4096,688]{0,1:T(8,128)(2,1)S(1)}, bf16[4096,688]{0,1:T(8,128)(2,1)}, u32[]{:S(2)}) %copy-start.1) | copy-done | bytes 5636120
  122.3 2.2 %copy-done.3 = bf16[4096,512]{1,0:T(8,128)(2,1)S(1)} copy-done((bf16[4096,512]{1,0:T(8,128)(2,1)S(1)}, bf16[4096,512]{1,0:T(8,128)(2,1)}, u32[]{:S(2)}) %copy-start.3) | copy-done | bytes 4194328
  125.4 1.6 %collective-permute-start.26 = (f32[2,86,256]{2,1,0:T(8,128)S(1)}, f32[2,86,256]{2,1,0:T(8,128)S(1)}, u32[]{:S(2)}, u32[]{:S(2)}) collective-permute-start(f32[2,86,256]{2,1,0:T(8,128)S(1)} %get-tuple-element.103), channel_id=1, source_target_pairs={{0,1},{1,0},{2,3},{3,2},{4,5},{5,4},{6,7},{7,6},{8,9},{9,8},{10,11... | collective-permute-start | bytes 528392 | tf_op jit(solution)/shard_map/ppermute | solution.py:307
  128.9 6.9 %update.1 = bf16[688,4096]{1,0:T(8,128)(2,1)} custom-call(s32[30]{0:T(128)S(1)} %stack.153.at_ref, bf16[172,256]{1,0:T(8,128)(2,1)S(1)} %get-tuple-element.85.own_ref, bf16[3,172,256]{2,1,0:T(8,128)(2,1)S(1)} %pad_maximum_fusion.own_far_ref, bf16[172,256]{1,0:T(8,128)(2,1)S(1)} %collective-permute-done.24.other_ref, ...), custom_call_target="tpu_custom_call" | custom-call | tf_op jit(solution)/shard_map/update/pallas_call | solution.py:267
  (104 shorter events, 19.1 us)
Async XLA Ops:
  7.2 71.5 %all-gather.2.cloned.1.call-start = ((), (), s32[]{:S(2)}) async-start(), calls=%async_computation | async-start | bytes 6340608 | tf_op jit(solution)/shard_map/all_gather | solution.py:362
  7.4 36.5 %collective-permute-start = (bf16[640,11008]{1,0:T(8,128)(2,1)}, bf16[640,11008]{1,0:T(8,128)(2,1)}, u32[]{:S(2)}, u32[]{:S(2)}) collective-permute-start(bf16[640,11008]{1,0:T(8,128)(2,1)} %mine_ref.3), channel_id=1, source_target_pairs={{0,1},{1,0},{2,3},{3,2},{4,5},{5,4},{6,7},{7,6},{8,9},{9,8},{10,11... | collective-permute-start | bytes 42270728 | tf_op jit(solution)/shard_map/ppermute | solution.py:307
  8.9 7.4 %collective-permute-start.3 = (bf16[512,512]{1,0:T(8,128)(2,1)}, bf16[512,512]{1,0:T(8,128)(2,1)S(1)}, u32[]{:S(2)}, u32[]{:S(2)}) collective-permute-start(bf16[512,512]{1,0:T(8,128)(2,1)} %param.8), channel_id=1, source_target_pairs={{0,1},{1,0},{2,3},{3,2},{4,5},{5,4},{6,7},{7,6},{8,9},{9,8},{10,11... | collective-permute-start | bytes 1572872 | tf_op jit(solution)/shard_map/ppermute | solution.py:307
  9.0 14.5 %collective-permute-start.2 = (bf16[512,512]{1,0:T(8,128)(2,1)}, bf16[512,512]{1,0:T(8,128)(2,1)S(1)}, u32[]{:S(2)}, u32[]{:S(2)}) collective-permute-start(bf16[512,512]{1,0:T(8,128)(2,1)} %param.8), channel_id=1, source_target_pairs={{0,2},{2,4},{4,6},{6,0},{1,3},{3,5},{5,7},{7,1},{8,10},{10,12},{12... | collective-permute-start | bytes 1572872 | tf_op jit(solution)/shard_map/ppermute | solution.py:26
  10.3 13.2 %collective-permute-start.1 = (bf16[512,512]{1,0:T(8,128)(2,1)}, bf16[512,512]{1,0:T(8,128)(2,1)S(1)}, u32[]{:S(2)}, u32[]{:S(2)}) collective-permute-start(bf16[512,512]{1,0:T(8,128)(2,1)} %param.8), channel_id=1, source_target_pairs={{0,6},{2,0},{4,2},{6,4},{1,7},{3,1},{5,3},{7,5},{8,14},{10,8},{12,... | collective-permute-start | bytes 1572872 | tf_op jit(solution)/shard_map/ppermute | solution.py:26
  11.6 16.1 %copy-start.4 = (bf16[640,4096]{1,0:T(8,128)(2,1)S(1)}, bf16[640,4096]{1,0:T(8,128)(2,1)}, u32[]{:S(2)}) copy-start(bf16[640,4096]{1,0:T(8,128)(2,1)} %param.6) | copy-start | bytes 15728644
  16.3 12.5 %copy-start.12 = (bf16[512,512]{1,0:T(8,128)(2,1)}, bf16[512,512]{1,0:T(8,128)(2,1)S(1)}, u32[]{:S(2)}) copy-start(bf16[512,512]{1,0:T(8,128)(2,1)S(1)} %collective-permute-done.3) | copy-start | bytes 1572868
  23.5 9.1 %collective-permute-start.7 = (bf16[512,512]{1,0:T(8,128)(2,1)S(1)}, bf16[512,512]{1,0:T(8,128)(2,1)S(1)}, u32[]{:S(2)}, u32[]{:S(2)}) collective-permute-start(bf16[512,512]{1,0:T(8,128)(2,1)S(1)} %collective-permute-done.2), channel_id=1, source_target_pairs={{0,1},{1,0},{2,3},{3,2},{4,5},{5,4},{6,7},{7,6},{8,9},{9,8},{10,11... | collective-permute-start | bytes 1572872 | tf_op jit(solution)/shard_map/ppermute | solution.py:307
  24.9 7.1 %collective-permute-start.6 = (bf16[512,512]{1,0:T(8,128)(2,1)S(1)}, bf16[512,512]{1,0:T(8,128)(2,1)S(1)}, u32[]{:S(2)}, u32[]{:S(2)}) collective-permute-start(bf16[512,512]{1,0:T(8,128)(2,1)S(1)} %collective-permute-done.1), channel_id=1, source_target_pairs={{0,1},{1,0},{2,3},{3,2},{4,5},{5,4},{6,7},{7,6},{8,9},{9,8},{10,11... | collective-permute-start | bytes 1572872 | tf_op jit(solution)/shard_map/ppermute | solution.py:307
  25.0 9.2 %collective-permute-start.5 = (bf16[256,512]{1,0:T(8,128)(2,1)S(1)}, bf16[256,512]{1,0:T(8,128)(2,1)S(1)}, u32[]{:S(2)}, u32[]{:S(2)}) collective-permute-start(bf16[256,512]{1,0:T(8,128)(2,1)S(1)} %slice.19), channel_id=1, source_target_pairs={{0,6},{2,0},{4,2},{6,4},{1,7},{3,1},{5,3},{7,5},{8,14},{10,8},{12,... | collective-permute-start | bytes 786440 | tf_op jit(solution)/shard_map/ppermute | solution.py:26
  27.7 8.3 %collective-permute-start.4 = (bf16[256,512]{1,0:T(8,128)(2,1)S(1)}, bf16[256,512]{1,0:T(8,128)(2,1)S(1)}, u32[]{:S(2)}, u32[]{:S(2)}) collective-permute-start(bf16[256,512]{1,0:T(8,128)(2,1)S(1)} %slice.18), channel_id=1, source_target_pairs={{0,2},{2,4},{4,6},{6,0},{1,3},{3,5},{5,7},{7,1},{8,10},{10,12},{12... | collective-permute-start | bytes 786440 | tf_op jit(solution)/shard_map/ppermute | solution.py:26
  36.2 3.3 %collective-permute-start.8 = (bf16[512,512]{1,0:T(8,128)(2,1)S(1)}, bf16[512,512]{1,0:T(8,128)(2,1)S(1)}, u32[]{:S(2)}, u32[]{:S(2)}) collective-permute-start(bf16[512,512]{1,0:T(8,128)(2,1)S(1)} %constant_dynamic-update-slice_fusion), channel_id=1, source_target_pairs={{0,1},{1,0},{2,3},{3,2},{4,5},{5,4},{6,7},{7,6},{8,9},{9,8},{10,11... | collective-permute-start | bytes 1572872 | tf_op jit(solution)/shard_map/ppermute | solution.py:307
  41.7 2.2 %collective-permute-start.9 = (bf16[640,512]{1,0:T(8,128)(2,1)S(1)}, bf16[640,512]{1,0:T(8,128)(2,1)S(1)}, u32[]{:S(2)}, u32[]{:S(2)}) collective-permute-start(bf16[640,512]{1,0:T(8,128)(2,1)S(1)} %add_convert_fusion.reduced_ref), channel_id=1, source_target_pairs={{0,1},{1,0},{2,3},{3,2},{4,5},{5,4},{6,7},{7,6},{8,9},{9,8},{10,11... | collective-permute-start | bytes 1966088 | tf_op jit(solution)/shard_map/ppermute | solution.py:307
  42.1 26.1 %collective-permute-start.11 = (f32[2,86,256]{2,1,0:T(8,128)S(1)}, f32[2,86,256]{2,1,0:T(8,128)S(1)}, u32[]{:S(2)}, u32[]{:S(2)}) collective-permute-start(f32[2,86,256]{2,1,0:T(8,128)S(1)} %get-tuple-element.105), channel_id=1, source_target_pairs={{0,1},{1,0},{2,3},{3,2},{4,5},{5,4},{6,7},{7,6},{8,9},{9,8},{10,11... | collective-permute-start | bytes 528392 | tf_op jit(solution)/shard_map/ppermute | solution.py:307
  50.0 28.7 %collective-permute-start.10 = (bf16[2,688,512]{2,1,0:T(8,128)(2,1)}, bf16[2,688,512]{2,1,0:T(8,128)(2,1)S(1)}, u32[]{:S(2)}, u32[]{:S(2)}) collective-permute-start(bf16[2,688,512]{2,1,0:T(8,128)(2,1)} %diagonal_grad.4), channel_id=1, source_target_pairs={{0,64},{1,17},{8,72},{9,25},{16,80},{17,1},{24,88},{25,9},{32,96},... | collective-permute-start | bytes 4227080 | tf_op jit(solution)/shard_map/ppermute | solution.py:291
  60.2 26.0 %collective-permute-start.12 = (bf16[2,688,512]{2,1,0:T(8,128)(2,1)}, bf16[2,688,512]{2,1,0:T(8,128)(2,1)}, u32[]{:S(2)}, u32[]{:S(2)}) collective-permute-start(bf16[2,688,512]{2,1,0:T(8,128)(2,1)} %diagonal_grad.6), channel_id=1, source_target_pairs={{0,32},{1,25},{8,40},{9,1},{16,48},{17,9},{24,56},{25,17},{32,64},... | collective-permute-start | bytes 4227080 | tf_op jit(solution)/shard_map/ppermute | solution.py:291
  67.0 19.2 %collective-permute-start.13 = (bf16[2,688,512]{2,1,0:T(8,128)(2,1)}, bf16[2,688,512]{2,1,0:T(8,128)(2,1)}, u32[]{:S(2)}, u32[]{:S(2)}) collective-permute-start(bf16[2,688,512]{2,1,0:T(8,128)(2,1)} %diagonal_grad.7), channel_id=1, source_target_pairs={{0,96},{1,9},{8,104},{9,17},{16,112},{17,25},{24,120},{25,1},{32,0... | collective-permute-start | bytes 4227080 | tf_op jit(solution)/shard_map/ppermute | solution.py:291
  75.3 10.9 %copy-start = (bf16[2,688,512]{2,1,0:T(8,128)(2,1)S(1)}, bf16[2,688,512]{2,1,0:T(8,128)(2,1)}, u32[]{:S(2)}) copy-start(bf16[2,688,512]{2,1,0:T(8,128)(2,1)} %diagonal_grad.5.refs_3_) | copy-start | bytes 4227076
  78.7 38.0 %copy-start.18 = (f32[2,172,256]{2,1,0:T(8,128)S(1)}, f32[2,172,256]{2,1,0:T(8,128)}, u32[]{:S(2)}) copy-start(f32[2,172,256]{2,1,0:T(8,128)} %maximum_select_fusion) | copy-start | bytes 1056772
  88.7 2.2 %collective-permute-start.14 = (bf16[2,688,256]{2,1,0:T(8,128)(2,1)S(1)}, bf16[2,688,256]{2,1,0:T(8,128)(2,1)S(1)}, u32[]{:S(2)}, u32[]{:S(2)}) collective-permute-start(bf16[2,688,256]{2,1,0:T(8,128)(2,1)S(1)} %get-tuple-element.74), channel_id=1, source_target_pairs={{0,1},{1,0},{2,3},{3,2},{4,5},{5,4},{6,7},{7,6},{8,9},{9,8},{10,11... | collective-permute-start | bytes 2113544 | tf_op jit(solution)/shard_map/ppermute | solution.py:307
  91.7 8.2 %collective-permute-start.15 = (bf16[4,172,256]{2,1,0:T(8,128)(2,1)S(1)}, bf16[4,172,256]{2,1,0:T(8,128)(2,1)S(1)}, u32[]{:S(2)}, u32[]{:S(2)}) collective-permute-start(bf16[4,172,256]{2,1,0:T(8,128)(2,1)S(1)} %get-tuple-element.76), channel_id=1, source_target_pairs={{0,80},{1,5},{2,82},{3,7},{4,84},{5,1},{6,86},{7,3},{8,88},{9,13},... | collective-permute-start | bytes 1056776 | tf_op jit(solution)/shard_map/ppermute | solution.py:196
  91.8 11.5 %collective-permute-start.16 = (bf16[4,172,256]{2,1,0:T(8,128)(2,1)S(1)}, bf16[4,172,256]{2,1,0:T(8,128)(2,1)S(1)}, u32[]{:S(2)}, u32[]{:S(2)}) collective-permute-start(bf16[4,172,256]{2,1,0:T(8,128)(2,1)S(1)} %get-tuple-element.77), channel_id=1, source_target_pairs={{0,40},{1,3},{2,42},{3,5},{4,44},{5,7},{6,46},{7,1},{8,48},{9,11},... | collective-permute-start | bytes 1056776 | tf_op jit(solution)/shard_map/ppermute | solution.py:196
  92.3 11.0 %collective-permute-start.17 = (bf16[4,172,256]{2,1,0:T(8,128)(2,1)S(1)}, bf16[4,172,256]{2,1,0:T(8,128)(2,1)S(1)}, u32[]{:S(2)}, u32[]{:S(2)}) collective-permute-start(bf16[4,172,256]{2,1,0:T(8,128)(2,1)S(1)} %get-tuple-element.78), channel_id=1, source_target_pairs={{0,120},{1,7},{2,122},{3,1},{4,124},{5,3},{6,126},{7,5},{8,96},{9,... | collective-permute-start | bytes 1056776 | tf_op jit(solution)/shard_map/ppermute | solution.py:196
  104.0 10.8 %collective-permute-start.18 = (bf16[172,256]{1,0:T(8,128)(2,1)S(1)}, bf16[172,256]{1,0:T(8,128)(2,1)S(1)}, u32[]{:S(2)}, u32[]{:S(2)}) collective-permute-start(bf16[172,256]{1,0:T(8,128)(2,1)S(1)} %get-tuple-element.80), channel_id=1, source_target_pairs={{0,4},{1,81},{2,6},{3,83},{4,0},{5,85},{6,2},{7,87},{8,12},{9,89},... | collective-permute-start | bytes 264200 | tf_op jit(solution)/shard_map/ppermute | solution.py:196
  110.0 6.7 %collective-permute-start.19 = (bf16[172,256]{1,0:T(8,128)(2,1)S(1)}, bf16[172,256]{1,0:T(8,128)(2,1)S(1)}, u32[]{:S(2)}, u32[]{:S(2)}) collective-permute-start(bf16[172,256]{1,0:T(8,128)(2,1)S(1)} %get-tuple-element.81), channel_id=1, source_target_pairs={{0,2},{1,41},{2,4},{3,43},{4,6},{5,45},{6,0},{7,47},{8,10},{9,49},... | collective-permute-start | bytes 264200 | tf_op jit(solution)/shard_map/ppermute | solution.py:196
  111.9 4.8 %collective-permute-start.20 = (bf16[172,256]{1,0:T(8,128)(2,1)S(1)}, bf16[172,256]{1,0:T(8,128)(2,1)S(1)}, u32[]{:S(2)}, u32[]{:S(2)}) collective-permute-start(bf16[172,256]{1,0:T(8,128)(2,1)S(1)} %get-tuple-element.82), channel_id=1, source_target_pairs={{0,6},{1,121},{2,0},{3,123},{4,2},{5,125},{6,4},{7,127},{8,14},{9,... | collective-permute-start | bytes 264200 | tf_op jit(solution)/shard_map/ppermute | solution.py:196
  116.9 8.4 %collective-permute-start.23 = (bf16[172,256]{1,0:T(8,128)(2,1)S(1)}, bf16[172,256]{1,0:T(8,128)(2,1)S(1)}, u32[]{:S(2)}, u32[]{:S(2)}) collective-permute-start(bf16[172,256]{1,0:T(8,128)(2,1)S(1)} %get-tuple-element.85.own_ref), channel_id=1, source_target_pairs={{0,2},{2,4},{4,6},{6,0},{1,3},{3,5},{5,7},{7,1},{8,10},{10,12},{12... | collective-permute-start | bytes 264200 | tf_op jit(solution)/shard_map/ppermute | solution.py:26
  117.0 8.3 %collective-permute-start.22 = (bf16[172,256]{1,0:T(8,128)(2,1)S(1)}, bf16[172,256]{1,0:T(8,128)(2,1)S(1)}, u32[]{:S(2)}, u32[]{:S(2)}) collective-permute-start(bf16[172,256]{1,0:T(8,128)(2,1)S(1)} %get-tuple-element.85.own_ref), channel_id=1, source_target_pairs={{0,6},{2,0},{4,2},{6,4},{1,7},{3,1},{5,3},{7,5},{8,14},{10,8},{12,... | collective-permute-start | bytes 264200 | tf_op jit(solution)/shard_map/ppermute | solution.py:26
  119.7 5.7 %collective-permute-start.21 = (bf16[172,256]{1,0:T(8,128)(2,1)S(1)}, bf16[172,256]{1,0:T(8,128)(2,1)S(1)}, u32[]{:S(2)}, u32[]{:S(2)}) collective-permute-start(bf16[172,256]{1,0:T(8,128)(2,1)S(1)} %get-tuple-element.85.own_ref), channel_id=1, source_target_pairs={{0,4},{2,6},{4,0},{6,2},{1,5},{3,7},{5,1},{7,3},{8,12},{10,14},{12... | collective-permute-start | bytes 264200 | tf_op jit(solution)/shard_map/ppermute | solution.py:26
  125.4 2.6 %collective-permute-start.26 = (f32[2,86,256]{2,1,0:T(8,128)S(1)}, f32[2,86,256]{2,1,0:T(8,128)S(1)}, u32[]{:S(2)}, u32[]{:S(2)}) collective-permute-start(f32[2,86,256]{2,1,0:T(8,128)S(1)} %get-tuple-element.103), channel_id=1, source_target_pairs={{0,1},{1,0},{2,3},{3,2},{4,5},{5,4},{6,7},{7,6},{8,9},{9,8},{10,11... | collective-permute-start | bytes 528392 | tf_op jit(solution)/shard_map/ppermute | solution.py:307
  127.0 1.8 %collective-permute-start.24 = (bf16[172,256]{1,0:T(8,128)(2,1)S(1)}, bf16[172,256]{1,0:T(8,128)(2,1)S(1)}, u32[]{:S(2)}, u32[]{:S(2)}) collective-permute-start(bf16[172,256]{1,0:T(8,128)(2,1)S(1)} %get-tuple-element.85.own_ref), channel_id=1, source_target_pairs={{0,1},{1,0},{2,3},{3,2},{4,5},{5,4},{6,7},{7,6},{8,9},{9,8},{10,11... | collective-permute-start | bytes 264200 | tf_op jit(solution)/shard_map/ppermute | solution.py:307
  127.1 1.8 %collective-permute-start.25 = (bf16[3,172,256]{2,1,0:T(8,128)(2,1)S(1)}, bf16[3,172,256]{2,1,0:T(8,128)(2,1)S(1)}, u32[]{:S(2)}, u32[]{:S(2)}) collective-permute-start(bf16[3,172,256]{2,1,0:T(8,128)(2,1)S(1)} %pad_maximum_fusion.own_far_ref), channel_id=1, source_target_pairs={{0,1},{1,0},{2,3},{3,2},{4,5},{5,4},{6,7},{7,6},{8,9},{9,8},{10,11... | collective-permute-start | bytes 792584 | tf_op jit(solution)/shard_map/ppermute | solution.py:307
  (17 other events, 70.3 us)
Sparse Core Ops, SparseCore 0:
  36.3 39.4 all-gather.1

commit v4 on v3

--- a/solution.py
+++ b/solution.py
@@ -108,7 +108,7 @@
             bytes_accessed=4 * count * tokens * window,
             transcendentals=0,
         ),
-        compiler_params=pltpu.CompilerParams(vmem_limit_bytes=52 << 20),
+        compiler_params=pltpu.CompilerParams(vmem_limit_bytes=50 << 20),
         name="diagonal_grad",
     )(table, mine, other, reduced, reduced_other)
 
@@ -120,23 +120,27 @@
     return total
 
 
-def halves_kernel(at_ref, *refs):
-    parts, outs = refs[:4], refs[4:6]
-    half = outs[0].shape[2]
-    for which in range(2):
-
-        @pl.when(at_ref[CORE] == which)
-        def _():
-            for j in range(2):
-                total = total_of(parts, j).astype(outs[0].dtype)
-                outs[which][j] = total[:, :half]
-                outs[1 - which][j] = total[:, half:]
-
-
-def sum_halves(table, parts):
+def half_kernel(at_ref, *refs):
+    parts, out = refs[:4], refs[4]
+    for j in range(out.shape[0]):
+        out[j] = total_of(parts, j).astype(out.dtype)
+
+
+def sum_half(table, parts, mine):
     blocks, block, columns = parts[0].shape
-    out = jax.ShapeDtypeStruct((blocks, block, columns // 2), jnp.bfloat16)
-    return in_vmem(halves_kernel, "sum_halves", [out, out], *parts, table=table)
+    half = pl.BlockSpec(
+        (blocks, block, columns // 2),
+        (lambda i, at: (0, 0, at[CORE])) if mine else (lambda i, at: (0, 0, 1 - at[CORE])),
+    )
+    return pl.pallas_call(
+        half_kernel,
+        grid_spec=pltpu.PrefetchScalarGridSpec(
+            num_scalar_prefetch=1, grid=(1,), in_specs=[half] * len(parts), out_specs=VMEM
+        ),
+        out_shape=jax.ShapeDtypeStruct((blocks, block, columns // 2), jnp.bfloat16),
+        compiler_params=pltpu.CompilerParams(vmem_limit_bytes=20 << 20),
+        name="sum_half",
+    )(table, *parts)
 
 
 def first_kernel(at_ref, *refs):
@@ -321,12 +325,11 @@
     table = jnp.stack([core, *firsts, *places, *first_out, 1 + 3 * core, *second_out, *quarter_at]).astype(jnp.int32)
     table, projector, out_grad = lax.optimization_barrier((table, projector, out_grad))
 
+    def columns_of(place):
+        return lax.dynamic_slice_in_dim(activations, places[place] * depth, depth, 1)
+
     def product(place, part):
-        return jnp.dot(
-            lax.dynamic_slice_in_dim(activations, places[place] * depth, depth, 1),
-            part,
-            preferred_element_type=jnp.float32,
-        )
+        return jnp.dot(columns_of(place), part, preferred_element_type=jnp.float32)
 
     near = [hop(projector, "x", -1), hop(projector, "x", 1)]
     here = [projector, swap(projector)]
@@ -338,11 +341,12 @@
     near = [near[0], swap(near[0]), near[1], swap(near[1])]
     for place, part in enumerate(near):
         total += product(2 + place, part)
-    far, total = lax.optimization_barrier((far, total))
+    last = [columns_of(6), columns_of(7)]
+    far, total, last = lax.optimization_barrier((far, total, last))
     far = [jnp.concatenate(far, axis=0)]
     far += [swap(far[0])]
-    for place, part in enumerate(far):
-        total += product(6 + place, part)
+    for columns, part in zip(last, far, strict=True):
+        total += jnp.dot(columns, part, preferred_element_type=jnp.float32)
     reduced = total.astype(jnp.bfloat16)
     reduced_other = swap(reduced)
 
@@ -371,7 +375,9 @@
     sums[0], projector_all, weight_all, moments = lax.optimization_barrier(
         (sums[0], projector_all, weight_all, moments)
     )
-    mine, other = sum_halves(table, sums)
+    other = sum_half(table, sums, False)
+    sums[0], other = lax.optimization_barrier((sums[0], other))
+    mine = sum_half(table, sums, True)
     sums = first_parts(table, mine, swap(other))
     sums = [sums[0], *(cross(sums[t], t, 0) for t in (2, 1, 3))]
     sums = second_parts(table, sums)

time: 143 us -> 141 us (0.986)
  matrix products: 10.6 us -> 6.78 us
  local copies, waits for them, and re-layouts: 9.08 us -> 11.8 us
  waiting for transfers between devices: 35.4 us -> 33.2 us
    pallas_call x0 -> x2, Pallas kernels: none -> 4.85 us  [sum_half(): pl.pallas_call(half_kernel, grid_spec=pltpu.PrefetchScalarGridSpec(num_sc...]
    ppermute x11, waiting for transfers between devices: 9.98 us -> 5.97 us  [swap(): return lax.ppermute(array, 'core', SWAP)]
    dot_general x8, matrix products: 10.6 us -> 6.78 us  [the longest x6 5.74 us: product(): return jnp.dot(columns_of(place), part, preferred_element_type=jnp.float32)]
    pallas_call x3 -> x2, Pallas kernels: 3.96 us -> 1.48 us  [in_vmem(): pl.pallas_call(kernel, in_specs=first + [VMEM] * (len(operands) - len(fir...]
    dynamic_slice x0 -> x1, local copies, waits for them, and re-layouts: none -> 2.21 us  [columns_of(): lax.dynamic_slice_in_dim(activations, places[place] * depth, depth, 1)]
    unnamed x50 -> x48, local copies, waits for them, and re-layouts: 8.13 us -> 8.62 us
  transfers between devices with their start and end apart: 28 -> 28, of which waited for: 11 -> 11; matrix products, arithmetic and copies ran while one was open for 9% -> 8% of each run, Pallas kernels for 18% -> 19%
where the time goes in v4:
time: 141 us
  Pallas kernels  37.9 us (27%)
  starting transfers between devices  34.9 us (25%)
  waiting for transfers between devices  33.2 us (24%)
  between operations  14.5 us (10%)
  local copies, waits for them, and re-layouts  11.8 us (8%)
  matrix products  6.78 us (5%)
  other arithmetic  2.04 us (1%)
    pallas_call x4, Pallas kernels, diagonal_grad(): pl.pallas_call(functools.partial(diagonal_kernel, numbers), in_specs=[SME...  23.8 us
    ppermute x6, starting transfers between devices, cross(): return lax.ppermute(array, ('y', 'z', 'x', 'core'), pairs)  13.7 us
    ppermute x6, waiting for transfers between devices, cross(): return lax.ppermute(array, ('y', 'z', 'x', 'core'), pairs)  10.6 us
    unnamed x48, local copies, waits for them, and re-layouts  8.62 us
    ppermute x3, waiting for transfers between devices, exchange(): return lax.ppermute(array, ('y', 'z', 'core'), pairs)  8.6 us
    ppermute x7, starting transfers between devices, hop(): lax.ppermute(array, axis, [(i, (i + distance) % SIDE) for i in range(SIDE)])  8.08 us
    ppermute x7, waiting for transfers between devices, hop(): lax.ppermute(array, axis, [(i, (i + distance) % SIDE) for i in range(SIDE)])  8.06 us
    ppermute x11, starting transfers between devices, swap(): return lax.ppermute(array, 'core', SWAP)  7.43 us
  transfers between devices with their start and end apart: 28, of which 11 were waited for; matrix products, arithmetic and copies ran while one was open for 8% of the time, Pallas kernels for 19%

profile of v4, /device:TPU:1, one launch (start us, length us, event | category | flops | bytes accessed | tf_op | source)
XLA Modules:
  0.0 141.1 jit_solution(6863447911881892475)
XLA Ops:
  7.4 1.5 %collective-permute-start = (bf16[640,11008]{1,0:T(8,128)(2,1)}, bf16[640,11008]{1,0:T(8,128)(2,1)}, u32[]{:S(2)}, u32[]{:S(2)}) collective-permute-start(bf16[640,11008]{1,0:T(8,128)(2,1)} %mine_ref.3), channel_id=1, source_target_pairs={{0,1},{1,0},{2,3},{3,2},{4,5},{5,4},{6,7},{7,6},{8,9},{9,8},{10,11... | collective-permute-start | bytes 42270728 | tf_op jit(solution)/shard_map/ppermute | solution.py:311
  9.0 1.3 collective-permute-start.2
  10.3 1.4 collective-permute-start.1
  11.6 2.2 %constant_dynamic-slice_fusion = (bf16[640,512]{1,0:T(8,128)(2,1)S(1)}, bf16[640,512]{1,0:T(8,128)(2,1)}) fusion(bf16[640,4096]{1,0:T(8,128)(2,1)} %param.6, s32[]{:T(128)S(6)} %select_n.92, s32[]{:T(128)S(6)} %select_n.91), kind=kLoop, calls=%fused_computation.45 | loop fusion | bytes 2621448 | tf_op jit(solution)/shard_map/dynamic_slice | solution.py:329
  13.9 1.9 %fusion.11 = f32[640,512]{1,0:T(8,128)S(1)} fusion(bf16[512,512]{1,0:T(8,128)(2,1)} %param.8, bf16[640,4096]{1,0:T(8,128)(2,1)} %param.6, s32[]{:T(128)S(6)} %select_n.85), kind=kOutput, calls=%fused_computation.12 | convolution fusion | flops 335544320 | bytes 2490372 | tf_op jit(solution)/shard_map/dot_general | solution.py:332
  16.3 1.8 %convolution_add_fusion = f32[640,512]{1,0:T(8,128)S(1)} fusion(f32[640,512]{1,0:T(8,128)S(1)} %fusion.11, bf16[512,512]{1,0:T(8,128)(2,1)S(1)} %collective-permute-done.3, bf16[640,4096]{1,0:T(8,128)(2,1)} %param.6, s32[]{:T(128)S(6)} %select_n.86), kind=kOutput, calls=%fused_computation | convolution fusion | flops 335872000 | bytes 3801092 | tf_op jit(solution)/shard_map/dot_general | solution.py:332
  18.0 5.4 %collective-permute-done.2 = bf16[512,512]{1,0:T(8,128)(2,1)S(1)} collective-permute-done((bf16[512,512]{1,0:T(8,128)(2,1)}, bf16[512,512]{1,0:T(8,128)(2,1)S(1)}, u32[]{:S(2)}, u32[]{:S(2)}) %collective-permute-start.2) | collective-permute-done | bytes 524320 | tf_op jit(solution)/shard_map/ppermute | solution.py:26
  23.5 1.4 collective-permute-start.7
  25.0 2.7 %collective-permute-start.5 = (bf16[256,512]{1,0:T(8,128)(2,1)S(1)}, bf16[256,512]{1,0:T(8,128)(2,1)S(1)}, u32[]{:S(2)}, u32[]{:S(2)}) collective-permute-start(bf16[256,512]{1,0:T(8,128)(2,1)S(1)} %slice.19), channel_id=1, source_target_pairs={{0,6},{2,0},{4,2},{6,4},{1,7},{3,1},{5,3},{7,5},{8,14},{10,8},{12,... | collective-permute-start | bytes 786440 | tf_op jit(solution)/shard_map/ppermute | solution.py:26
  28.7 3.3 %collective-permute-done.6 = bf16[512,512]{1,0:T(8,128)(2,1)S(1)} collective-permute-done((bf16[512,512]{1,0:T(8,128)(2,1)S(1)}, bf16[512,512]{1,0:T(8,128)(2,1)S(1)}, u32[]{:S(2)}, u32[]{:S(2)}) %collective-permute-start.6) | collective-permute-done | bytes 524320 | tf_op jit(solution)/shard_map/ppermute | solution.py:311
  33.4 2.6 %collective-permute-done.4 = bf16[256,512]{1,0:T(8,128)(2,1)S(1)} collective-permute-done((bf16[256,512]{1,0:T(8,128)(2,1)S(1)}, bf16[256,512]{1,0:T(8,128)(2,1)S(1)}, u32[]{:S(2)}, u32[]{:S(2)}) %collective-permute-start.4) | collective-permute-done | bytes 262176 | tf_op jit(solution)/shard_map/ppermute | solution.py:26
  36.1 1.7 %collective-permute-start.8 = (bf16[512,512]{1,0:T(8,128)(2,1)S(1)}, bf16[512,512]{1,0:T(8,128)(2,1)S(1)}, u32[]{:S(2)}, u32[]{:S(2)}) collective-permute-start(bf16[512,512]{1,0:T(8,128)(2,1)S(1)} %constant_dynamic-update-slice_fusion), channel_id=1, source_target_pairs={{0,1},{1,0},{2,3},{3,2},{4,5},{5,4},{6,7},{7,6},{8,9},{9,8},{10,11... | collective-permute-start | bytes 1572872 | tf_op jit(solution)/shard_map/ppermute | solution.py:311
  42.2 6.2 %diagonal_grad.4 = bf16[2,688,512]{2,1,0:T(8,128)(2,1)} custom-call(s32[30]{0:T(128)S(1)} %stack.153.at_ref, bf16[640,11008]{1,0:T(8,128)(2,1)} %mine_ref.3, bf16[640,11008]{1,0:T(8,128)(2,1)} %collective-permute-done.other_ref, bf16[640,512]{1,0:T(8,128)(2,1)S(1)} %add_convert_fusion.reduced_ref, bf16[640,512]{1,0:T(8,128)(2,1)S(1)} %collective-permute-done.9.reduced_other_ref), custom_call_target="tpu_custom_call" | custom-call | flops 2348810240 | bytes 4587520 | tf_op jit(solution)/shard_map/diagonal_grad/pallas_call | solution.py:95
  48.4 3.8 %collective-permute-start.10 = (bf16[2,688,512]{2,1,0:T(8,128)(2,1)}, bf16[2,688,512]{2,1,0:T(8,128)(2,1)}, u32[]{:S(2)}, u32[]{:S(2)}) collective-permute-start(bf16[2,688,512]{2,1,0:T(8,128)(2,1)} %diagonal_grad.4), channel_id=1, source_target_pairs={{0,64},{1,17},{8,72},{9,25},{16,80},{17,1},{24,88},{25,9},{32,96},... | collective-permute-start | bytes 4227080 | tf_op jit(solution)/shard_map/ppermute | solution.py:295
  52.2 6.2 %diagonal_grad.6 = bf16[2,688,512]{2,1,0:T(8,128)(2,1)} custom-call(s32[30]{0:T(128)S(1)} %stack.153.at_ref, bf16[640,11008]{1,0:T(8,128)(2,1)} %mine_ref.3, bf16[640,11008]{1,0:T(8,128)(2,1)} %collective-permute-done.other_ref, bf16[640,512]{1,0:T(8,128)(2,1)S(1)} %add_convert_fusion.reduced_ref, bf16[640,512]{1,0:T(8,128)(2,1)S(1)} %collective-permute-done.9.reduced_other_ref), custom_call_target="tpu_custom_call" | custom-call | flops 2348810240 | bytes 4587520 | tf_op jit(solution)/shard_map/diagonal_grad/pallas_call | solution.py:95
  59.0 6.2 %diagonal_grad.7 = bf16[2,688,512]{2,1,0:T(8,128)(2,1)} custom-call(s32[30]{0:T(128)S(1)} %stack.153.at_ref, bf16[640,11008]{1,0:T(8,128)(2,1)} %mine_ref.3, bf16[640,11008]{1,0:T(8,128)(2,1)} %collective-permute-done.other_ref, bf16[640,512]{1,0:T(8,128)(2,1)S(1)} %add_convert_fusion.reduced_ref, bf16[640,512]{1,0:T(8,128)(2,1)S(1)} %collective-permute-done.9.reduced_other_ref), custom_call_target="tpu_custom_call" | custom-call | flops 2348810240 | bytes 4587520 | tf_op jit(solution)/shard_map/diagonal_grad/pallas_call | solution.py:95
  67.2 5.2 %diagonal_grad.5.refs_3_ = bf16[2,688,512]{2,1,0:T(8,128)(2,1)S(1)} custom-call(s32[30]{0:T(128)S(1)} %stack.153.at_ref, bf16[640,11008]{1,0:T(8,128)(2,1)} %mine_ref.3, bf16[640,11008]{1,0:T(8,128)(2,1)} %collective-permute-done.other_ref, bf16[640,512]{1,0:T(8,128)(2,1)S(1)} %add_convert_fusion.reduced_ref, ...), custom_call_target="tpu_custom_call" | custom-call | flops 2348810240 | bytes 4587520 | tf_op jit(solution)/shard_map/diagonal_grad/pallas_call | solution.py:95
  73.8 2.0 %copy-done.1 = bf16[4096,512]{1,0:T(8,128)(2,1)} copy-done((bf16[4096,512]{1,0:T(8,128)(2,1)}, bf16[4096,512]{1,0:T(8,128)(2,1)S(1)}, u32[]{:S(2)}) %copy-start.1) | copy-done | bytes 4194328
  75.8 8.6 %collective-permute-done.12.refs_1_ = bf16[2,688,512]{2,1,0:T(8,128)(2,1)} collective-permute-done((bf16[2,688,512]{2,1,0:T(8,128)(2,1)}, bf16[2,688,512]{2,1,0:T(8,128)(2,1)}, u32[]{:S(2)}, u32[]{:S(2)}) %collective-permute-start.12) | collective-permute-done | bytes 1409056 | tf_op jit(solution)/shard_map/ppermute | solution.py:295
  84.4 2.4 %sum_half.2 = bf16[2,688,256]{2,1,0:T(8,128)(2,1)S(1)} custom-call(s32[30]{0:T(128)S(1)} %stack.153.at_ref, bf16[2,688,512]{2,1,0:T(8,128)(2,1)} %collective-permute-done.10.refs_0_, bf16[2,688,512]{2,1,0:T(8,128)(2,1)} %collective-permute-done.12.refs_1_, bf16[2,688,512]{2,1,0:T(8,128)(2,1)} %collective-permute-done.13.refs_2_, ...), custom_call_target="tpu_custom_call" | custom-call | tf_op jit(solution)/shard_map/sum_half/pallas_call | solution.py:135
  87.4 2.4 %sum_half.3.refs_0_ = bf16[2,688,256]{2,1,0:T(8,128)(2,1)S(1)} custom-call(s32[30]{0:T(128)S(1)} %stack.153.at_ref, bf16[2,688,512]{2,1,0:T(8,128)(2,1)} %collective-permute-done.10.refs_0_, bf16[2,688,512]{2,1,0:T(8,128)(2,1)} %collective-permute-done.12.refs_1_, bf16[2,688,512]{2,1,0:T(8,128)(2,1)} %collective-permute-done.13.refs_2_, ...), custom_call_target="tpu_custom_call" | custom-call | tf_op jit(solution)/shard_map/sum_half/pallas_call | solution.py:135
  91.2 2.2 %collective-permute-start.17 = (bf16[4,172,256]{2,1,0:T(8,128)(2,1)S(1)}, bf16[4,172,256]{2,1,0:T(8,128)(2,1)S(1)}, u32[]{:S(2)}, u32[]{:S(2)}) collective-permute-start(bf16[4,172,256]{2,1,0:T(8,128)(2,1)S(1)} %get-tuple-element.82), channel_id=1, source_target_pairs={{0,120},{1,7},{2,122},{3,1},{4,124},{5,3},{6,126},{7,5},{8,96},{9,... | collective-permute-start | bytes 1056776 | tf_op jit(solution)/shard_map/ppermute | solution.py:200
  93.4 5.4 %collective-permute-done.15.refs_1_ = bf16[4,172,256]{2,1,0:T(8,128)(2,1)S(1)} collective-permute-done((bf16[4,172,256]{2,1,0:T(8,128)(2,1)S(1)}, bf16[4,172,256]{2,1,0:T(8,128)(2,1)S(1)}, u32[]{:S(2)}, u32[]{:S(2)}) %collective-permute-start.15) | collective-permute-done | bytes 352288 | tf_op jit(solution)/shard_map/ppermute | solution.py:200
  98.8 3.3 %collective-permute-done.16.refs_2_ = bf16[4,172,256]{2,1,0:T(8,128)(2,1)S(1)} collective-permute-done((bf16[4,172,256]{2,1,0:T(8,128)(2,1)S(1)}, bf16[4,172,256]{2,1,0:T(8,128)(2,1)S(1)}, u32[]{:S(2)}, u32[]{:S(2)}) %collective-permute-start.16) | collective-permute-done | bytes 352288 | tf_op jit(solution)/shard_map/ppermute | solution.py:200
  102.8 6.1 %collective-permute-start.18 = (bf16[172,256]{1,0:T(8,128)(2,1)S(1)}, bf16[172,256]{1,0:T(8,128)(2,1)S(1)}, u32[]{:S(2)}, u32[]{:S(2)}) collective-permute-start(bf16[172,256]{1,0:T(8,128)(2,1)S(1)} %get-tuple-element.84), channel_id=1, source_target_pairs={{0,4},{1,81},{2,6},{3,83},{4,0},{5,85},{6,2},{7,87},{8,12},{9,89},... | collective-permute-start | bytes 264200 | tf_op jit(solution)/shard_map/ppermute | solution.py:200
  108.9 1.8 %collective-permute-start.19 = (bf16[172,256]{1,0:T(8,128)(2,1)S(1)}, bf16[172,256]{1,0:T(8,128)(2,1)S(1)}, u32[]{:S(2)}, u32[]{:S(2)}) collective-permute-start(bf16[172,256]{1,0:T(8,128)(2,1)S(1)} %get-tuple-element.85), channel_id=1, source_target_pairs={{0,2},{1,41},{2,4},{3,43},{4,6},{5,45},{6,0},{7,47},{8,10},{9,49},... | collective-permute-start | bytes 264200 | tf_op jit(solution)/shard_map/ppermute | solution.py:200
  110.7 3.0 %collective-permute-start.20 = (bf16[172,256]{1,0:T(8,128)(2,1)S(1)}, bf16[172,256]{1,0:T(8,128)(2,1)S(1)}, u32[]{:S(2)}, u32[]{:S(2)}) collective-permute-start(bf16[172,256]{1,0:T(8,128)(2,1)S(1)} %get-tuple-element.86), channel_id=1, source_target_pairs={{0,6},{1,121},{2,0},{3,123},{4,2},{5,125},{6,4},{7,127},{8,14},{9,... | collective-permute-start | bytes 264200 | tf_op jit(solution)/shard_map/ppermute | solution.py:200
  113.7 1.9 %collective-permute-done.19 = bf16[172,256]{1,0:T(8,128)(2,1)S(1)} collective-permute-done((bf16[172,256]{1,0:T(8,128)(2,1)S(1)}, bf16[172,256]{1,0:T(8,128)(2,1)S(1)}, u32[]{:S(2)}, u32[]{:S(2)}) %collective-permute-start.19) | collective-permute-done | bytes 88096 | tf_op jit(solution)/shard_map/ppermute | solution.py:200
  115.9 2.7 %collective-permute-start.22 = (bf16[172,256]{1,0:T(8,128)(2,1)S(1)}, bf16[172,256]{1,0:T(8,128)(2,1)S(1)}, u32[]{:S(2)}, u32[]{:S(2)}) collective-permute-start(bf16[172,256]{1,0:T(8,128)(2,1)S(1)} %get-tuple-element.89.own_ref), channel_id=1, source_target_pairs={{0,6},{2,0},{4,2},{6,4},{1,7},{3,1},{5,3},{7,5},{8,14},{10,8},{12,... | collective-permute-start | bytes 264200 | tf_op jit(solution)/shard_map/ppermute | solution.py:26
  118.6 2.6 %copy-done = bf16[4096,688]{0,1:T(8,128)(2,1)S(1)} copy-done((bf16[4096,688]{0,1:T(8,128)(2,1)S(1)}, bf16[4096,688]{0,1:T(8,128)(2,1)}, u32[]{:S(2)}) %copy-start) | copy-done | bytes 5636120
  121.2 2.2 %copy-done.2 = bf16[4096,512]{1,0:T(8,128)(2,1)S(1)} copy-done((bf16[4096,512]{1,0:T(8,128)(2,1)S(1)}, bf16[4096,512]{1,0:T(8,128)(2,1)}, u32[]{:S(2)}) %copy-start.2) | copy-done | bytes 4194328
  127.3 6.9 %update.1 = bf16[688,4096]{1,0:T(8,128)(2,1)} custom-call(s32[30]{0:T(128)S(1)} %stack.153.at_ref, bf16[172,256]{1,0:T(8,128)(2,1)S(1)} %get-tuple-element.89.own_ref, bf16[3,172,256]{2,1,0:T(8,128)(2,1)S(1)} %pad_maximum_fusion.own_far_ref, bf16[172,256]{1,0:T(8,128)(2,1)S(1)} %collective-permute-done.24.other_ref, ...), custom_call_target="tpu_custom_call" | custom-call | tf_op jit(solution)/shard_map/update/pallas_call | solution.py:271
  (104 shorter events, 18.3 us)
Async XLA Ops:
  7.2 68.7 %all-gather.2.cloned.1.call-start = ((), (), s32[]{:S(2)}) async-start(), calls=%async_computation | async-start | bytes 6340608 | tf_op jit(solution)/shard_map/all_gather | solution.py:366
  7.4 34.9 %collective-permute-start = (bf16[640,11008]{1,0:T(8,128)(2,1)}, bf16[640,11008]{1,0:T(8,128)(2,1)}, u32[]{:S(2)}, u32[]{:S(2)}) collective-permute-start(bf16[640,11008]{1,0:T(8,128)(2,1)} %mine_ref.3), channel_id=1, source_target_pairs={{0,1},{1,0},{2,3},{3,2},{4,5},{5,4},{6,7},{7,6},{8,9},{9,8},{10,11... | collective-permute-start | bytes 42270728 | tf_op jit(solution)/shard_map/ppermute | solution.py:311
  8.9 7.4 %collective-permute-start.3 = (bf16[512,512]{1,0:T(8,128)(2,1)}, bf16[512,512]{1,0:T(8,128)(2,1)S(1)}, u32[]{:S(2)}, u32[]{:S(2)}) collective-permute-start(bf16[512,512]{1,0:T(8,128)(2,1)} %param.8), channel_id=1, source_target_pairs={{0,1},{1,0},{2,3},{3,2},{4,5},{5,4},{6,7},{7,6},{8,9},{9,8},{10,11... | collective-permute-start | bytes 1572872 | tf_op jit(solution)/shard_map/ppermute | solution.py:311
  9.0 14.5 %collective-permute-start.2 = (bf16[512,512]{1,0:T(8,128)(2,1)}, bf16[512,512]{1,0:T(8,128)(2,1)S(1)}, u32[]{:S(2)}, u32[]{:S(2)}) collective-permute-start(bf16[512,512]{1,0:T(8,128)(2,1)} %param.8), channel_id=1, source_target_pairs={{0,2},{2,4},{4,6},{6,0},{1,3},{3,5},{5,7},{7,1},{8,10},{10,12},{12... | collective-permute-start | bytes 1572872 | tf_op jit(solution)/shard_map/ppermute | solution.py:26
  10.3 13.2 %collective-permute-start.1 = (bf16[512,512]{1,0:T(8,128)(2,1)}, bf16[512,512]{1,0:T(8,128)(2,1)S(1)}, u32[]{:S(2)}, u32[]{:S(2)}) collective-permute-start(bf16[512,512]{1,0:T(8,128)(2,1)} %param.8), channel_id=1, source_target_pairs={{0,6},{2,0},{4,2},{6,4},{1,7},{3,1},{5,3},{7,5},{8,14},{10,8},{12,... | collective-permute-start | bytes 1572872 | tf_op jit(solution)/shard_map/ppermute | solution.py:26
  13.9 13.8 %copy-start.3 = (bf16[640,4096]{1,0:T(8,128)(2,1)S(1)}, bf16[640,4096]{1,0:T(8,128)(2,1)}, u32[]{:S(2)}) copy-start(bf16[640,4096]{1,0:T(8,128)(2,1)} %param.6) | copy-start | bytes 15728644
  16.3 12.5 %copy-start.12 = (bf16[512,512]{1,0:T(8,128)(2,1)}, bf16[512,512]{1,0:T(8,128)(2,1)S(1)}, u32[]{:S(2)}) copy-start(bf16[512,512]{1,0:T(8,128)(2,1)S(1)} %collective-permute-done.3) | copy-start | bytes 1572868
  23.5 9.1 %copy-start.6 = (bf16[512,512]{1,0:T(8,128)(2,1)}, bf16[512,512]{1,0:T(8,128)(2,1)S(1)}, u32[]{:S(2)}) copy-start(bf16[512,512]{1,0:T(8,128)(2,1)S(1)} %collective-permute-done.1) | copy-start | bytes 1572868
  23.5 9.3 %collective-permute-start.7 = (bf16[512,512]{1,0:T(8,128)(2,1)S(1)}, bf16[512,512]{1,0:T(8,128)(2,1)S(1)}, u32[]{:S(2)}, u32[]{:S(2)}) collective-permute-start(bf16[512,512]{1,0:T(8,128)(2,1)S(1)} %collective-permute-done.2), channel_id=1, source_target_pairs={{0,1},{1,0},{2,3},{3,2},{4,5},{5,4},{6,7},{7,6},{8,9},{9,8},{10,11... | collective-permute-start | bytes 1572872 | tf_op jit(solution)/shard_map/ppermute | solution.py:311
  24.9 7.1 %collective-permute-start.6 = (bf16[512,512]{1,0:T(8,128)(2,1)S(1)}, bf16[512,512]{1,0:T(8,128)(2,1)S(1)}, u32[]{:S(2)}, u32[]{:S(2)}) collective-permute-start(bf16[512,512]{1,0:T(8,128)(2,1)S(1)} %collective-permute-done.1), channel_id=1, source_target_pairs={{0,1},{1,0},{2,3},{3,2},{4,5},{5,4},{6,7},{7,6},{8,9},{9,8},{10,11... | collective-permute-start | bytes 1572872 | tf_op jit(solution)/shard_map/ppermute | solution.py:311
  25.0 8.4 %collective-permute-start.5 = (bf16[256,512]{1,0:T(8,128)(2,1)S(1)}, bf16[256,512]{1,0:T(8,128)(2,1)S(1)}, u32[]{:S(2)}, u32[]{:S(2)}) collective-permute-start(bf16[256,512]{1,0:T(8,128)(2,1)S(1)} %slice.19), channel_id=1, source_target_pairs={{0,6},{2,0},{4,2},{6,4},{1,7},{3,1},{5,3},{7,5},{8,14},{10,8},{12,... | collective-permute-start | bytes 786440 | tf_op jit(solution)/shard_map/ppermute | solution.py:26
  27.7 8.3 %collective-permute-start.4 = (bf16[256,512]{1,0:T(8,128)(2,1)S(1)}, bf16[256,512]{1,0:T(8,128)(2,1)S(1)}, u32[]{:S(2)}, u32[]{:S(2)}) collective-permute-start(bf16[256,512]{1,0:T(8,128)(2,1)S(1)} %slice.18), channel_id=1, source_target_pairs={{0,2},{2,4},{4,6},{6,0},{1,3},{3,5},{5,7},{7,1},{8,10},{10,12},{12... | collective-permute-start | bytes 786440 | tf_op jit(solution)/shard_map/ppermute | solution.py:26
  36.1 3.2 %collective-permute-start.8 = (bf16[512,512]{1,0:T(8,128)(2,1)S(1)}, bf16[512,512]{1,0:T(8,128)(2,1)S(1)}, u32[]{:S(2)}, u32[]{:S(2)}) collective-permute-start(bf16[512,512]{1,0:T(8,128)(2,1)S(1)} %constant_dynamic-update-slice_fusion), channel_id=1, source_target_pairs={{0,1},{1,0},{2,3},{3,2},{4,5},{5,4},{6,7},{7,6},{8,9},{9,8},{10,11... | collective-permute-start | bytes 1572872 | tf_op jit(solution)/shard_map/ppermute | solution.py:311
  40.1 2.1 %collective-permute-start.9 = (bf16[640,512]{1,0:T(8,128)(2,1)S(1)}, bf16[640,512]{1,0:T(8,128)(2,1)S(1)}, u32[]{:S(2)}, u32[]{:S(2)}) collective-permute-start(bf16[640,512]{1,0:T(8,128)(2,1)S(1)} %add_convert_fusion.reduced_ref), channel_id=1, source_target_pairs={{0,1},{1,0},{2,3},{3,2},{4,5},{5,4},{6,7},{7,6},{8,9},{9,8},{10,11... | collective-permute-start | bytes 1966088 | tf_op jit(solution)/shard_map/ppermute | solution.py:311
  41.5 25.0 %collective-permute-start.11 = (f32[2,86,256]{2,1,0:T(8,128)S(1)}, f32[2,86,256]{2,1,0:T(8,128)S(1)}, u32[]{:S(2)}, u32[]{:S(2)}) collective-permute-start(f32[2,86,256]{2,1,0:T(8,128)S(1)} %get-tuple-element.111), channel_id=1, source_target_pairs={{0,1},{1,0},{2,3},{3,2},{4,5},{5,4},{6,7},{7,6},{8,9},{9,8},{10,11... | collective-permute-start | bytes 528392 | tf_op jit(solution)/shard_map/ppermute | solution.py:311
  48.4 27.5 %collective-permute-start.10 = (bf16[2,688,512]{2,1,0:T(8,128)(2,1)}, bf16[2,688,512]{2,1,0:T(8,128)(2,1)}, u32[]{:S(2)}, u32[]{:S(2)}) collective-permute-start(bf16[2,688,512]{2,1,0:T(8,128)(2,1)} %diagonal_grad.4), channel_id=1, source_target_pairs={{0,64},{1,17},{8,72},{9,25},{16,80},{17,1},{24,88},{25,9},{32,96},... | collective-permute-start | bytes 4227080 | tf_op jit(solution)/shard_map/ppermute | solution.py:295
  58.4 26.0 %collective-permute-start.12 = (bf16[2,688,512]{2,1,0:T(8,128)(2,1)}, bf16[2,688,512]{2,1,0:T(8,128)(2,1)}, u32[]{:S(2)}, u32[]{:S(2)}) collective-permute-start(bf16[2,688,512]{2,1,0:T(8,128)(2,1)} %diagonal_grad.6), channel_id=1, source_target_pairs={{0,32},{1,25},{8,40},{9,1},{16,48},{17,9},{24,56},{25,17},{32,64},... | collective-permute-start | bytes 4227080 | tf_op jit(solution)/shard_map/ppermute | solution.py:295
  65.2 19.3 %collective-permute-start.13 = (bf16[2,688,512]{2,1,0:T(8,128)(2,1)}, bf16[2,688,512]{2,1,0:T(8,128)(2,1)}, u32[]{:S(2)}, u32[]{:S(2)}) collective-permute-start(bf16[2,688,512]{2,1,0:T(8,128)(2,1)} %diagonal_grad.7), channel_id=1, source_target_pairs={{0,96},{1,9},{8,104},{9,17},{16,112},{17,25},{24,120},{25,1},{32,0... | collective-permute-start | bytes 4227080 | tf_op jit(solution)/shard_map/ppermute | solution.py:295
  86.9 28.8 %copy-start.18 = (f32[2,172,256]{2,1,0:T(8,128)S(1)}, f32[2,172,256]{2,1,0:T(8,128)}, u32[]{:S(2)}) copy-start(f32[2,172,256]{2,1,0:T(8,128)} %maximum_select_fusion) | copy-start | bytes 1056772
  86.9 2.9 %collective-permute-start.14 = (bf16[2,688,256]{2,1,0:T(8,128)(2,1)S(1)}, bf16[2,688,256]{2,1,0:T(8,128)(2,1)S(1)}, u32[]{:S(2)}, u32[]{:S(2)}) collective-permute-start(bf16[2,688,256]{2,1,0:T(8,128)(2,1)S(1)} %sum_half.2), channel_id=1, source_target_pairs={{0,1},{1,0},{2,3},{3,2},{4,5},{5,4},{6,7},{7,6},{8,9},{9,8},{10,11... | collective-permute-start | bytes 2113544 | tf_op jit(solution)/shard_map/ppermute | solution.py:311
  90.6 8.2 %collective-permute-start.15 = (bf16[4,172,256]{2,1,0:T(8,128)(2,1)S(1)}, bf16[4,172,256]{2,1,0:T(8,128)(2,1)S(1)}, u32[]{:S(2)}, u32[]{:S(2)}) collective-permute-start(bf16[4,172,256]{2,1,0:T(8,128)(2,1)S(1)} %get-tuple-element.80), channel_id=1, source_target_pairs={{0,80},{1,5},{2,82},{3,7},{4,84},{5,1},{6,86},{7,3},{8,88},{9,13},... | collective-permute-start | bytes 1056776 | tf_op jit(solution)/shard_map/ppermute | solution.py:200
  90.7 11.4 %collective-permute-start.16 = (bf16[4,172,256]{2,1,0:T(8,128)(2,1)S(1)}, bf16[4,172,256]{2,1,0:T(8,128)(2,1)S(1)}, u32[]{:S(2)}, u32[]{:S(2)}) collective-permute-start(bf16[4,172,256]{2,1,0:T(8,128)(2,1)S(1)} %get-tuple-element.81), channel_id=1, source_target_pairs={{0,40},{1,3},{2,42},{3,5},{4,44},{5,7},{6,46},{7,1},{8,48},{9,11},... | collective-permute-start | bytes 1056776 | tf_op jit(solution)/shard_map/ppermute | solution.py:200
  91.2 10.9 %collective-permute-start.17 = (bf16[4,172,256]{2,1,0:T(8,128)(2,1)S(1)}, bf16[4,172,256]{2,1,0:T(8,128)(2,1)S(1)}, u32[]{:S(2)}, u32[]{:S(2)}) collective-permute-start(bf16[4,172,256]{2,1,0:T(8,128)(2,1)S(1)} %get-tuple-element.82), channel_id=1, source_target_pairs={{0,120},{1,7},{2,122},{3,1},{4,124},{5,3},{6,126},{7,5},{8,96},{9,... | collective-permute-start | bytes 1056776 | tf_op jit(solution)/shard_map/ppermute | solution.py:200
  102.8 10.9 %collective-permute-start.18 = (bf16[172,256]{1,0:T(8,128)(2,1)S(1)}, bf16[172,256]{1,0:T(8,128)(2,1)S(1)}, u32[]{:S(2)}, u32[]{:S(2)}) collective-permute-start(bf16[172,256]{1,0:T(8,128)(2,1)S(1)} %get-tuple-element.84), channel_id=1, source_target_pairs={{0,4},{1,81},{2,6},{3,83},{4,0},{5,85},{6,2},{7,87},{8,12},{9,89},... | collective-permute-start | bytes 264200 | tf_op jit(solution)/shard_map/ppermute | solution.py:200
  108.9 6.7 %collective-permute-start.19 = (bf16[172,256]{1,0:T(8,128)(2,1)S(1)}, bf16[172,256]{1,0:T(8,128)(2,1)S(1)}, u32[]{:S(2)}, u32[]{:S(2)}) collective-permute-start(bf16[172,256]{1,0:T(8,128)(2,1)S(1)} %get-tuple-element.85), channel_id=1, source_target_pairs={{0,2},{1,41},{2,4},{3,43},{4,6},{5,45},{6,0},{7,47},{8,10},{9,49},... | collective-permute-start | bytes 264200 | tf_op jit(solution)/shard_map/ppermute | solution.py:200
  110.7 4.9 %collective-permute-start.20 = (bf16[172,256]{1,0:T(8,128)(2,1)S(1)}, bf16[172,256]{1,0:T(8,128)(2,1)S(1)}, u32[]{:S(2)}, u32[]{:S(2)}) collective-permute-start(bf16[172,256]{1,0:T(8,128)(2,1)S(1)} %get-tuple-element.86), channel_id=1, source_target_pairs={{0,6},{1,121},{2,0},{3,123},{4,2},{5,125},{6,4},{7,127},{8,14},{9,... | collective-permute-start | bytes 264200 | tf_op jit(solution)/shard_map/ppermute | solution.py:200
  115.8 8.4 %collective-permute-start.23 = (bf16[172,256]{1,0:T(8,128)(2,1)S(1)}, bf16[172,256]{1,0:T(8,128)(2,1)S(1)}, u32[]{:S(2)}, u32[]{:S(2)}) collective-permute-start(bf16[172,256]{1,0:T(8,128)(2,1)S(1)} %get-tuple-element.89.own_ref), channel_id=1, source_target_pairs={{0,2},{2,4},{4,6},{6,0},{1,3},{3,5},{5,7},{7,1},{8,10},{10,12},{12... | collective-permute-start | bytes 264200 | tf_op jit(solution)/shard_map/ppermute | solution.py:26
  115.9 8.3 %collective-permute-start.22 = (bf16[172,256]{1,0:T(8,128)(2,1)S(1)}, bf16[172,256]{1,0:T(8,128)(2,1)S(1)}, u32[]{:S(2)}, u32[]{:S(2)}) collective-permute-start(bf16[172,256]{1,0:T(8,128)(2,1)S(1)} %get-tuple-element.89.own_ref), channel_id=1, source_target_pairs={{0,6},{2,0},{4,2},{6,4},{1,7},{3,1},{5,3},{7,5},{8,14},{10,8},{12,... | collective-permute-start | bytes 264200 | tf_op jit(solution)/shard_map/ppermute | solution.py:26
  118.6 5.7 %collective-permute-start.21 = (bf16[172,256]{1,0:T(8,128)(2,1)S(1)}, bf16[172,256]{1,0:T(8,128)(2,1)S(1)}, u32[]{:S(2)}, u32[]{:S(2)}) collective-permute-start(bf16[172,256]{1,0:T(8,128)(2,1)S(1)} %get-tuple-element.89.own_ref), channel_id=1, source_target_pairs={{0,4},{2,6},{4,0},{6,2},{1,5},{3,7},{5,1},{7,3},{8,12},{10,14},{12... | collective-permute-start | bytes 264200 | tf_op jit(solution)/shard_map/ppermute | solution.py:26
  124.3 2.1 %collective-permute-start.26 = (f32[2,86,256]{2,1,0:T(8,128)S(1)}, f32[2,86,256]{2,1,0:T(8,128)S(1)}, u32[]{:S(2)}, u32[]{:S(2)}) collective-permute-start(f32[2,86,256]{2,1,0:T(8,128)S(1)} %get-tuple-element.109), channel_id=1, source_target_pairs={{0,1},{1,0},{2,3},{3,2},{4,5},{5,4},{6,7},{7,6},{8,9},{9,8},{10,11... | collective-permute-start | bytes 528392 | tf_op jit(solution)/shard_map/ppermute | solution.py:311
  125.4 1.8 %collective-permute-start.24 = (bf16[172,256]{1,0:T(8,128)(2,1)S(1)}, bf16[172,256]{1,0:T(8,128)(2,1)S(1)}, u32[]{:S(2)}, u32[]{:S(2)}) collective-permute-start(bf16[172,256]{1,0:T(8,128)(2,1)S(1)} %get-tuple-element.89.own_ref), channel_id=1, source_target_pairs={{0,1},{1,0},{2,3},{3,2},{4,5},{5,4},{6,7},{7,6},{8,9},{9,8},{10,11... | collective-permute-start | bytes 264200 | tf_op jit(solution)/shard_map/ppermute | solution.py:311
  125.5 1.8 %collective-permute-start.25 = (bf16[3,172,256]{2,1,0:T(8,128)(2,1)S(1)}, bf16[3,172,256]{2,1,0:T(8,128)(2,1)S(1)}, u32[]{:S(2)}, u32[]{:S(2)}) collective-permute-start(bf16[3,172,256]{2,1,0:T(8,128)(2,1)S(1)} %pad_maximum_fusion.own_far_ref), channel_id=1, source_target_pairs={{0,1},{1,0},{2,3},{3,2},{4,5},{5,4},{6,7},{7,6},{8,9},{9,8},{10,11... | collective-permute-start | bytes 792584 | tf_op jit(solution)/shard_map/ppermute | solution.py:311
  (16 other events, 54.9 us)
Sparse Core Ops, SparseCore 0:
  36.2 39.4 all-gather.1

commit v5 on v4

--- a/solution.py
+++ b/solution.py
@@ -48,18 +48,18 @@
 
 
 def diagonal_kernel(
-    numbers, at_ref, mine_ref, other_ref, reduced_ref, reduced_other_ref, *refs
+    pairs, at_ref, mine_ref, other_ref, reduced_ref, reduced_other_ref, *refs
 ):
-    outs, (windows, reduced, held, sems) = refs[:-4], refs[-4:]
+    out_ref, windows, reduced, held, sems = refs
     contract = (((0,), (0,)), ((), ()))
     tokens, hidden = mine_ref.shape
     hidden //= 2
     window = held.shape[0]
-    blocks, block, _ = outs[0].shape
+    block = out_ref.shape[1]
     offset = pl.multiple_of(at_ref[CORE] * hidden, 128)
     skips, copies = [], []
-    for i, (n, j) in enumerate((n, j) for n in numbers for j in range(blocks)):
-        first = at_ref[FIRST + blocks * n + j] * block
+    for i, (n, j) in enumerate(pairs):
+        first = at_ref[FIRST + 2 * n + j] * block
         start = pl.multiple_of(jnp.minimum(first // 128 * 128, hidden - window), 128)
         skips.append(pl.multiple_of(first - start, 16))
         copies.append(
@@ -83,20 +83,20 @@
             windows[i], reduced[...], contract, preferred_element_type=jnp.float32
         )
         held[...] = total.astype(held.dtype)
-        outs[i // blocks][i % blocks] = held[pl.ds(skip, block)]
-
-
-def diagonal_grad(numbers, table, mine, other, reduced, reduced_other):
+        out_ref[i] = held[pl.ds(skip, block)]
+
+
+def diagonal_grad(pairs, table, mine, other, reduced, reduced_other):
     tokens, hidden = mine.shape
     columns = reduced.shape[1]
-    out = jax.ShapeDtypeStruct((2, hidden // SIDE**2, columns), jnp.bfloat16)
+    out = jax.ShapeDtypeStruct((len(pairs), hidden // SIDE**2, columns), jnp.bfloat16)
     window = 896
-    count = 2 * len(numbers)
+    count = len(pairs)
     return pl.pallas_call(
-        functools.partial(diagonal_kernel, numbers),
+        functools.partial(diagonal_kernel, pairs),
         in_specs=[SMEM] + [ANY] * 2 + [VMEM] * 2,
-        out_specs=[VMEM] * len(numbers),
-        out_shape=[out] * len(numbers),
+        out_specs=VMEM,
+        out_shape=out,
         scratch_shapes=[
             pltpu.VMEM((count, 2 * tokens, window), jnp.bfloat16),
             pltpu.VMEM((2 * tokens, columns), jnp.bfloat16),
@@ -367,8 +367,12 @@
 
     sums = []
     for number, distance in enumerate(DISTANCES):
-        (part,) = diagonal_grad((number,), table, out_grad, other, reduced, reduced_other)
-        sums.append(exchange(part, distance) if distance else part)
+        pairs = [(number, 0), (number, 1)]
+        arrived = []
+        for some in ([pairs[:1], pairs[1:]] if number == 0 else [pairs]):
+            part = diagonal_grad(some, table, out_grad, other, reduced, reduced_other)
+            arrived.append(exchange(part, distance) if distance else part)
+        sums.append(jnp.concatenate(arrived, axis=0))
     parts = [*here, *near, *far]
     sums[3], parts = lax.optimization_barrier((sums[3], parts))
     projector_all = jnp.concatenate(parts, axis=0)

time: 141 us -> 149 us (1.057)
  waiting for transfers between devices: 33.2 us -> 37.6 us
    ppermute x3 -> x4, waiting for transfers between devices: 8.6 us -> 11.6 us  [exchange(): return lax.ppermute(array, ('y', 'z', 'core'), pairs)]
    unnamed x48 -> x50, local copies, waits for them, and re-layouts: 8.62 us -> 9.97 us
    ppermute x3 -> x4, starting transfers between devices: 5.6 us -> 6.79 us  [exchange(): return lax.ppermute(array, ('y', 'z', 'core'), pairs)]
    pallas_call x4 -> x5, Pallas kernels: 23.8 us -> 24.9 us  [diagonal_grad(): pl.pallas_call(functools.partial(diagonal_kernel, pairs), in_specs=[SMEM]...]
  transfers between devices with their start and end apart: 28 -> 29, of which waited for: 11 -> 12; matrix products, arithmetic and copies ran while one was open for 8% -> 9% of each run, Pallas kernels for 19% -> 19%
where the time goes in v5:
time: 149 us
  Pallas kernels  38.7 us (26%)
  waiting for transfers between devices  37.6 us (25%)
  starting transfers between devices  34.8 us (23%)
  between operations  14.5 us (10%)
  local copies, waits for them, and re-layouts  13.1 us (9%)
  matrix products  6.77 us (5%)
  other arithmetic  3.31 us (2%)
    pallas_call x5, Pallas kernels, diagonal_grad(): pl.pallas_call(functools.partial(diagonal_kernel, pairs), in_specs=[SMEM]...  24.9 us
    ppermute x6, starting transfers between devices, cross(): return lax.ppermute(array, ('y', 'z', 'x', 'core'), pairs)  12.4 us
    ppermute x4, waiting for transfers between devices, exchange(): return lax.ppermute(array, ('y', 'z', 'core'), pairs)  11.6 us
    ppermute x6, waiting for transfers between devices, cross(): return lax.ppermute(array, ('y', 'z', 'x', 'core'), pairs)  11.3 us
    unnamed x50, local copies, waits for them, and re-layouts  9.97 us
    ppermute x7, starting transfers between devices, hop(): lax.ppermute(array, axis, [(i, (i + distance) % SIDE) for i in range(SIDE)])  8.08 us
    ppermute x7, waiting for transfers between devices, hop(): lax.ppermute(array, axis, [(i, (i + distance) % SIDE) for i in range(SIDE)])  8.07 us
    ppermute x11, starting transfers between devices, swap(): return lax.ppermute(array, 'core', SWAP)  7.48 us
  transfers between devices with their start and end apart: 29, of which 12 were waited for; matrix products, arithmetic and copies ran while one was open for 9% of the time, Pallas kernels for 19%

profile of v5, /device:TPU:1, one launch (start us, length us, event | category | flops | bytes accessed | tf_op | source)
XLA Modules:
  0.0 148.9 jit_solution(12888101333650502217)
XLA Ops:
  7.4 1.5 %collective-permute-start = (bf16[640,11008]{1,0:T(8,128)(2,1)}, bf16[640,11008]{1,0:T(8,128)(2,1)}, u32[]{:S(2)}, u32[]{:S(2)}) collective-permute-start(bf16[640,11008]{1,0:T(8,128)(2,1)} %mine_ref.4), channel_id=1, source_target_pairs={{0,1},{1,0},{2,3},{3,2},{4,5},{5,4},{6,7},{7,6},{8,9},{9,8},{10,11... | collective-permute-start | bytes 42270728 | tf_op jit(solution)/shard_map/ppermute | solution.py:311
  11.6 2.2 %constant_dynamic-slice_fusion = (bf16[640,512]{1,0:T(8,128)(2,1)S(1)}, bf16[640,512]{1,0:T(8,128)(2,1)}) fusion(bf16[640,4096]{1,0:T(8,128)(2,1)} %param.6, s32[]{:T(128)S(6)} %select_n.92, s32[]{:T(128)S(6)} %select_n.91), kind=kLoop, calls=%fused_computation.46 | loop fusion | bytes 2621448 | tf_op jit(solution)/shard_map/dynamic_slice | solution.py:329
  13.9 1.9 %fusion.11 = f32[640,512]{1,0:T(8,128)S(1)} fusion(bf16[512,512]{1,0:T(8,128)(2,1)} %param.8, bf16[640,4096]{1,0:T(8,128)(2,1)} %param.6, s32[]{:T(128)S(6)} %select_n.85), kind=kOutput, calls=%fused_computation.13 | convolution fusion | flops 335544320 | bytes 2490372 | tf_op jit(solution)/shard_map/dot_general | solution.py:332
  16.3 1.8 %convolution_add_fusion = f32[640,512]{1,0:T(8,128)S(1)} fusion(f32[640,512]{1,0:T(8,128)S(1)} %fusion.11, bf16[512,512]{1,0:T(8,128)(2,1)S(1)} %collective-permute-done.3, bf16[640,4096]{1,0:T(8,128)(2,1)} %param.6, s32[]{:T(128)S(6)} %select_n.86), kind=kOutput, calls=%fused_computation | convolution fusion | flops 335872000 | bytes 3801092 | tf_op jit(solution)/shard_map/dot_general | solution.py:332
  18.0 5.4 %collective-permute-done.2 = bf16[512,512]{1,0:T(8,128)(2,1)S(1)} collective-permute-done((bf16[512,512]{1,0:T(8,128)(2,1)}, bf16[512,512]{1,0:T(8,128)(2,1)S(1)}, u32[]{:S(2)}, u32[]{:S(2)}) %collective-permute-start.2) | collective-permute-done | bytes 524320 | tf_op jit(solution)/shard_map/ppermute | solution.py:26
  23.5 1.4 collective-permute-start.7
  25.0 2.7 %collective-permute-start.5 = (bf16[256,512]{1,0:T(8,128)(2,1)S(1)}, bf16[256,512]{1,0:T(8,128)(2,1)S(1)}, u32[]{:S(2)}, u32[]{:S(2)}) collective-permute-start(bf16[256,512]{1,0:T(8,128)(2,1)S(1)} %slice.19), channel_id=1, source_target_pairs={{0,6},{2,0},{4,2},{6,4},{1,7},{3,1},{5,3},{7,5},{8,14},{10,8},{12,... | collective-permute-start | bytes 786440 | tf_op jit(solution)/shard_map/ppermute | solution.py:26
  28.7 3.3 %collective-permute-done.6 = bf16[512,512]{1,0:T(8,128)(2,1)S(1)} collective-permute-done((bf16[512,512]{1,0:T(8,128)(2,1)S(1)}, bf16[512,512]{1,0:T(8,128)(2,1)S(1)}, u32[]{:S(2)}, u32[]{:S(2)}) %collective-permute-start.6) | collective-permute-done | bytes 524320 | tf_op jit(solution)/shard_map/ppermute | solution.py:311
  33.4 2.6 %collective-permute-done.4 = bf16[256,512]{1,0:T(8,128)(2,1)S(1)} collective-permute-done((bf16[256,512]{1,0:T(8,128)(2,1)S(1)}, bf16[256,512]{1,0:T(8,128)(2,1)S(1)}, u32[]{:S(2)}, u32[]{:S(2)}) %collective-permute-start.4) | collective-permute-done | bytes 262176 | tf_op jit(solution)/shard_map/ppermute | solution.py:26
  36.1 1.7 %collective-permute-start.8 = (bf16[512,512]{1,0:T(8,128)(2,1)S(1)}, bf16[512,512]{1,0:T(8,128)(2,1)S(1)}, u32[]{:S(2)}, u32[]{:S(2)}) collective-permute-start(bf16[512,512]{1,0:T(8,128)(2,1)S(1)} %constant_dynamic-update-slice_fusion), channel_id=1, source_target_pairs={{0,1},{1,0},{2,3},{3,2},{4,5},{5,4},{6,7},{7,6},{8,9},{9,8},{10,11... | collective-permute-start | bytes 1572872 | tf_op jit(solution)/shard_map/ppermute | solution.py:311
  43.8 3.6 %diagonal_grad.5 = bf16[1,688,512]{2,1,0:T(8,128)(2,1)S(1)} custom-call(s32[30]{0:T(128)S(1)} %stack.153.at_ref, bf16[640,11008]{1,0:T(8,128)(2,1)} %mine_ref.4, bf16[640,11008]{1,0:T(8,128)(2,1)} %collective-permute-done.other_ref, bf16[640,512]{1,0:T(8,128)(2,1)S(1)} %add_convert_fusion.reduced_ref, ...), custom_call_target="tpu_custom_call" | custom-call | flops 1174405120 | bytes 2293760 | tf_op jit(solution)/shard_map/diagonal_grad/pallas_call | solution.py:95
  47.4 3.9 %collective-permute-start.10 = (bf16[1,688,512]{2,1,0:T(8,128)(2,1)S(1)}, bf16[1,688,512]{2,1,0:T(8,128)(2,1)S(1)}, u32[]{:S(2)}, u32[]{:S(2)}) collective-permute-start(bf16[1,688,512]{2,1,0:T(8,128)(2,1)S(1)} %diagonal_grad.5), channel_id=1, source_target_pairs={{0,64},{1,17},{8,72},{9,25},{16,80},{17,1},{24,88},{25,9},{32,96},... | collective-permute-start | bytes 2113544 | tf_op jit(solution)/shard_map/ppermute | solution.py:295
  51.3 6.2 %diagonal_grad.8 = bf16[2,688,512]{2,1,0:T(8,128)(2,1)} custom-call(s32[30]{0:T(128)S(1)} %stack.153.at_ref, bf16[640,11008]{1,0:T(8,128)(2,1)} %mine_ref.4, bf16[640,11008]{1,0:T(8,128)(2,1)} %collective-permute-done.other_ref, bf16[640,512]{1,0:T(8,128)(2,1)S(1)} %add_convert_fusion.reduced_ref, bf16[640,512]{1,0:T(8,128)(2,1)S(1)} %collective-permute-done.9.reduced_other_ref), custom_call_target="tpu_custom_call" | custom-call | flops 2348810240 | bytes 4587520 | tf_op jit(solution)/shard_map/diagonal_grad/pallas_call | solution.py:95
  58.0 6.3 %diagonal_grad.9 = bf16[2,688,512]{2,1,0:T(8,128)(2,1)} custom-call(s32[30]{0:T(128)S(1)} %stack.153.at_ref, bf16[640,11008]{1,0:T(8,128)(2,1)} %mine_ref.4, bf16[640,11008]{1,0:T(8,128)(2,1)} %collective-permute-done.other_ref, bf16[640,512]{1,0:T(8,128)(2,1)S(1)} %add_convert_fusion.reduced_ref, bf16[640,512]{1,0:T(8,128)(2,1)S(1)} %collective-permute-done.9.reduced_other_ref), custom_call_target="tpu_custom_call" | custom-call | flops 2348810240 | bytes 4587520 | tf_op jit(solution)/shard_map/diagonal_grad/pallas_call | solution.py:95
  65.6 3.7 %diagonal_grad.6 = bf16[1,688,512]{2,1,0:T(8,128)(2,1)S(1)} custom-call(s32[30]{0:T(128)S(1)} %stack.153.at_ref, bf16[640,11008]{1,0:T(8,128)(2,1)} %mine_ref.4, bf16[640,11008]{1,0:T(8,128)(2,1)} %collective-permute-done.other_ref, bf16[640,512]{1,0:T(8,128)(2,1)S(1)} %add_convert_fusion.reduced_ref, ...), custom_call_target="tpu_custom_call" | custom-call | flops 1174405120 | bytes 2293760 | tf_op jit(solution)/shard_map/diagonal_grad/pallas_call | solution.py:95
  70.4 5.1 %diagonal_grad.7.refs_3_ = bf16[2,688,512]{2,1,0:T(8,128)(2,1)S(1)} custom-call(s32[30]{0:T(128)S(1)} %stack.153.at_ref, bf16[640,11008]{1,0:T(8,128)(2,1)} %mine_ref.4, bf16[640,11008]{1,0:T(8,128)(2,1)} %collective-permute-done.other_ref, bf16[640,512]{1,0:T(8,128)(2,1)S(1)} %add_convert_fusion.reduced_ref, ...), custom_call_target="tpu_custom_call" | custom-call | flops 2348810240 | bytes 4587520 | tf_op jit(solution)/shard_map/diagonal_grad/pallas_call | solution.py:95
  76.9 2.0 %copy-done.2 = bf16[4096,512]{1,0:T(8,128)(2,1)} copy-done((bf16[4096,512]{1,0:T(8,128)(2,1)}, bf16[4096,512]{1,0:T(8,128)(2,1)S(1)}, u32[]{:S(2)}) %copy-start.2) | copy-done | bytes 4194328
  79.0 11.5 %collective-permute-done.11 = bf16[1,688,512]{2,1,0:T(8,128)(2,1)S(1)} collective-permute-done((bf16[1,688,512]{2,1,0:T(8,128)(2,1)S(1)}, bf16[1,688,512]{2,1,0:T(8,128)(2,1)S(1)}, u32[]{:S(2)}, u32[]{:S(2)}) %collective-permute-start.11) | collective-permute-done | bytes 704544 | tf_op jit(solution)/shard_map/ppermute | solution.py:295
  93.1 2.2 %sum_half.2 = bf16[2,688,256]{2,1,0:T(8,128)(2,1)S(1)} custom-call(s32[30]{0:T(128)S(1)} %stack.153.at_ref, bf16[2,688,512]{2,1,0:T(8,128)(2,1)S(1)} %copy-done, bf16[2,688,512]{2,1,0:T(8,128)(2,1)} %collective-permute-done.13.refs_1_, bf16[2,688,512]{2,1,0:T(8,128)(2,1)} %collective-permute-done.14.refs_2_, bf16[2,688,512]{2,1,0:T(8,128)(2,1)S(1)} %diagonal_grad.7.refs_3_), custom_call_target="tpu_custom_call" | custom-call | tf_op jit(solution)/shard_map/sum_half/pallas_call | solution.py:135
  95.5 2.2 %sum_half.3.refs_0_ = bf16[2,688,256]{2,1,0:T(8,128)(2,1)S(1)} custom-call(s32[30]{0:T(128)S(1)} %stack.153.at_ref, bf16[2,688,512]{2,1,0:T(8,128)(2,1)S(1)} %copy-done, bf16[2,688,512]{2,1,0:T(8,128)(2,1)} %collective-permute-done.13.refs_1_, bf16[2,688,512]{2,1,0:T(8,128)(2,1)} %collective-permute-done.14.refs_2_, ...), custom_call_target="tpu_custom_call" | custom-call | tf_op jit(solution)/shard_map/sum_half/pallas_call | solution.py:135
  99.1 2.3 %collective-permute-start.18 = (bf16[4,172,256]{2,1,0:T(8,128)(2,1)S(1)}, bf16[4,172,256]{2,1,0:T(8,128)(2,1)S(1)}, u32[]{:S(2)}, u32[]{:S(2)}) collective-permute-start(bf16[4,172,256]{2,1,0:T(8,128)(2,1)S(1)} %get-tuple-element.82), channel_id=1, source_target_pairs={{0,120},{1,7},{2,122},{3,1},{4,124},{5,3},{6,126},{7,5},{8,96},{9,... | collective-permute-start | bytes 1056776 | tf_op jit(solution)/shard_map/ppermute | solution.py:200
  101.4 5.4 %collective-permute-done.16.refs_1_ = bf16[4,172,256]{2,1,0:T(8,128)(2,1)S(1)} collective-permute-done((bf16[4,172,256]{2,1,0:T(8,128)(2,1)S(1)}, bf16[4,172,256]{2,1,0:T(8,128)(2,1)S(1)}, u32[]{:S(2)}, u32[]{:S(2)}) %collective-permute-start.16) | collective-permute-done | bytes 352288 | tf_op jit(solution)/shard_map/ppermute | solution.py:200
  106.7 3.4 %collective-permute-done.17.refs_2_ = bf16[4,172,256]{2,1,0:T(8,128)(2,1)S(1)} collective-permute-done((bf16[4,172,256]{2,1,0:T(8,128)(2,1)S(1)}, bf16[4,172,256]{2,1,0:T(8,128)(2,1)S(1)}, u32[]{:S(2)}, u32[]{:S(2)}) %collective-permute-start.17) | collective-permute-done | bytes 352288 | tf_op jit(solution)/shard_map/ppermute | solution.py:200
  110.8 4.8 %collective-permute-start.19 = (bf16[172,256]{1,0:T(8,128)(2,1)S(1)}, bf16[172,256]{1,0:T(8,128)(2,1)S(1)}, u32[]{:S(2)}, u32[]{:S(2)}) collective-permute-start(bf16[172,256]{1,0:T(8,128)(2,1)S(1)} %get-tuple-element.84), channel_id=1, source_target_pairs={{0,4},{1,81},{2,6},{3,83},{4,0},{5,85},{6,2},{7,87},{8,12},{9,89},... | collective-permute-start | bytes 264200 | tf_op jit(solution)/shard_map/ppermute | solution.py:200
  115.6 2.8 %collective-permute-start.20 = (bf16[172,256]{1,0:T(8,128)(2,1)S(1)}, bf16[172,256]{1,0:T(8,128)(2,1)S(1)}, u32[]{:S(2)}, u32[]{:S(2)}) collective-permute-start(bf16[172,256]{1,0:T(8,128)(2,1)S(1)} %get-tuple-element.85), channel_id=1, source_target_pairs={{0,2},{1,41},{2,4},{3,43},{4,6},{5,45},{6,0},{7,47},{8,10},{9,49},... | collective-permute-start | bytes 264200 | tf_op jit(solution)/shard_map/ppermute | solution.py:200
  118.4 2.0 %collective-permute-start.21 = (bf16[172,256]{1,0:T(8,128)(2,1)S(1)}, bf16[172,256]{1,0:T(8,128)(2,1)S(1)}, u32[]{:S(2)}, u32[]{:S(2)}) collective-permute-start(bf16[172,256]{1,0:T(8,128)(2,1)S(1)} %get-tuple-element.86), channel_id=1, source_target_pairs={{0,6},{1,121},{2,0},{3,123},{4,2},{5,125},{6,4},{7,127},{8,14},{9,... | collective-permute-start | bytes 264200 | tf_op jit(solution)/shard_map/ppermute | solution.py:200
  120.4 1.9 %collective-permute-done.20 = bf16[172,256]{1,0:T(8,128)(2,1)S(1)} collective-permute-done((bf16[172,256]{1,0:T(8,128)(2,1)S(1)}, bf16[172,256]{1,0:T(8,128)(2,1)S(1)}, u32[]{:S(2)}, u32[]{:S(2)}) %collective-permute-start.20) | collective-permute-done | bytes 88096 | tf_op jit(solution)/shard_map/ppermute | solution.py:200
  123.2 2.7 %collective-permute-start.23 = (bf16[172,256]{1,0:T(8,128)(2,1)S(1)}, bf16[172,256]{1,0:T(8,128)(2,1)S(1)}, u32[]{:S(2)}, u32[]{:S(2)}) collective-permute-start(bf16[172,256]{1,0:T(8,128)(2,1)S(1)} %get-tuple-element.89.own_ref), channel_id=1, source_target_pairs={{0,6},{2,0},{4,2},{6,4},{1,7},{3,1},{5,3},{7,5},{8,14},{10,8},{12,... | collective-permute-start | bytes 264200 | tf_op jit(solution)/shard_map/ppermute | solution.py:26
  125.9 2.6 %copy-done.1 = bf16[4096,688]{0,1:T(8,128)(2,1)S(1)} copy-done((bf16[4096,688]{0,1:T(8,128)(2,1)S(1)}, bf16[4096,688]{0,1:T(8,128)(2,1)}, u32[]{:S(2)}) %copy-start.1) | copy-done | bytes 5636120
  128.5 2.2 %copy-done.3 = bf16[4096,512]{1,0:T(8,128)(2,1)S(1)} copy-done((bf16[4096,512]{1,0:T(8,128)(2,1)S(1)}, bf16[4096,512]{1,0:T(8,128)(2,1)}, u32[]{:S(2)}) %copy-start.3) | copy-done | bytes 4194328
  131.7 1.5 %collective-permute-start.27 = (f32[2,86,256]{2,1,0:T(8,128)S(1)}, f32[2,86,256]{2,1,0:T(8,128)S(1)}, u32[]{:S(2)}, u32[]{:S(2)}) collective-permute-start(f32[2,86,256]{2,1,0:T(8,128)S(1)} %get-tuple-element.109), channel_id=1, source_target_pairs={{0,1},{1,0},{2,3},{3,2},{4,5},{5,4},{6,7},{7,6},{8,9},{9,8},{10,11... | collective-permute-start | bytes 528392 | tf_op jit(solution)/shard_map/ppermute | solution.py:311
  135.1 6.9 %update.1 = bf16[688,4096]{1,0:T(8,128)(2,1)} custom-call(s32[30]{0:T(128)S(1)} %stack.153.at_ref, bf16[172,256]{1,0:T(8,128)(2,1)S(1)} %get-tuple-element.89.own_ref, bf16[3,172,256]{2,1,0:T(8,128)(2,1)S(1)} %pad_maximum_fusion.1.own_far_ref, bf16[172,256]{1,0:T(8,128)(2,1)S(1)} %collective-permute-done.25.other_ref, ...), custom_call_target="tpu_custom_call" | custom-call | tf_op jit(solution)/shard_map/update/pallas_call | solution.py:271
  (110 shorter events, 24.6 us)
Async XLA Ops:
  7.2 84.6 %all-gather.2.cloned.1.call-start = ((), (), s32[]{:S(2)}) async-start(), calls=%async_computation | async-start | bytes 6340608 | tf_op jit(solution)/shard_map/all_gather | solution.py:366
  7.4 36.4 %collective-permute-start = (bf16[640,11008]{1,0:T(8,128)(2,1)}, bf16[640,11008]{1,0:T(8,128)(2,1)}, u32[]{:S(2)}, u32[]{:S(2)}) collective-permute-start(bf16[640,11008]{1,0:T(8,128)(2,1)} %mine_ref.4), channel_id=1, source_target_pairs={{0,1},{1,0},{2,3},{3,2},{4,5},{5,4},{6,7},{7,6},{8,9},{9,8},{10,11... | collective-permute-start | bytes 42270728 | tf_op jit(solution)/shard_map/ppermute | solution.py:311
  8.9 7.4 %collective-permute-start.3 = (bf16[512,512]{1,0:T(8,128)(2,1)}, bf16[512,512]{1,0:T(8,128)(2,1)S(1)}, u32[]{:S(2)}, u32[]{:S(2)}) collective-permute-start(bf16[512,512]{1,0:T(8,128)(2,1)} %param.8), channel_id=1, source_target_pairs={{0,1},{1,0},{2,3},{3,2},{4,5},{5,4},{6,7},{7,6},{8,9},{9,8},{10,11... | collective-permute-start | bytes 1572872 | tf_op jit(solution)/shard_map/ppermute | solution.py:311
  9.0 14.5 %collective-permute-start.2 = (bf16[512,512]{1,0:T(8,128)(2,1)}, bf16[512,512]{1,0:T(8,128)(2,1)S(1)}, u32[]{:S(2)}, u32[]{:S(2)}) collective-permute-start(bf16[512,512]{1,0:T(8,128)(2,1)} %param.8), channel_id=1, source_target_pairs={{0,2},{2,4},{4,6},{6,0},{1,3},{3,5},{5,7},{7,1},{8,10},{10,12},{12... | collective-permute-start | bytes 1572872 | tf_op jit(solution)/shard_map/ppermute | solution.py:26
  10.3 13.2 %collective-permute-start.1 = (bf16[512,512]{1,0:T(8,128)(2,1)}, bf16[512,512]{1,0:T(8,128)(2,1)S(1)}, u32[]{:S(2)}, u32[]{:S(2)}) collective-permute-start(bf16[512,512]{1,0:T(8,128)(2,1)} %param.8), channel_id=1, source_target_pairs={{0,6},{2,0},{4,2},{6,4},{1,7},{3,1},{5,3},{7,5},{8,14},{10,8},{12,... | collective-permute-start | bytes 1572872 | tf_op jit(solution)/shard_map/ppermute | solution.py:26
  13.9 13.8 %copy-start.4 = (bf16[640,4096]{1,0:T(8,128)(2,1)S(1)}, bf16[640,4096]{1,0:T(8,128)(2,1)}, u32[]{:S(2)}) copy-start(bf16[640,4096]{1,0:T(8,128)(2,1)} %param.6) | copy-start | bytes 15728644
  16.3 12.5 %copy-start.13 = (bf16[512,512]{1,0:T(8,128)(2,1)}, bf16[512,512]{1,0:T(8,128)(2,1)S(1)}, u32[]{:S(2)}) copy-start(bf16[512,512]{1,0:T(8,128)(2,1)S(1)} %collective-permute-done.3) | copy-start | bytes 1572868
  23.5 9.3 %collective-permute-start.7 = (bf16[512,512]{1,0:T(8,128)(2,1)S(1)}, bf16[512,512]{1,0:T(8,128)(2,1)S(1)}, u32[]{:S(2)}, u32[]{:S(2)}) collective-permute-start(bf16[512,512]{1,0:T(8,128)(2,1)S(1)} %collective-permute-done.2), channel_id=1, source_target_pairs={{0,1},{1,0},{2,3},{3,2},{4,5},{5,4},{6,7},{7,6},{8,9},{9,8},{10,11... | collective-permute-start | bytes 1572872 | tf_op jit(solution)/shard_map/ppermute | solution.py:311
  24.9 7.1 %collective-permute-start.6 = (bf16[512,512]{1,0:T(8,128)(2,1)S(1)}, bf16[512,512]{1,0:T(8,128)(2,1)S(1)}, u32[]{:S(2)}, u32[]{:S(2)}) collective-permute-start(bf16[512,512]{1,0:T(8,128)(2,1)S(1)} %collective-permute-done.1), channel_id=1, source_target_pairs={{0,1},{1,0},{2,3},{3,2},{4,5},{5,4},{6,7},{7,6},{8,9},{9,8},{10,11... | collective-permute-start | bytes 1572872 | tf_op jit(solution)/shard_map/ppermute | solution.py:311
  25.0 8.4 %collective-permute-start.5 = (bf16[256,512]{1,0:T(8,128)(2,1)S(1)}, bf16[256,512]{1,0:T(8,128)(2,1)S(1)}, u32[]{:S(2)}, u32[]{:S(2)}) collective-permute-start(bf16[256,512]{1,0:T(8,128)(2,1)S(1)} %slice.19), channel_id=1, source_target_pairs={{0,6},{2,0},{4,2},{6,4},{1,7},{3,1},{5,3},{7,5},{8,14},{10,8},{12,... | collective-permute-start | bytes 786440 | tf_op jit(solution)/shard_map/ppermute | solution.py:26
  27.7 8.3 %collective-permute-start.4 = (bf16[256,512]{1,0:T(8,128)(2,1)S(1)}, bf16[256,512]{1,0:T(8,128)(2,1)S(1)}, u32[]{:S(2)}, u32[]{:S(2)}) collective-permute-start(bf16[256,512]{1,0:T(8,128)(2,1)S(1)} %slice.18), channel_id=1, source_target_pairs={{0,2},{2,4},{4,6},{6,0},{1,3},{3,5},{5,7},{7,1},{8,10},{10,12},{12... | collective-permute-start | bytes 786440 | tf_op jit(solution)/shard_map/ppermute | solution.py:26
  36.1 3.2 %collective-permute-start.8 = (bf16[512,512]{1,0:T(8,128)(2,1)S(1)}, bf16[512,512]{1,0:T(8,128)(2,1)S(1)}, u32[]{:S(2)}, u32[]{:S(2)}) collective-permute-start(bf16[512,512]{1,0:T(8,128)(2,1)S(1)} %constant_dynamic-update-slice_fusion), channel_id=1, source_target_pairs={{0,1},{1,0},{2,3},{3,2},{4,5},{5,4},{6,7},{7,6},{8,9},{9,8},{10,11... | collective-permute-start | bytes 1572872 | tf_op jit(solution)/shard_map/ppermute | solution.py:311
  40.1 3.6 %collective-permute-start.9 = (bf16[640,512]{1,0:T(8,128)(2,1)S(1)}, bf16[640,512]{1,0:T(8,128)(2,1)S(1)}, u32[]{:S(2)}, u32[]{:S(2)}) collective-permute-start(bf16[640,512]{1,0:T(8,128)(2,1)S(1)} %add_convert_fusion.reduced_ref), channel_id=1, source_target_pairs={{0,1},{1,0},{2,3},{3,2},{4,5},{5,4},{6,7},{7,6},{8,9},{9,8},{10,11... | collective-permute-start | bytes 1966088 | tf_op jit(solution)/shard_map/ppermute | solution.py:311
  41.5 1.5 %collective-permute-start.12 = (f32[2,86,256]{2,1,0:T(8,128)S(1)}, f32[2,86,256]{2,1,0:T(8,128)S(1)}, u32[]{:S(2)}, u32[]{:S(2)}) collective-permute-start(f32[2,86,256]{2,1,0:T(8,128)S(1)} %get-tuple-element.111), channel_id=1, source_target_pairs={{0,1},{1,0},{2,3},{3,2},{4,5},{5,4},{6,7},{7,6},{8,9},{9,8},{10,11... | collective-permute-start | bytes 528392 | tf_op jit(solution)/shard_map/ppermute | solution.py:311
  47.4 31.6 %collective-permute-start.10 = (bf16[1,688,512]{2,1,0:T(8,128)(2,1)S(1)}, bf16[1,688,512]{2,1,0:T(8,128)(2,1)S(1)}, u32[]{:S(2)}, u32[]{:S(2)}) collective-permute-start(bf16[1,688,512]{2,1,0:T(8,128)(2,1)S(1)} %diagonal_grad.5), channel_id=1, source_target_pairs={{0,64},{1,17},{8,72},{9,25},{16,80},{17,1},{24,88},{25,9},{32,96},... | collective-permute-start | bytes 2113544 | tf_op jit(solution)/shard_map/ppermute | solution.py:295
  57.4 34.3 %collective-permute-start.13 = (bf16[2,688,512]{2,1,0:T(8,128)(2,1)}, bf16[2,688,512]{2,1,0:T(8,128)(2,1)}, u32[]{:S(2)}, u32[]{:S(2)}) collective-permute-start(bf16[2,688,512]{2,1,0:T(8,128)(2,1)} %diagonal_grad.8), channel_id=1, source_target_pairs={{0,32},{1,25},{8,40},{9,1},{16,48},{17,9},{24,56},{25,17},{32,64},... | collective-permute-start | bytes 4227080 | tf_op jit(solution)/shard_map/ppermute | solution.py:295
  64.4 27.4 %collective-permute-start.14 = (bf16[2,688,512]{2,1,0:T(8,128)(2,1)}, bf16[2,688,512]{2,1,0:T(8,128)(2,1)}, u32[]{:S(2)}, u32[]{:S(2)}) collective-permute-start(bf16[2,688,512]{2,1,0:T(8,128)(2,1)} %diagonal_grad.9), channel_id=1, source_target_pairs={{0,96},{1,9},{8,104},{9,17},{16,112},{17,25},{24,120},{25,1},{32,0... | collective-permute-start | bytes 4227080 | tf_op jit(solution)/shard_map/ppermute | solution.py:295
  69.3 21.2 %collective-permute-start.11 = (bf16[1,688,512]{2,1,0:T(8,128)(2,1)S(1)}, bf16[1,688,512]{2,1,0:T(8,128)(2,1)S(1)}, u32[]{:S(2)}, u32[]{:S(2)}) collective-permute-start(bf16[1,688,512]{2,1,0:T(8,128)(2,1)S(1)} %diagonal_grad.6), channel_id=1, source_target_pairs={{0,64},{1,17},{8,72},{9,25},{16,80},{17,1},{24,88},{25,9},{32,96},... | collective-permute-start | bytes 2113544 | tf_op jit(solution)/shard_map/ppermute | solution.py:295
  95.4 27.6 %copy-start.19 = (f32[2,172,256]{2,1,0:T(8,128)S(1)}, f32[2,172,256]{2,1,0:T(8,128)}, u32[]{:S(2)}) copy-start(f32[2,172,256]{2,1,0:T(8,128)} %maximum_select_fusion) | copy-start | bytes 1056772
  95.4 2.3 %collective-permute-start.15 = (bf16[2,688,256]{2,1,0:T(8,128)(2,1)S(1)}, bf16[2,688,256]{2,1,0:T(8,128)(2,1)S(1)}, u32[]{:S(2)}, u32[]{:S(2)}) collective-permute-start(bf16[2,688,256]{2,1,0:T(8,128)(2,1)S(1)} %sum_half.2), channel_id=1, source_target_pairs={{0,1},{1,0},{2,3},{3,2},{4,5},{5,4},{6,7},{7,6},{8,9},{9,8},{10,11... | collective-permute-start | bytes 2113544 | tf_op jit(solution)/shard_map/ppermute | solution.py:311
  98.5 8.2 %collective-permute-start.16 = (bf16[4,172,256]{2,1,0:T(8,128)(2,1)S(1)}, bf16[4,172,256]{2,1,0:T(8,128)(2,1)S(1)}, u32[]{:S(2)}, u32[]{:S(2)}) collective-permute-start(bf16[4,172,256]{2,1,0:T(8,128)(2,1)S(1)} %get-tuple-element.80), channel_id=1, source_target_pairs={{0,80},{1,5},{2,82},{3,7},{4,84},{5,1},{6,86},{7,3},{8,88},{9,13},... | collective-permute-start | bytes 1056776 | tf_op jit(solution)/shard_map/ppermute | solution.py:200
  98.6 11.5 %collective-permute-start.17 = (bf16[4,172,256]{2,1,0:T(8,128)(2,1)S(1)}, bf16[4,172,256]{2,1,0:T(8,128)(2,1)S(1)}, u32[]{:S(2)}, u32[]{:S(2)}) collective-permute-start(bf16[4,172,256]{2,1,0:T(8,128)(2,1)S(1)} %get-tuple-element.81), channel_id=1, source_target_pairs={{0,40},{1,3},{2,42},{3,5},{4,44},{5,7},{6,46},{7,1},{8,48},{9,11},... | collective-permute-start | bytes 1056776 | tf_op jit(solution)/shard_map/ppermute | solution.py:200
  99.1 11.0 %collective-permute-start.18 = (bf16[4,172,256]{2,1,0:T(8,128)(2,1)S(1)}, bf16[4,172,256]{2,1,0:T(8,128)(2,1)S(1)}, u32[]{:S(2)}, u32[]{:S(2)}) collective-permute-start(bf16[4,172,256]{2,1,0:T(8,128)(2,1)S(1)} %get-tuple-element.82), channel_id=1, source_target_pairs={{0,120},{1,7},{2,122},{3,1},{4,124},{5,3},{6,126},{7,5},{8,96},{9,... | collective-permute-start | bytes 1056776 | tf_op jit(solution)/shard_map/ppermute | solution.py:200
  110.8 9.6 %collective-permute-start.19 = (bf16[172,256]{1,0:T(8,128)(2,1)S(1)}, bf16[172,256]{1,0:T(8,128)(2,1)S(1)}, u32[]{:S(2)}, u32[]{:S(2)}) collective-permute-start(bf16[172,256]{1,0:T(8,128)(2,1)S(1)} %get-tuple-element.84), channel_id=1, source_target_pairs={{0,4},{1,81},{2,6},{3,83},{4,0},{5,85},{6,2},{7,87},{8,12},{9,89},... | collective-permute-start | bytes 264200 | tf_op jit(solution)/shard_map/ppermute | solution.py:200
  115.6 6.7 %collective-permute-start.20 = (bf16[172,256]{1,0:T(8,128)(2,1)S(1)}, bf16[172,256]{1,0:T(8,128)(2,1)S(1)}, u32[]{:S(2)}, u32[]{:S(2)}) collective-permute-start(bf16[172,256]{1,0:T(8,128)(2,1)S(1)} %get-tuple-element.85), channel_id=1, source_target_pairs={{0,2},{1,41},{2,4},{3,43},{4,6},{5,45},{6,0},{7,47},{8,10},{9,49},... | collective-permute-start | bytes 264200 | tf_op jit(solution)/shard_map/ppermute | solution.py:200
  118.4 4.5 %collective-permute-start.21 = (bf16[172,256]{1,0:T(8,128)(2,1)S(1)}, bf16[172,256]{1,0:T(8,128)(2,1)S(1)}, u32[]{:S(2)}, u32[]{:S(2)}) collective-permute-start(bf16[172,256]{1,0:T(8,128)(2,1)S(1)} %get-tuple-element.86), channel_id=1, source_target_pairs={{0,6},{1,121},{2,0},{3,123},{4,2},{5,125},{6,4},{7,127},{8,14},{9,... | collective-permute-start | bytes 264200 | tf_op jit(solution)/shard_map/ppermute | solution.py:200
  123.2 8.4 %collective-permute-start.24 = (bf16[172,256]{1,0:T(8,128)(2,1)S(1)}, bf16[172,256]{1,0:T(8,128)(2,1)S(1)}, u32[]{:S(2)}, u32[]{:S(2)}) collective-permute-start(bf16[172,256]{1,0:T(8,128)(2,1)S(1)} %get-tuple-element.89.own_ref), channel_id=1, source_target_pairs={{0,2},{2,4},{4,6},{6,0},{1,3},{3,5},{5,7},{7,1},{8,10},{10,12},{12... | collective-permute-start | bytes 264200 | tf_op jit(solution)/shard_map/ppermute | solution.py:26
  123.2 8.3 %collective-permute-start.23 = (bf16[172,256]{1,0:T(8,128)(2,1)S(1)}, bf16[172,256]{1,0:T(8,128)(2,1)S(1)}, u32[]{:S(2)}, u32[]{:S(2)}) collective-permute-start(bf16[172,256]{1,0:T(8,128)(2,1)S(1)} %get-tuple-element.89.own_ref), channel_id=1, source_target_pairs={{0,6},{2,0},{4,2},{6,4},{1,7},{3,1},{5,3},{7,5},{8,14},{10,8},{12,... | collective-permute-start | bytes 264200 | tf_op jit(solution)/shard_map/ppermute | solution.py:26
  125.9 5.7 %collective-permute-start.22 = (bf16[172,256]{1,0:T(8,128)(2,1)S(1)}, bf16[172,256]{1,0:T(8,128)(2,1)S(1)}, u32[]{:S(2)}, u32[]{:S(2)}) collective-permute-start(bf16[172,256]{1,0:T(8,128)(2,1)S(1)} %get-tuple-element.89.own_ref), channel_id=1, source_target_pairs={{0,4},{2,6},{4,0},{6,2},{1,5},{3,7},{5,1},{7,3},{8,12},{10,14},{12... | collective-permute-start | bytes 264200 | tf_op jit(solution)/shard_map/ppermute | solution.py:26
  131.7 2.6 %collective-permute-start.27 = (f32[2,86,256]{2,1,0:T(8,128)S(1)}, f32[2,86,256]{2,1,0:T(8,128)S(1)}, u32[]{:S(2)}, u32[]{:S(2)}) collective-permute-start(f32[2,86,256]{2,1,0:T(8,128)S(1)} %get-tuple-element.109), channel_id=1, source_target_pairs={{0,1},{1,0},{2,3},{3,2},{4,5},{5,4},{6,7},{7,6},{8,9},{9,8},{10,11... | collective-permute-start | bytes 528392 | tf_op jit(solution)/shard_map/ppermute | solution.py:311
  133.2 1.8 %collective-permute-start.25 = (bf16[172,256]{1,0:T(8,128)(2,1)S(1)}, bf16[172,256]{1,0:T(8,128)(2,1)S(1)}, u32[]{:S(2)}, u32[]{:S(2)}) collective-permute-start(bf16[172,256]{1,0:T(8,128)(2,1)S(1)} %get-tuple-element.89.own_ref), channel_id=1, source_target_pairs={{0,1},{1,0},{2,3},{3,2},{4,5},{5,4},{6,7},{7,6},{8,9},{9,8},{10,11... | collective-permute-start | bytes 264200 | tf_op jit(solution)/shard_map/ppermute | solution.py:311
  133.3 1.8 %collective-permute-start.26 = (bf16[3,172,256]{2,1,0:T(8,128)(2,1)S(1)}, bf16[3,172,256]{2,1,0:T(8,128)(2,1)S(1)}, u32[]{:S(2)}, u32[]{:S(2)}) collective-permute-start(bf16[3,172,256]{2,1,0:T(8,128)(2,1)S(1)} %pad_maximum_fusion.1.own_far_ref), channel_id=1, source_target_pairs={{0,1},{1,0},{2,3},{3,2},{4,5},{5,4},{6,7},{7,6},{8,9},{9,8},{10,11... | collective-permute-start | bytes 792584 | tf_op jit(solution)/shard_map/ppermute | solution.py:311
  (18 other events, 69.5 us)
Sparse Core Ops, SparseCore 0:
  36.2 39.4 all-gather.1

commit v6 on v4

--- a/solution.py
+++ b/solution.py
@@ -122,20 +122,20 @@
 
 def half_kernel(at_ref, *refs):
     parts, out = refs[:4], refs[4]
-    for j in range(out.shape[0]):
-        out[j] = total_of(parts, j).astype(out.dtype)
+    out[...] = total_of(parts, Ellipsis).astype(out.dtype)
 
 
 def sum_half(table, parts, mine):
     blocks, block, columns = parts[0].shape
     half = pl.BlockSpec(
-        (blocks, block, columns // 2),
-        (lambda i, at: (0, 0, at[CORE])) if mine else (lambda i, at: (0, 0, 1 - at[CORE])),
-    )
+        (1, block, columns // 2),
+        (lambda i, at: (i, 0, at[CORE])) if mine else (lambda i, at: (i, 0, 1 - at[CORE])),
+    )
+    out = pl.BlockSpec((1, block, columns // 2), lambda i, at: (i, 0, 0))
     return pl.pallas_call(
         half_kernel,
         grid_spec=pltpu.PrefetchScalarGridSpec(
-            num_scalar_prefetch=1, grid=(1,), in_specs=[half] * len(parts), out_specs=VMEM
+            num_scalar_prefetch=1, grid=(blocks,), in_specs=[half] * len(parts), out_specs=out
         ),
         out_shape=jax.ShapeDtypeStruct((blocks, block, columns // 2), jnp.bfloat16),
         compiler_params=pltpu.CompilerParams(vmem_limit_bytes=20 << 20),

time: 141 us -> 141 us (level)
  no operation moved by 1% of the time
where the time goes in v6:
time: 141 us
  Pallas kernels  37.6 us (27%)
  starting transfers between devices  34.9 us (25%)
  waiting for transfers between devices  33.2 us (24%)
  between operations  14.5 us (10%)
  local copies, waits for them, and re-layouts  11.8 us (8%)
  matrix products  6.78 us (5%)
  other arithmetic  2.04 us (1%)
    pallas_call x4, Pallas kernels, diagonal_grad(): pl.pallas_call(functools.partial(diagonal_kernel, numbers), in_specs=[SME...  23.8 us
    ppermute x6, starting transfers between devices, cross(): return lax.ppermute(array, ('y', 'z', 'x', 'core'), pairs)  13.7 us
    ppermute x6, waiting for transfers between devices, cross(): return lax.ppermute(array, ('y', 'z', 'x', 'core'), pairs)  10.6 us
    unnamed x48, local copies, waits for them, and re-layouts  8.62 us
    ppermute x3, waiting for transfers between devices, exchange(): return lax.ppermute(array, ('y', 'z', 'core'), pairs)  8.6 us
    ppermute x7, starting transfers between devices, hop(): lax.ppermute(array, axis, [(i, (i + distance) % SIDE) for i in range(SIDE)])  8.08 us
    ppermute x7, waiting for transfers between devices, hop(): lax.ppermute(array, axis, [(i, (i + distance) % SIDE) for i in range(SIDE)])  8.06 us
    ppermute x11, starting transfers between devices, swap(): return lax.ppermute(array, 'core', SWAP)  7.43 us
  transfers between devices with their start and end apart: 28, of which 11 were waited for; matrix products, arithmetic and copies ran while one was open for 8% of the time, Pallas kernels for 19%

profile of v6, /device:TPU:1, one launch (start us, length us, event | category | flops | bytes accessed | tf_op | source)
XLA Modules:
  0.0 140.8 jit_solution(8919533716438621086)
XLA Ops:
  7.4 1.5 %collective-permute-start = (bf16[640,11008]{1,0:T(8,128)(2,1)}, bf16[640,11008]{1,0:T(8,128)(2,1)}, u32[]{:S(2)}, u32[]{:S(2)}) collective-permute-start(bf16[640,11008]{1,0:T(8,128)(2,1)} %mine_ref.3), channel_id=1, source_target_pairs={{0,1},{1,0},{2,3},{3,2},{4,5},{5,4},{6,7},{7,6},{8,9},{9,8},{10,11... | collective-permute-start | bytes 42270728 | tf_op jit(solution)/shard_map/ppermute | solution.py:311
  9.0 1.3 collective-permute-start.2
  10.3 1.4 collective-permute-start.1
  11.6 2.2 %constant_dynamic-slice_fusion = (bf16[640,512]{1,0:T(8,128)(2,1)S(1)}, bf16[640,512]{1,0:T(8,128)(2,1)}) fusion(bf16[640,4096]{1,0:T(8,128)(2,1)} %param.6, s32[]{:T(128)S(6)} %select_n.92, s32[]{:T(128)S(6)} %select_n.91), kind=kLoop, calls=%fused_computation.45 | loop fusion | bytes 2621448 | tf_op jit(solution)/shard_map/dynamic_slice | solution.py:329
  13.9 1.9 %fusion.11 = f32[640,512]{1,0:T(8,128)S(1)} fusion(bf16[512,512]{1,0:T(8,128)(2,1)} %param.8, bf16[640,4096]{1,0:T(8,128)(2,1)} %param.6, s32[]{:T(128)S(6)} %select_n.85), kind=kOutput, calls=%fused_computation.12 | convolution fusion | flops 335544320 | bytes 2490372 | tf_op jit(solution)/shard_map/dot_general | solution.py:332
  16.3 1.8 %convolution_add_fusion = f32[640,512]{1,0:T(8,128)S(1)} fusion(f32[640,512]{1,0:T(8,128)S(1)} %fusion.11, bf16[512,512]{1,0:T(8,128)(2,1)S(1)} %collective-permute-done.3, bf16[640,4096]{1,0:T(8,128)(2,1)} %param.6, s32[]{:T(128)S(6)} %select_n.86), kind=kOutput, calls=%fused_computation | convolution fusion | flops 335872000 | bytes 3801092 | tf_op jit(solution)/shard_map/dot_general | solution.py:332
  18.0 5.4 %collective-permute-done.2 = bf16[512,512]{1,0:T(8,128)(2,1)S(1)} collective-permute-done((bf16[512,512]{1,0:T(8,128)(2,1)}, bf16[512,512]{1,0:T(8,128)(2,1)S(1)}, u32[]{:S(2)}, u32[]{:S(2)}) %collective-permute-start.2) | collective-permute-done | bytes 524320 | tf_op jit(solution)/shard_map/ppermute | solution.py:26
  23.5 1.4 collective-permute-start.7
  25.0 2.7 %collective-permute-start.5 = (bf16[256,512]{1,0:T(8,128)(2,1)S(1)}, bf16[256,512]{1,0:T(8,128)(2,1)S(1)}, u32[]{:S(2)}, u32[]{:S(2)}) collective-permute-start(bf16[256,512]{1,0:T(8,128)(2,1)S(1)} %slice.19), channel_id=1, source_target_pairs={{0,6},{2,0},{4,2},{6,4},{1,7},{3,1},{5,3},{7,5},{8,14},{10,8},{12,... | collective-permute-start | bytes 786440 | tf_op jit(solution)/shard_map/ppermute | solution.py:26
  28.7 3.3 %collective-permute-done.6 = bf16[512,512]{1,0:T(8,128)(2,1)S(1)} collective-permute-done((bf16[512,512]{1,0:T(8,128)(2,1)S(1)}, bf16[512,512]{1,0:T(8,128)(2,1)S(1)}, u32[]{:S(2)}, u32[]{:S(2)}) %collective-permute-start.6) | collective-permute-done | bytes 524320 | tf_op jit(solution)/shard_map/ppermute | solution.py:311
  33.4 2.6 %collective-permute-done.4 = bf16[256,512]{1,0:T(8,128)(2,1)S(1)} collective-permute-done((bf16[256,512]{1,0:T(8,128)(2,1)S(1)}, bf16[256,512]{1,0:T(8,128)(2,1)S(1)}, u32[]{:S(2)}, u32[]{:S(2)}) %collective-permute-start.4) | collective-permute-done | bytes 262176 | tf_op jit(solution)/shard_map/ppermute | solution.py:26
  36.1 1.7 %collective-permute-start.8 = (bf16[512,512]{1,0:T(8,128)(2,1)S(1)}, bf16[512,512]{1,0:T(8,128)(2,1)S(1)}, u32[]{:S(2)}, u32[]{:S(2)}) collective-permute-start(bf16[512,512]{1,0:T(8,128)(2,1)S(1)} %constant_dynamic-update-slice_fusion), channel_id=1, source_target_pairs={{0,1},{1,0},{2,3},{3,2},{4,5},{5,4},{6,7},{7,6},{8,9},{9,8},{10,11... | collective-permute-start | bytes 1572872 | tf_op jit(solution)/shard_map/ppermute | solution.py:311
  42.2 6.2 %diagonal_grad.4 = bf16[2,688,512]{2,1,0:T(8,128)(2,1)} custom-call(s32[30]{0:T(128)S(1)} %stack.153.at_ref, bf16[640,11008]{1,0:T(8,128)(2,1)} %mine_ref.3, bf16[640,11008]{1,0:T(8,128)(2,1)} %collective-permute-done.other_ref, bf16[640,512]{1,0:T(8,128)(2,1)S(1)} %add_convert_fusion.reduced_ref, bf16[640,512]{1,0:T(8,128)(2,1)S(1)} %collective-permute-done.9.reduced_other_ref), custom_call_target="tpu_custom_call" | custom-call | flops 2348810240 | bytes 4587520 | tf_op jit(solution)/shard_map/diagonal_grad/pallas_call | solution.py:95
  48.4 3.8 %collective-permute-start.10 = (bf16[2,688,512]{2,1,0:T(8,128)(2,1)}, bf16[2,688,512]{2,1,0:T(8,128)(2,1)}, u32[]{:S(2)}, u32[]{:S(2)}) collective-permute-start(bf16[2,688,512]{2,1,0:T(8,128)(2,1)} %diagonal_grad.4), channel_id=1, source_target_pairs={{0,64},{1,17},{8,72},{9,25},{16,80},{17,1},{24,88},{25,9},{32,96},... | collective-permute-start | bytes 4227080 | tf_op jit(solution)/shard_map/ppermute | solution.py:295
  52.2 6.2 %diagonal_grad.6 = bf16[2,688,512]{2,1,0:T(8,128)(2,1)} custom-call(s32[30]{0:T(128)S(1)} %stack.153.at_ref, bf16[640,11008]{1,0:T(8,128)(2,1)} %mine_ref.3, bf16[640,11008]{1,0:T(8,128)(2,1)} %collective-permute-done.other_ref, bf16[640,512]{1,0:T(8,128)(2,1)S(1)} %add_convert_fusion.reduced_ref, bf16[640,512]{1,0:T(8,128)(2,1)S(1)} %collective-permute-done.9.reduced_other_ref), custom_call_target="tpu_custom_call" | custom-call | flops 2348810240 | bytes 4587520 | tf_op jit(solution)/shard_map/diagonal_grad/pallas_call | solution.py:95
  59.0 6.2 %diagonal_grad.7 = bf16[2,688,512]{2,1,0:T(8,128)(2,1)} custom-call(s32[30]{0:T(128)S(1)} %stack.153.at_ref, bf16[640,11008]{1,0:T(8,128)(2,1)} %mine_ref.3, bf16[640,11008]{1,0:T(8,128)(2,1)} %collective-permute-done.other_ref, bf16[640,512]{1,0:T(8,128)(2,1)S(1)} %add_convert_fusion.reduced_ref, bf16[640,512]{1,0:T(8,128)(2,1)S(1)} %collective-permute-done.9.reduced_other_ref), custom_call_target="tpu_custom_call" | custom-call | flops 2348810240 | bytes 4587520 | tf_op jit(solution)/shard_map/diagonal_grad/pallas_call | solution.py:95
  67.2 5.2 %diagonal_grad.5.refs_3_ = bf16[2,688,512]{2,1,0:T(8,128)(2,1)S(1)} custom-call(s32[30]{0:T(128)S(1)} %stack.153.at_ref, bf16[640,11008]{1,0:T(8,128)(2,1)} %mine_ref.3, bf16[640,11008]{1,0:T(8,128)(2,1)} %collective-permute-done.other_ref, bf16[640,512]{1,0:T(8,128)(2,1)S(1)} %add_convert_fusion.reduced_ref, ...), custom_call_target="tpu_custom_call" | custom-call | flops 2348810240 | bytes 4587520 | tf_op jit(solution)/shard_map/diagonal_grad/pallas_call | solution.py:95
  73.8 2.0 %copy-done.1 = bf16[4096,512]{1,0:T(8,128)(2,1)} copy-done((bf16[4096,512]{1,0:T(8,128)(2,1)}, bf16[4096,512]{1,0:T(8,128)(2,1)S(1)}, u32[]{:S(2)}) %copy-start.1) | copy-done | bytes 4194328
  75.8 8.6 %collective-permute-done.12.refs_1_ = bf16[2,688,512]{2,1,0:T(8,128)(2,1)} collective-permute-done((bf16[2,688,512]{2,1,0:T(8,128)(2,1)}, bf16[2,688,512]{2,1,0:T(8,128)(2,1)}, u32[]{:S(2)}, u32[]{:S(2)}) %collective-permute-start.12) | collective-permute-done | bytes 1409056 | tf_op jit(solution)/shard_map/ppermute | solution.py:295
  84.4 2.3 %sum_half.2 = bf16[2,688,256]{2,1,0:T(8,128)(2,1)S(1)} custom-call(s32[30]{0:T(128)S(1)} %stack.153.at_ref, bf16[2,688,512]{2,1,0:T(8,128)(2,1)} %collective-permute-done.10.refs_0_, bf16[2,688,512]{2,1,0:T(8,128)(2,1)} %collective-permute-done.12.refs_1_, bf16[2,688,512]{2,1,0:T(8,128)(2,1)} %collective-permute-done.13.refs_2_, ...), custom_call_target="tpu_custom_call" | custom-call | tf_op jit(solution)/shard_map/sum_half/pallas_call | solution.py:135
  87.3 2.3 %sum_half.3.refs_0_ = bf16[2,688,256]{2,1,0:T(8,128)(2,1)S(1)} custom-call(s32[30]{0:T(128)S(1)} %stack.153.at_ref, bf16[2,688,512]{2,1,0:T(8,128)(2,1)} %collective-permute-done.10.refs_0_, bf16[2,688,512]{2,1,0:T(8,128)(2,1)} %collective-permute-done.12.refs_1_, bf16[2,688,512]{2,1,0:T(8,128)(2,1)} %collective-permute-done.13.refs_2_, ...), custom_call_target="tpu_custom_call" | custom-call | tf_op jit(solution)/shard_map/sum_half/pallas_call | solution.py:135
  91.0 2.2 %collective-permute-start.17 = (bf16[4,172,256]{2,1,0:T(8,128)(2,1)S(1)}, bf16[4,172,256]{2,1,0:T(8,128)(2,1)S(1)}, u32[]{:S(2)}, u32[]{:S(2)}) collective-permute-start(bf16[4,172,256]{2,1,0:T(8,128)(2,1)S(1)} %get-tuple-element.82), channel_id=1, source_target_pairs={{0,120},{1,7},{2,122},{3,1},{4,124},{5,3},{6,126},{7,5},{8,96},{9,... | collective-permute-start | bytes 1056776 | tf_op jit(solution)/shard_map/ppermute | solution.py:200
  93.2 5.4 %collective-permute-done.15.refs_1_ = bf16[4,172,256]{2,1,0:T(8,128)(2,1)S(1)} collective-permute-done((bf16[4,172,256]{2,1,0:T(8,128)(2,1)S(1)}, bf16[4,172,256]{2,1,0:T(8,128)(2,1)S(1)}, u32[]{:S(2)}, u32[]{:S(2)}) %collective-permute-start.15) | collective-permute-done | bytes 352288 | tf_op jit(solution)/shard_map/ppermute | solution.py:200
  98.6 3.3 %collective-permute-done.16.refs_2_ = bf16[4,172,256]{2,1,0:T(8,128)(2,1)S(1)} collective-permute-done((bf16[4,172,256]{2,1,0:T(8,128)(2,1)S(1)}, bf16[4,172,256]{2,1,0:T(8,128)(2,1)S(1)}, u32[]{:S(2)}, u32[]{:S(2)}) %collective-permute-start.16) | collective-permute-done | bytes 352288 | tf_op jit(solution)/shard_map/ppermute | solution.py:200
  102.6 6.1 %collective-permute-start.18 = (bf16[172,256]{1,0:T(8,128)(2,1)S(1)}, bf16[172,256]{1,0:T(8,128)(2,1)S(1)}, u32[]{:S(2)}, u32[]{:S(2)}) collective-permute-start(bf16[172,256]{1,0:T(8,128)(2,1)S(1)} %get-tuple-element.84), channel_id=1, source_target_pairs={{0,4},{1,81},{2,6},{3,83},{4,0},{5,85},{6,2},{7,87},{8,12},{9,89},... | collective-permute-start | bytes 264200 | tf_op jit(solution)/shard_map/ppermute | solution.py:200
  108.7 1.8 %collective-permute-start.19 = (bf16[172,256]{1,0:T(8,128)(2,1)S(1)}, bf16[172,256]{1,0:T(8,128)(2,1)S(1)}, u32[]{:S(2)}, u32[]{:S(2)}) collective-permute-start(bf16[172,256]{1,0:T(8,128)(2,1)S(1)} %get-tuple-element.85), channel_id=1, source_target_pairs={{0,2},{1,41},{2,4},{3,43},{4,6},{5,45},{6,0},{7,47},{8,10},{9,49},... | collective-permute-start | bytes 264200 | tf_op jit(solution)/shard_map/ppermute | solution.py:200
  110.5 3.0 %collective-permute-start.20 = (bf16[172,256]{1,0:T(8,128)(2,1)S(1)}, bf16[172,256]{1,0:T(8,128)(2,1)S(1)}, u32[]{:S(2)}, u32[]{:S(2)}) collective-permute-start(bf16[172,256]{1,0:T(8,128)(2,1)S(1)} %get-tuple-element.86), channel_id=1, source_target_pairs={{0,6},{1,121},{2,0},{3,123},{4,2},{5,125},{6,4},{7,127},{8,14},{9,... | collective-permute-start | bytes 264200 | tf_op jit(solution)/shard_map/ppermute | solution.py:200
  113.5 1.9 %collective-permute-done.19 = bf16[172,256]{1,0:T(8,128)(2,1)S(1)} collective-permute-done((bf16[172,256]{1,0:T(8,128)(2,1)S(1)}, bf16[172,256]{1,0:T(8,128)(2,1)S(1)}, u32[]{:S(2)}, u32[]{:S(2)}) %collective-permute-start.19) | collective-permute-done | bytes 88096 | tf_op jit(solution)/shard_map/ppermute | solution.py:200
  115.7 2.7 %collective-permute-start.22 = (bf16[172,256]{1,0:T(8,128)(2,1)S(1)}, bf16[172,256]{1,0:T(8,128)(2,1)S(1)}, u32[]{:S(2)}, u32[]{:S(2)}) collective-permute-start(bf16[172,256]{1,0:T(8,128)(2,1)S(1)} %get-tuple-element.89.own_ref), channel_id=1, source_target_pairs={{0,6},{2,0},{4,2},{6,4},{1,7},{3,1},{5,3},{7,5},{8,14},{10,8},{12,... | collective-permute-start | bytes 264200 | tf_op jit(solution)/shard_map/ppermute | solution.py:26
  118.3 2.6 %copy-done = bf16[4096,688]{0,1:T(8,128)(2,1)S(1)} copy-done((bf16[4096,688]{0,1:T(8,128)(2,1)S(1)}, bf16[4096,688]{0,1:T(8,128)(2,1)}, u32[]{:S(2)}) %copy-start) | copy-done | bytes 5636120
  120.9 2.2 %copy-done.2 = bf16[4096,512]{1,0:T(8,128)(2,1)S(1)} copy-done((bf16[4096,512]{1,0:T(8,128)(2,1)S(1)}, bf16[4096,512]{1,0:T(8,128)(2,1)}, u32[]{:S(2)}) %copy-start.2) | copy-done | bytes 4194328
  127.0 6.9 %update.1 = bf16[688,4096]{1,0:T(8,128)(2,1)} custom-call(s32[30]{0:T(128)S(1)} %stack.153.at_ref, bf16[172,256]{1,0:T(8,128)(2,1)S(1)} %get-tuple-element.89.own_ref, bf16[3,172,256]{2,1,0:T(8,128)(2,1)S(1)} %pad_maximum_fusion.own_far_ref, bf16[172,256]{1,0:T(8,128)(2,1)S(1)} %collective-permute-done.24.other_ref, ...), custom_call_target="tpu_custom_call" | custom-call | tf_op jit(solution)/shard_map/update/pallas_call | solution.py:271
  (104 shorter events, 18.3 us)
Async XLA Ops:
  7.2 68.7 %all-gather.2.cloned.1.call-start = ((), (), s32[]{:S(2)}) async-start(), calls=%async_computation | async-start | bytes 6340608 | tf_op jit(solution)/shard_map/all_gather | solution.py:366
  7.4 34.9 %collective-permute-start = (bf16[640,11008]{1,0:T(8,128)(2,1)}, bf16[640,11008]{1,0:T(8,128)(2,1)}, u32[]{:S(2)}, u32[]{:S(2)}) collective-permute-start(bf16[640,11008]{1,0:T(8,128)(2,1)} %mine_ref.3), channel_id=1, source_target_pairs={{0,1},{1,0},{2,3},{3,2},{4,5},{5,4},{6,7},{7,6},{8,9},{9,8},{10,11... | collective-permute-start | bytes 42270728 | tf_op jit(solution)/shard_map/ppermute | solution.py:311
  8.9 7.4 %collective-permute-start.3 = (bf16[512,512]{1,0:T(8,128)(2,1)}, bf16[512,512]{1,0:T(8,128)(2,1)S(1)}, u32[]{:S(2)}, u32[]{:S(2)}) collective-permute-start(bf16[512,512]{1,0:T(8,128)(2,1)} %param.8), channel_id=1, source_target_pairs={{0,1},{1,0},{2,3},{3,2},{4,5},{5,4},{6,7},{7,6},{8,9},{9,8},{10,11... | collective-permute-start | bytes 1572872 | tf_op jit(solution)/shard_map/ppermute | solution.py:311
  9.0 14.5 %collective-permute-start.2 = (bf16[512,512]{1,0:T(8,128)(2,1)}, bf16[512,512]{1,0:T(8,128)(2,1)S(1)}, u32[]{:S(2)}, u32[]{:S(2)}) collective-permute-start(bf16[512,512]{1,0:T(8,128)(2,1)} %param.8), channel_id=1, source_target_pairs={{0,2},{2,4},{4,6},{6,0},{1,3},{3,5},{5,7},{7,1},{8,10},{10,12},{12... | collective-permute-start | bytes 1572872 | tf_op jit(solution)/shard_map/ppermute | solution.py:26
  10.3 13.2 %collective-permute-start.1 = (bf16[512,512]{1,0:T(8,128)(2,1)}, bf16[512,512]{1,0:T(8,128)(2,1)S(1)}, u32[]{:S(2)}, u32[]{:S(2)}) collective-permute-start(bf16[512,512]{1,0:T(8,128)(2,1)} %param.8), channel_id=1, source_target_pairs={{0,6},{2,0},{4,2},{6,4},{1,7},{3,1},{5,3},{7,5},{8,14},{10,8},{12,... | collective-permute-start | bytes 1572872 | tf_op jit(solution)/shard_map/ppermute | solution.py:26
  13.9 13.8 %copy-start.3 = (bf16[640,4096]{1,0:T(8,128)(2,1)S(1)}, bf16[640,4096]{1,0:T(8,128)(2,1)}, u32[]{:S(2)}) copy-start(bf16[640,4096]{1,0:T(8,128)(2,1)} %param.6) | copy-start | bytes 15728644
  16.3 12.5 %copy-start.12 = (bf16[512,512]{1,0:T(8,128)(2,1)}, bf16[512,512]{1,0:T(8,128)(2,1)S(1)}, u32[]{:S(2)}) copy-start(bf16[512,512]{1,0:T(8,128)(2,1)S(1)} %collective-permute-done.3) | copy-start | bytes 1572868
  23.5 9.1 %copy-start.6 = (bf16[512,512]{1,0:T(8,128)(2,1)}, bf16[512,512]{1,0:T(8,128)(2,1)S(1)}, u32[]{:S(2)}) copy-start(bf16[512,512]{1,0:T(8,128)(2,1)S(1)} %collective-permute-done.1) | copy-start | bytes 1572868
  23.5 9.3 %collective-permute-start.7 = (bf16[512,512]{1,0:T(8,128)(2,1)S(1)}, bf16[512,512]{1,0:T(8,128)(2,1)S(1)}, u32[]{:S(2)}, u32[]{:S(2)}) collective-permute-start(bf16[512,512]{1,0:T(8,128)(2,1)S(1)} %collective-permute-done.2), channel_id=1, source_target_pairs={{0,1},{1,0},{2,3},{3,2},{4,5},{5,4},{6,7},{7,6},{8,9},{9,8},{10,11... | collective-permute-start | bytes 1572872 | tf_op jit(solution)/shard_map/ppermute | solution.py:311
  24.9 7.1 %collective-permute-start.6 = (bf16[512,512]{1,0:T(8,128)(2,1)S(1)}, bf16[512,512]{1,0:T(8,128)(2,1)S(1)}, u32[]{:S(2)}, u32[]{:S(2)}) collective-permute-start(bf16[512,512]{1,0:T(8,128)(2,1)S(1)} %collective-permute-done.1), channel_id=1, source_target_pairs={{0,1},{1,0},{2,3},{3,2},{4,5},{5,4},{6,7},{7,6},{8,9},{9,8},{10,11... | collective-permute-start | bytes 1572872 | tf_op jit(solution)/shard_map/ppermute | solution.py:311
  25.0 8.4 %collective-permute-start.5 = (bf16[256,512]{1,0:T(8,128)(2,1)S(1)}, bf16[256,512]{1,0:T(8,128)(2,1)S(1)}, u32[]{:S(2)}, u32[]{:S(2)}) collective-permute-start(bf16[256,512]{1,0:T(8,128)(2,1)S(1)} %slice.19), channel_id=1, source_target_pairs={{0,6},{2,0},{4,2},{6,4},{1,7},{3,1},{5,3},{7,5},{8,14},{10,8},{12,... | collective-permute-start | bytes 786440 | tf_op jit(solution)/shard_map/ppermute | solution.py:26
  27.7 8.3 %collective-permute-start.4 = (bf16[256,512]{1,0:T(8,128)(2,1)S(1)}, bf16[256,512]{1,0:T(8,128)(2,1)S(1)}, u32[]{:S(2)}, u32[]{:S(2)}) collective-permute-start(bf16[256,512]{1,0:T(8,128)(2,1)S(1)} %slice.18), channel_id=1, source_target_pairs={{0,2},{2,4},{4,6},{6,0},{1,3},{3,5},{5,7},{7,1},{8,10},{10,12},{12... | collective-permute-start | bytes 786440 | tf_op jit(solution)/shard_map/ppermute | solution.py:26
  36.1 3.2 %collective-permute-start.8 = (bf16[512,512]{1,0:T(8,128)(2,1)S(1)}, bf16[512,512]{1,0:T(8,128)(2,1)S(1)}, u32[]{:S(2)}, u32[]{:S(2)}) collective-permute-start(bf16[512,512]{1,0:T(8,128)(2,1)S(1)} %constant_dynamic-update-slice_fusion), channel_id=1, source_target_pairs={{0,1},{1,0},{2,3},{3,2},{4,5},{5,4},{6,7},{7,6},{8,9},{9,8},{10,11... | collective-permute-start | bytes 1572872 | tf_op jit(solution)/shard_map/ppermute | solution.py:311
  40.1 2.1 %collective-permute-start.9 = (bf16[640,512]{1,0:T(8,128)(2,1)S(1)}, bf16[640,512]{1,0:T(8,128)(2,1)S(1)}, u32[]{:S(2)}, u32[]{:S(2)}) collective-permute-start(bf16[640,512]{1,0:T(8,128)(2,1)S(1)} %add_convert_fusion.reduced_ref), channel_id=1, source_target_pairs={{0,1},{1,0},{2,3},{3,2},{4,5},{5,4},{6,7},{7,6},{8,9},{9,8},{10,11... | collective-permute-start | bytes 1966088 | tf_op jit(solution)/shard_map/ppermute | solution.py:311
  41.5 25.0 %collective-permute-start.11 = (f32[2,86,256]{2,1,0:T(8,128)S(1)}, f32[2,86,256]{2,1,0:T(8,128)S(1)}, u32[]{:S(2)}, u32[]{:S(2)}) collective-permute-start(f32[2,86,256]{2,1,0:T(8,128)S(1)} %get-tuple-element.111), channel_id=1, source_target_pairs={{0,1},{1,0},{2,3},{3,2},{4,5},{5,4},{6,7},{7,6},{8,9},{9,8},{10,11... | collective-permute-start | bytes 528392 | tf_op jit(solution)/shard_map/ppermute | solution.py:311
  48.4 27.5 %collective-permute-start.10 = (bf16[2,688,512]{2,1,0:T(8,128)(2,1)}, bf16[2,688,512]{2,1,0:T(8,128)(2,1)}, u32[]{:S(2)}, u32[]{:S(2)}) collective-permute-start(bf16[2,688,512]{2,1,0:T(8,128)(2,1)} %diagonal_grad.4), channel_id=1, source_target_pairs={{0,64},{1,17},{8,72},{9,25},{16,80},{17,1},{24,88},{25,9},{32,96},... | collective-permute-start | bytes 4227080 | tf_op jit(solution)/shard_map/ppermute | solution.py:295
  58.4 26.0 %collective-permute-start.12 = (bf16[2,688,512]{2,1,0:T(8,128)(2,1)}, bf16[2,688,512]{2,1,0:T(8,128)(2,1)}, u32[]{:S(2)}, u32[]{:S(2)}) collective-permute-start(bf16[2,688,512]{2,1,0:T(8,128)(2,1)} %diagonal_grad.6), channel_id=1, source_target_pairs={{0,32},{1,25},{8,40},{9,1},{16,48},{17,9},{24,56},{25,17},{32,64},... | collective-permute-start | bytes 4227080 | tf_op jit(solution)/shard_map/ppermute | solution.py:295
  65.2 19.3 %collective-permute-start.13 = (bf16[2,688,512]{2,1,0:T(8,128)(2,1)}, bf16[2,688,512]{2,1,0:T(8,128)(2,1)}, u32[]{:S(2)}, u32[]{:S(2)}) collective-permute-start(bf16[2,688,512]{2,1,0:T(8,128)(2,1)} %diagonal_grad.7), channel_id=1, source_target_pairs={{0,96},{1,9},{8,104},{9,17},{16,112},{17,25},{24,120},{25,1},{32,0... | collective-permute-start | bytes 4227080 | tf_op jit(solution)/shard_map/ppermute | solution.py:295
  86.8 28.7 %copy-start.18 = (f32[2,172,256]{2,1,0:T(8,128)S(1)}, f32[2,172,256]{2,1,0:T(8,128)}, u32[]{:S(2)}) copy-start(f32[2,172,256]{2,1,0:T(8,128)} %maximum_select_fusion) | copy-start | bytes 1056772
  86.8 2.8 %collective-permute-start.14 = (bf16[2,688,256]{2,1,0:T(8,128)(2,1)S(1)}, bf16[2,688,256]{2,1,0:T(8,128)(2,1)S(1)}, u32[]{:S(2)}, u32[]{:S(2)}) collective-permute-start(bf16[2,688,256]{2,1,0:T(8,128)(2,1)S(1)} %sum_half.2), channel_id=1, source_target_pairs={{0,1},{1,0},{2,3},{3,2},{4,5},{5,4},{6,7},{7,6},{8,9},{9,8},{10,11... | collective-permute-start | bytes 2113544 | tf_op jit(solution)/shard_map/ppermute | solution.py:311
  90.4 8.2 %collective-permute-start.15 = (bf16[4,172,256]{2,1,0:T(8,128)(2,1)S(1)}, bf16[4,172,256]{2,1,0:T(8,128)(2,1)S(1)}, u32[]{:S(2)}, u32[]{:S(2)}) collective-permute-start(bf16[4,172,256]{2,1,0:T(8,128)(2,1)S(1)} %get-tuple-element.80), channel_id=1, source_target_pairs={{0,80},{1,5},{2,82},{3,7},{4,84},{5,1},{6,86},{7,3},{8,88},{9,13},... | collective-permute-start | bytes 1056776 | tf_op jit(solution)/shard_map/ppermute | solution.py:200
  90.5 11.4 %collective-permute-start.16 = (bf16[4,172,256]{2,1,0:T(8,128)(2,1)S(1)}, bf16[4,172,256]{2,1,0:T(8,128)(2,1)S(1)}, u32[]{:S(2)}, u32[]{:S(2)}) collective-permute-start(bf16[4,172,256]{2,1,0:T(8,128)(2,1)S(1)} %get-tuple-element.81), channel_id=1, source_target_pairs={{0,40},{1,3},{2,42},{3,5},{4,44},{5,7},{6,46},{7,1},{8,48},{9,11},... | collective-permute-start | bytes 1056776 | tf_op jit(solution)/shard_map/ppermute | solution.py:200
  91.0 10.9 %collective-permute-start.17 = (bf16[4,172,256]{2,1,0:T(8,128)(2,1)S(1)}, bf16[4,172,256]{2,1,0:T(8,128)(2,1)S(1)}, u32[]{:S(2)}, u32[]{:S(2)}) collective-permute-start(bf16[4,172,256]{2,1,0:T(8,128)(2,1)S(1)} %get-tuple-element.82), channel_id=1, source_target_pairs={{0,120},{1,7},{2,122},{3,1},{4,124},{5,3},{6,126},{7,5},{8,96},{9,... | collective-permute-start | bytes 1056776 | tf_op jit(solution)/shard_map/ppermute | solution.py:200
  102.6 10.9 %collective-permute-start.18 = (bf16[172,256]{1,0:T(8,128)(2,1)S(1)}, bf16[172,256]{1,0:T(8,128)(2,1)S(1)}, u32[]{:S(2)}, u32[]{:S(2)}) collective-permute-start(bf16[172,256]{1,0:T(8,128)(2,1)S(1)} %get-tuple-element.84), channel_id=1, source_target_pairs={{0,4},{1,81},{2,6},{3,83},{4,0},{5,85},{6,2},{7,87},{8,12},{9,89},... | collective-permute-start | bytes 264200 | tf_op jit(solution)/shard_map/ppermute | solution.py:200
  108.7 6.7 %collective-permute-start.19 = (bf16[172,256]{1,0:T(8,128)(2,1)S(1)}, bf16[172,256]{1,0:T(8,128)(2,1)S(1)}, u32[]{:S(2)}, u32[]{:S(2)}) collective-permute-start(bf16[172,256]{1,0:T(8,128)(2,1)S(1)} %get-tuple-element.85), channel_id=1, source_target_pairs={{0,2},{1,41},{2,4},{3,43},{4,6},{5,45},{6,0},{7,47},{8,10},{9,49},... | collective-permute-start | bytes 264200 | tf_op jit(solution)/shard_map/ppermute | solution.py:200
  110.5 4.9 %collective-permute-start.20 = (bf16[172,256]{1,0:T(8,128)(2,1)S(1)}, bf16[172,256]{1,0:T(8,128)(2,1)S(1)}, u32[]{:S(2)}, u32[]{:S(2)}) collective-permute-start(bf16[172,256]{1,0:T(8,128)(2,1)S(1)} %get-tuple-element.86), channel_id=1, source_target_pairs={{0,6},{1,121},{2,0},{3,123},{4,2},{5,125},{6,4},{7,127},{8,14},{9,... | collective-permute-start | bytes 264200 | tf_op jit(solution)/shard_map/ppermute | solution.py:200
  115.6 8.4 %collective-permute-start.23 = (bf16[172,256]{1,0:T(8,128)(2,1)S(1)}, bf16[172,256]{1,0:T(8,128)(2,1)S(1)}, u32[]{:S(2)}, u32[]{:S(2)}) collective-permute-start(bf16[172,256]{1,0:T(8,128)(2,1)S(1)} %get-tuple-element.89.own_ref), channel_id=1, source_target_pairs={{0,2},{2,4},{4,6},{6,0},{1,3},{3,5},{5,7},{7,1},{8,10},{10,12},{12... | collective-permute-start | bytes 264200 | tf_op jit(solution)/shard_map/ppermute | solution.py:26
  115.7 8.3 %collective-permute-start.22 = (bf16[172,256]{1,0:T(8,128)(2,1)S(1)}, bf16[172,256]{1,0:T(8,128)(2,1)S(1)}, u32[]{:S(2)}, u32[]{:S(2)}) collective-permute-start(bf16[172,256]{1,0:T(8,128)(2,1)S(1)} %get-tuple-element.89.own_ref), channel_id=1, source_target_pairs={{0,6},{2,0},{4,2},{6,4},{1,7},{3,1},{5,3},{7,5},{8,14},{10,8},{12,... | collective-permute-start | bytes 264200 | tf_op jit(solution)/shard_map/ppermute | solution.py:26
  118.3 5.7 %collective-permute-start.21 = (bf16[172,256]{1,0:T(8,128)(2,1)S(1)}, bf16[172,256]{1,0:T(8,128)(2,1)S(1)}, u32[]{:S(2)}, u32[]{:S(2)}) collective-permute-start(bf16[172,256]{1,0:T(8,128)(2,1)S(1)} %get-tuple-element.89.own_ref), channel_id=1, source_target_pairs={{0,4},{2,6},{4,0},{6,2},{1,5},{3,7},{5,1},{7,3},{8,12},{10,14},{12... | collective-permute-start | bytes 264200 | tf_op jit(solution)/shard_map/ppermute | solution.py:26
  124.1 2.1 %collective-permute-start.26 = (f32[2,86,256]{2,1,0:T(8,128)S(1)}, f32[2,86,256]{2,1,0:T(8,128)S(1)}, u32[]{:S(2)}, u32[]{:S(2)}) collective-permute-start(f32[2,86,256]{2,1,0:T(8,128)S(1)} %get-tuple-element.109), channel_id=1, source_target_pairs={{0,1},{1,0},{2,3},{3,2},{4,5},{5,4},{6,7},{7,6},{8,9},{9,8},{10,11... | collective-permute-start | bytes 528392 | tf_op jit(solution)/shard_map/ppermute | solution.py:311
  125.2 1.8 %collective-permute-start.24 = (bf16[172,256]{1,0:T(8,128)(2,1)S(1)}, bf16[172,256]{1,0:T(8,128)(2,1)S(1)}, u32[]{:S(2)}, u32[]{:S(2)}) collective-permute-start(bf16[172,256]{1,0:T(8,128)(2,1)S(1)} %get-tuple-element.89.own_ref), channel_id=1, source_target_pairs={{0,1},{1,0},{2,3},{3,2},{4,5},{5,4},{6,7},{7,6},{8,9},{9,8},{10,11... | collective-permute-start | bytes 264200 | tf_op jit(solution)/shard_map/ppermute | solution.py:311
  125.3 1.8 %collective-permute-start.25 = (bf16[3,172,256]{2,1,0:T(8,128)(2,1)S(1)}, bf16[3,172,256]{2,1,0:T(8,128)(2,1)S(1)}, u32[]{:S(2)}, u32[]{:S(2)}) collective-permute-start(bf16[3,172,256]{2,1,0:T(8,128)(2,1)S(1)} %pad_maximum_fusion.own_far_ref), channel_id=1, source_target_pairs={{0,1},{1,0},{2,3},{3,2},{4,5},{5,4},{6,7},{7,6},{8,9},{9,8},{10,11... | collective-permute-start | bytes 792584 | tf_op jit(solution)/shard_map/ppermute | solution.py:311
  (16 other events, 54.9 us)
Sparse Core Ops, SparseCore 0:
  36.2 39.4 all-gather.1
